TPU v7x, 128 devices: a whole 4x4x4 slice. The times are simulated.
128 devices in a mesh: rows: 128 (over x, y, z, core).
Axes of the slice: x: 4, y: 4, z: 4, core: 2. Of those that a mesh axis runs over, the one named last changes fastest.
Arguments:
- features: bfloat16 [524288, 128], P('rows'), may hold values from -6 to 6
- weight: bfloat16 [128, 256], replicated, may hold values from -0.5 to 0.5
- adjacency_tiles: bfloat16 [4096, 6, 128, 128], P('rows'), may hold values from -0.15625 to 0.15625
- tile_columns: int32 [4096, 6], P('rows'), may hold values from 0 to 159
- send_rows: int32 [128, 128, 128], P('rows'), may hold values from -1 to 4095, as said below
- hub_owner: int32 [4], replicated, may hold values from 0 to 127
- hub_rows: int32 [4, 128], replicated, may hold values from 0 to 4095
- hub_tiles: bfloat16 [4, 524288, 128], P(None, 'rows'), may hold values from -0.15625 to 0.15625
- cotangent: bfloat16 [524288, 256], P('rows'), may hold values from -6 to 6
Outputs:
- output: bfloat16 [524288, 256], P('rows')
- grad_features: bfloat16 [524288, 128], P('rows')
- grad_weight: float32 [128, 256], replicated
Inputs may be any that keep to these rules, and one draw needn't show every extreme that they name: `send_rows`: in each list the live entries (not -1) come first; every list has 32 or more live entries, and every device has one full list of 128 live entries to some peer. Rows may repeat.
All inputs are finite; a program needn't handle non-finite values.
Results may differ from a plain program's by a relative error of at most 0.0075.
Values may be sent and summed in bfloat16 or wider, within the bound.
No kernel may reach another device: no remote copies, remote signals or barrier semaphores. Data moves between devices by JAX's collectives and lax.ppermute only.
A program may use at most 192 MiB of HBM per device.

v0:
```python
import jax
import jax.numpy as jnp
from jax import lax
from jax.sharding import PartitionSpec as P


def broadcast(block, axis, holder):
    block = jnp.where(lax.axis_index(axis) == holder, block, jnp.zeros_like(block))
    return lax.psum(block, axis)


def body(
    features,
    weight,
    adjacency_tiles,
    tile_columns,
    send_rows,
    hub_owner,
    hub_rows,
    hub_tiles,
    cotangent,
):
    peers = lax.axis_size("rows")
    device = lax.axis_index("rows")
    local_rows = features.shape[0]
    width_out = weight.shape[1]
    blocks = adjacency_tiles.shape[0]
    per_block = adjacency_tiles.shape[1]
    block_rows = adjacency_tiles.shape[2]
    projected = jnp.dot(features, weight, preferred_element_type=jnp.float32).astype(jnp.bfloat16)
    send_lists = send_rows[0]
    live_slots = send_lists >= 0
    safe_rows = jnp.maximum(send_lists, 0)
    outgoing = jnp.where(live_slots[:, :, None], projected[safe_rows], jnp.zeros((), jnp.bfloat16))
    halo_proj = lax.all_to_all(outgoing, "rows", split_axis=0, concat_axis=0, tiled=True)
    columns = jnp.concatenate([projected.reshape(blocks, block_rows, width_out), halo_proj], axis=0)
    gathered = columns[tile_columns]
    aggregate = jnp.einsum(
        "btij,btjh->bih", adjacency_tiles, gathered, preferred_element_type=jnp.float32
    )
    aggregate = aggregate.reshape(local_rows, width_out)
    sections = hub_rows.shape[0]
    owned = hub_owner == device
    pieces = []
    for section in range(sections):
        pieces.append(broadcast(projected[hub_rows[section]], "rows", hub_owner[section]))
    hub_blocks = jnp.stack(pieces)
    aggregate = aggregate + jnp.einsum(
        "sri,sih->rh", hub_tiles, hub_blocks, preferred_element_type=jnp.float32
    )
    output = jax.nn.gelu(aggregate).astype(jnp.bfloat16)
    activated, pullback = jax.vjp(jax.nn.gelu, aggregate)
    grad_preact = pullback(cotangent.astype(jnp.float32))[0].astype(jnp.bfloat16)
    grad_blocks = grad_preact.reshape(blocks, block_rows, width_out)

    def add_tile(position, accumulated):
        tile_slab = lax.dynamic_index_in_dim(adjacency_tiles, position, 1, keepdims=False)
        targets = lax.dynamic_index_in_dim(tile_columns, position, 1, keepdims=False)
        contribution = jnp.einsum(
            "bij,bih->bjh", tile_slab, grad_blocks, preferred_element_type=jnp.float32
        )
        return accumulated.at[targets].add(contribution)

    accumulated = lax.fori_loop(
        0, per_block, add_tile, jnp.zeros((blocks + peers, block_rows, width_out), jnp.float32)
    )
    halo_adjoint = accumulated[blocks:].astype(jnp.bfloat16)
    returned = lax.all_to_all(halo_adjoint, "rows", split_axis=0, concat_axis=0, tiled=True).astype(
        jnp.float32
    )
    returned = jnp.where(live_slots[:, :, None], returned, jnp.zeros((), jnp.float32))
    grad_proj = accumulated[:blocks].reshape(local_rows, width_out)
    grad_proj = grad_proj.at[safe_rows.reshape(-1)].add(returned.reshape(-1, width_out))
    hub_terms = jnp.einsum(
        "sri,rh->sih", hub_tiles, grad_preact, preferred_element_type=jnp.float32
    )
    hub_sums = lax.psum(hub_terms, "rows")
    hub_share = jnp.where(owned[:, None, None], hub_sums, jnp.zeros((), jnp.float32))
    grad_proj = (
        grad_proj.at[hub_rows.reshape(-1)]
        .add(hub_share.reshape(-1, width_out))
        .astype(jnp.bfloat16)
    )
    grad_features = lax.dot_general(
        grad_proj, weight, (((1,), (1,)), ((), ())), preferred_element_type=jnp.float32
    )
    weight_terms = lax.dot_general(
        features, grad_proj, (((0,), (0,)), ((), ())), preferred_element_type=jnp.float32
    )
    grad_weight = lax.psum(weight_terms, "rows")
    return (output, grad_features.astype(jnp.bfloat16), grad_weight)


def solution(mesh):
    return jax.shard_map(
        body,
        mesh=mesh,
        in_specs=(
            P("rows", None),
            P(),
            P("rows", None, None, None),
            P("rows", None),
            P("rows", None, None),
            P(),
            P(),
            P(None, "rows", None),
            P("rows", None),
        ),
        out_specs=(P("rows", None), P("rows", None), P()),
        check_vma=False,
    )
```

profile of v0, /device:TPU:1, one launch (start us, length us, event | category | flops | bytes accessed | tf_op | source)
XLA Modules:
  0.0 940.3 jit_solution(8127458033838010756)
XLA Ops:
  7.2 0.9 compare_bitcast_fusion
  8.1 0.9 broadcast_clamp_fusion
  9.0 1.5 convolution_convert_fusion
  10.5 65.2 %gather_fusion = bf16[16384,256]{1,0:T(8,128)(2,1)} fusion(bf16[4096,256]{1,0:T(8,128)(2,1)S(1)} %convolution_convert_fusion, s32[16384]{0:T(1024)S(1)} %broadcast_clamp_fusion), kind=kCustom, calls=%fused_computation | custom fusion | bytes 16842752 | tf_op jit(solution)/shard_map/gather | solution.py:34
  75.7 8.0 broadcast_select_fusion
  83.7 12.0 %all-to-all-start = ((bf16[128,128,256]{2,1,0:T(8,128)(2,1)}), bf16[128,128,256]{2,1,0:T(8,128)(2,1)}, u32[]{:S(2)}, u32[]{:S(2)}) async-start(bf16[128,128,256]{2,1,0:T(8,128)(2,1)} %broadcast_select_fusion), calls=%async_computation | async-start | bytes 16777216 | tf_op jit(solution)/shard_map/all_to_all | solution.py:35
  95.7 0.0 all-reduce.9.cloned.1.call-start
  95.8 0.7 fusion.35
  99.0 0.8 gather_fusion.5
  99.9 0.1 copy.26
  100.0 0.9 gather_fusion.4
  100.8 0.1 copy.25
  101.0 0.8 gather_fusion.3
  101.8 0.1 copy.24
  101.9 0.9 gather_fusion.2
  102.8 0.1 copy.23
  102.9 0.6 select_bitcast_fusion
  103.6 0.6 select_bitcast_fusion.1
  104.2 0.6 select_bitcast_fusion.2
  104.8 0.6 select_bitcast_fusion.3
  105.5 0.1 copy.22
  105.6 0.1 reshape.218
  105.7 4.3 copy.28
  110.0 87.7 %all-to-all-done = bf16[128,128,256]{2,1,0:T(8,128)(2,1)} async-done(((bf16[128,128,256]{2,1,0:T(8,128)(2,1)}), bf16[128,128,256]{2,1,0:T(8,128)(2,1)}, u32[]{:S(2)}, u32[]{:S(2)}) %all-to-all-start) | async-done | bytes 8388640 | tf_op jit(solution)/shard_map/all_to_all | solution.py:35
  197.7 8.7 pad_maximum_fusion
  206.3 12.2 %gather_fusion.1 = bf16[192,128,256]{2,1,0:T(8,128)(2,1)} fusion(bf16[160,128,256]{2,1,0:T(8,128)(2,1)} %pad_maximum_fusion, s32[1024]{0:T(1024)S(1)} %pad_clamp_fusion.4), kind=kCustom, calls=%fused_computation.1 | custom fusion | bytes 25166592 | tf_op jit(solution)/shard_map/gather | solution.py:37
  218.6 10.6 %fusion.36 = f32[32,256,128,1]{1,2,3,0:T(8,128)} fusion(bf16[32,6,128,128]{3,2,1,0:T(8,128)(2,1)} %param.13, bf16[32,6,128,256]{3,2,1,0:T(8,128)(2,1)} %bitcast.88), kind=kOutput, calls=%fused_computation.77 | convolution fusion | flops 1610612736 | bytes 23068672 | tf_op jit(solution)/shard_map/btij,btjh->bih/dot_general | solution.py:38
  229.2 5.8 copy.27
  235.0 86.1 %all-reduce.9.cloned.1.call-done = (bf16[1,128,256]{1,2,0:T(8,128)(2,1)}, bf16[1,128,256]{1,2,0:T(8,128)(2,1)}, bf16[1,128,256]{1,2,0:T(8,128)(2,1)}, bf16[1,128,256]{1,2,0:T(8,128)(2,1)}) async-done(((bf16[1,128,256]{1,2,0:T(8,128)(2,1)}, bf16[1,128,256]{1,2,0:T(8,128)(2,1)}, bf16[1,128,256]{1,2,0:T(8,128)(2,1)}, bf16[1,128,256]{1,2,0:T(8,128)(2,1)}), (bf16[1,128,256]{1,2,0:T(8,128)(2,1)}, ...) | async-done | bytes 262160 | tf_op jit(solution)/shard_map/psum | solution.py:9
  321.1 9.6 %fusion.8 = (bf16[4096,256]{0,1:T(8,128)(2,1)}, bf16[4096,256]{0,1:T(8,128)(2,1)}) fusion(bf16[4096,256]{0,1:T(8,128)(2,1)S(1)} %copy-done.3, f32[4096,256]{0,1:T(8,128)} %copy.27, bf16[4,4096,128]{2,1,0:T(8,128)(2,1)} %param.18, bf16[1,128,256]{1,2,0:T(8,128)(2,1)} %get-tuple-element.124, bf16[1,128,256]{1,2,0:T(8,128)(2,1)} %get-tuple-element.125, ...), kind=kOutput, calls=%fused_computation.29 | convolution fusion | flops 1099300864 | bytes 14942208 | tf_op jit(solution)/shard_map/sri,sih->rh/dot_general | solution.py:48
  330.7 3.3 copy.35
  334.0 9.6 %broadcast_in_dim.56 = f32[160,128,256]{2,1,0:T(8,128)} broadcast(f32[]{:T(128)} %constant.70.clone.1), dimensions={} | broadcast | bytes 20971524 | tf_op jit(solution)/shard_map/broadcast_in_dim | solution.py:65
  343.6 84.7 %while.13 = (s32[]{:T(128)}, f32[160,128,256]{2,1,0:T(8,128)}, s32[32,6]{0,1:T(8,128)S(1)}, bf16[32,6,128,128]{3,2,1,0:T(8,128)(2,1)}, bf16[32,128,256]{2,1,0:T(8,128)(2,1)S(1)}, /*index=5*/s32[]{:T(128)}) while((s32[]{:T(128)}, f32[160,128,256]{2,1,0:T(8,128)}, s32[32,6]{0,1:T(8,128)S(1)}, bf16[32,6,128,128]{3,2,1,0:T(8,128)(2,1)}, ...), condition=%wide.region_6.7_spmd, body=%wide.region_4.6_spmd.sunk | while | flops 269484128 | bytes 19923412 | solution.py:64
  343.6 3.9 fusion.53
  347.6 10.2 %scatter_fusion = f32[160,128,256]{2,1,0:T(8,128)} fusion(f32[160,128,256]{2,1,0:T(8,128)} %get-tuple-element.180, s32[32]{0:T(128)S(1)} %fusion.52, f32[32,128,256]{2,1,0:T(8,128)} %fusion.53), kind=kCustom, calls=%fused_computation.6.clone.1 | custom fusion | flops 1048576 | bytes 12583040 | tf_op jit(solution)/shard_map/while/body/eval_jaxpr/scatter-add | solution.py:62
  357.7 3.9 fusion.53
  361.7 10.2 %scatter_fusion = f32[160,128,256]{2,1,0:T(8,128)} fusion(f32[160,128,256]{2,1,0:T(8,128)} %get-tuple-element.180, s32[32]{0:T(128)S(1)} %fusion.52, f32[32,128,256]{2,1,0:T(8,128)} %fusion.53), kind=kCustom, calls=%fused_computation.6.clone.1 | custom fusion | flops 1048576 | bytes 12583040 | tf_op jit(solution)/shard_map/while/body/eval_jaxpr/scatter-add | solution.py:62
  371.9 3.9 fusion.53
  375.9 10.1 %scatter_fusion = f32[160,128,256]{2,1,0:T(8,128)} fusion(f32[160,128,256]{2,1,0:T(8,128)} %get-tuple-element.180, s32[32]{0:T(128)S(1)} %fusion.52, f32[32,128,256]{2,1,0:T(8,128)} %fusion.53), kind=kCustom, calls=%fused_computation.6.clone.1 | custom fusion | flops 1048576 | bytes 12583040 | tf_op jit(solution)/shard_map/while/body/eval_jaxpr/scatter-add | solution.py:62
  386.0 3.9 fusion.53
  389.9 10.2 %scatter_fusion = f32[160,128,256]{2,1,0:T(8,128)} fusion(f32[160,128,256]{2,1,0:T(8,128)} %get-tuple-element.180, s32[32]{0:T(128)S(1)} %fusion.52, f32[32,128,256]{2,1,0:T(8,128)} %fusion.53), kind=kCustom, calls=%fused_computation.6.clone.1 | custom fusion | flops 1048576 | bytes 12583040 | tf_op jit(solution)/shard_map/while/body/eval_jaxpr/scatter-add | solution.py:62
  400.1 3.9 fusion.53
  404.0 10.2 %scatter_fusion = f32[160,128,256]{2,1,0:T(8,128)} fusion(f32[160,128,256]{2,1,0:T(8,128)} %get-tuple-element.180, s32[32]{0:T(128)S(1)} %fusion.52, f32[32,128,256]{2,1,0:T(8,128)} %fusion.53), kind=kCustom, calls=%fused_computation.6.clone.1 | custom fusion | flops 1048576 | bytes 12583040 | tf_op jit(solution)/shard_map/while/body/eval_jaxpr/scatter-add | solution.py:62
  414.2 3.9 fusion.53
  418.1 10.1 %scatter_fusion = f32[160,128,256]{2,1,0:T(8,128)} fusion(f32[160,128,256]{2,1,0:T(8,128)} %get-tuple-element.180, s32[32]{0:T(128)S(1)} %fusion.52, f32[32,128,256]{2,1,0:T(8,128)} %fusion.53), kind=kCustom, calls=%fused_computation.6.clone.1 | custom fusion | flops 1048576 | bytes 12583040 | tf_op jit(solution)/shard_map/while/body/eval_jaxpr/scatter-add | solution.py:62
  428.3 9.1 slice.59
  437.4 7.1 all-to-all-start.1
  444.4 0.0 all-reduce.5.cloned.1.call-start
  444.5 4.2 fusion.18
  448.7 0.0 all-reduce.5.cloned.1.call-update
  448.8 0.0 all-reduce.7.cloned.1.call-start
  448.9 4.7 slice.39
  453.6 2.4 copy.32
  456.0 216.1 %all-reduce.5.cloned.1.call-done = f32[4,128,256]{1,2,0:T(8,128)} async-done(((f32[4,128,256]{1,2,0:T(8,128)}), f32[4,128,256]{1,2,0:T(8,128)}) %all-reduce.5.cloned.1.call-update) | async-done | bytes 524304 | tf_op jit(solution)/shard_map/psum | solution.py:77
  672.1 1.1 broadcast_select_fusion.1
  673.3 0.2 copy.31
  673.5 9.6 %convert_select_fusion = f32[128,128,256]{2,1,0:T(8,128)} fusion(bf16[128,128,256]{2,1,0:T(8,128)(2,1)} %all-to-all-done.1, pred[128,128]{1,0:T(8,128)(4,1)S(1)} %compare_bitcast_fusion), kind=kLoop, calls=%fused_computation.16 | loop fusion | flops 8388608 | bytes 25182208 | tf_op jit(solution)/shard_map/jit(_where)/select_n | solution.py:71
  683.0 100.6 %scatter_fusion.1 = f32[4096,256]{1,0:T(8,128)} fusion(f32[4096,256]{1,0:T(8,128)} %bitcast.85, s32[16384]{0:T(1024)S(1)} %maximum_bitcast_fusion, f32[16384,256]{1,0:T(8,128)} %bitcast.89), kind=kCustom, calls=%fused_computation.7 | custom fusion | flops 4194304 | bytes 50397184 | tf_op jit(solution)/shard_map/scatter-add | solution.py:73
  783.7 7.1 scatter_fusion.2
  790.8 3.6 convolution_bitcast_fusion.1
  794.4 0.0 all-reduce.7.cloned.1.call-update
  794.5 3.9 convolution_convert_fusion.1
  798.3 133.8 %all-reduce.7.cloned.1.call-done = f32[128,256]{0,1:T(8,128)} async-done(((f32[128,256]{0,1:T(8,128)}), f32[128,256]{0,1:T(8,128)}) %all-reduce.7.cloned.1.call-update) | async-done | bytes 131088 | tf_op jit(solution)/shard_map/psum | solution.py:90
  932.1 1.7 copy.33
  (34 shorter events, 0.1 us)
Async XLA Ops:
  7.2 1.8 copy-start
  83.7 12.0 %copy-start.7 = (s32[4]{0:T(128)S(1)}, s32[4]{0:T(128)}, u32[]{:S(2)}) copy-start(s32[4]{0:T(128)} %param.16) | copy-start | bytes 52
  83.7 15.3 %copy-start.6 = (s32[4,128]{1,0:T(4,128)S(1)}, s32[4,128]{1,0:T(4,128)}, u32[]{:S(2)}) copy-start(s32[4,128]{1,0:T(4,128)} %param.17) | copy-start | bytes 6148
  83.7 21.8 %copy-start.8 = (s32[32,6]{0,1:T(8,128)S(1)}, s32[32,6]{0,1:T(8,128)}, u32[]{:S(2)}) copy-start(s32[32,6]{0,1:T(8,128)} %param.14) | copy-start | bytes 2308
  83.7 114.0 %all-to-all-start = ((bf16[128,128,256]{2,1,0:T(8,128)(2,1)}), bf16[128,128,256]{2,1,0:T(8,128)(2,1)}, u32[]{:S(2)}, u32[]{:S(2)}) async-start(bf16[128,128,256]{2,1,0:T(8,128)(2,1)} %broadcast_select_fusion), calls=%async_computation | async-start | bytes 16777216 | tf_op jit(solution)/shard_map/all_to_all | solution.py:35
  95.7 225.4 %all-reduce.9.cloned.1.call-start = ((), (), s32[]{:S(2)}) async-start(), calls=%async_computation.4 | async-start | bytes 524288 | tf_op jit(solution)/shard_map/psum | solution.py:9
  229.2 91.9 %copy-start.3 = (bf16[4096,256]{0,1:T(8,128)(2,1)S(1)}, bf16[4096,256]{0,1:T(8,128)(2,1)}, u32[]{:S(2)}) copy-start(bf16[4096,256]{0,1:T(8,128)(2,1)} %copy.28) | copy-start | bytes 6291460
  437.4 7.1 copy-start.4
  437.4 7.1 copy-start.2
  437.4 236.1 %all-to-all-start.1 = ((bf16[128,128,256]{2,1,0:T(8,128)(2,1)}), bf16[128,128,256]{2,1,0:T(8,128)(2,1)}, u32[]{:S(2)}, u32[]{:S(2)}) async-start(bf16[128,128,256]{2,1,0:T(8,128)(2,1)} %slice.59), calls=%async_computation.1 | async-start | bytes 16777216 | tf_op jit(solution)/shard_map/all_to_all | solution.py:68
  444.4 227.7 %all-reduce.5.cloned.1.call-start = ((), (), s32[]{:S(2)}) async-start(), calls=%async_computation.2 | async-start | bytes 1048576 | tf_op jit(solution)/shard_map/psum | solution.py:77
  448.8 483.4 %all-reduce.7.cloned.1.call-start = ((), (), s32[]{:S(2)}) async-start(), calls=%async_computation.3 | async-start | bytes 262144 | tf_op jit(solution)/shard_map/psum | solution.py:90
  448.8 4.8 copy-start.1
  790.8 3.7 copy-start.5
Sparse Core Ops, SparseCore 0:
  105.6 215.4 all-reduce.8
  450.6 221.4 all-reduce.4
  794.6 137.5 all-reduce.6
where the time goes:
time: 942 us; the launch traced here: 940 us
  waiting for transfers between devices  524 us (56%)
  other arithmetic  200 us (21%)
  local copies, waits for them, and re-layouts  123 us (13%)
  matrix products  57.2 us (6%)
  starting transfers between devices  19.1 us (2%)
  between operations  16.6 us (2%)
    psum x1, waiting for transfers between devices, body(): hub_sums = lax.psum(hub_terms, 'rows')  216 us
    psum x1, waiting for transfers between devices, body(): grad_weight = lax.psum(weight_terms, 'rows')  134 us
    scatter-add x1, other arithmetic, body(): grad_proj.at[safe_rows.reshape(-1)].add(returned.reshape(-1, width_out))  101 us
    all_to_all x1, waiting for transfers between devices, body(): lax.all_to_all(outgoing, 'rows', split_axis=0, concat_axis=0, tiled=True)  87.7 us
    psum x1, waiting for transfers between devices, broadcast(): return lax.psum(block, axis)  86.1 us
    gather x1, local copies, waits for them, and re-layouts, body(): projected[safe_rows]  65.2 us
    scatter-add x6, other arithmetic, add_tile(): return accumulated.at[targets].add(contribution)  60.9 us
    dot_general x6, matrix products, add_tile(): jnp.einsum('bij,bih->bjh', tile_slab, grad_blocks, preferred_element_type...  23.7 us
  transfers between devices with their start and end apart: 5, of which 4 were waited for; matrix products, arithmetic and copies ran while one was open for 7% of the time, Pallas kernels for 0%

commit v1 on v0

v1 whole, which is shorter than its diff:
```python
import functools

import jax
import jax.numpy as jnp
from jax import lax
from jax.experimental import pallas as pl
from jax.experimental.pallas import tpu as pltpu
from jax.sharding import PartitionSpec as P

BF = jnp.bfloat16
F32 = jnp.float32
VMEM_LIMIT = 56 * 2**20
UNROLL = 32
PAD = 8
GELU_A = 0.7978845608028654
GELU_B = 0.044715


def hub_gather_kernel(rows_ref, x_ref, out_ref, wide):
    peers, sections, width = out_ref.shape
    wide[...] = x_ref[...].astype(F32)
    group = 16

    def body(step, carry):
        first = step * group
        for section in range(sections):
            for slot in range(group):
                row = rows_ref[section * peers + first + slot]
                out_ref[first + slot, section : section + 1, :] = wide[pl.ds(row, 1), :]
        return carry

    lax.fori_loop(0, peers // group, body, 0)


def hub_gather(features, hub_rows):
    sections, peers = hub_rows.shape
    rows, width = features.shape
    return pl.pallas_call(
        hub_gather_kernel,
        grid_spec=pltpu.PrefetchScalarGridSpec(
            num_scalar_prefetch=1,
            grid=(1,),
            in_specs=[pl.BlockSpec((rows, width), lambda i, *_: (0, 0))],
            out_specs=pl.BlockSpec((peers, sections, width), lambda i, *_: (0, 0, 0)),
            scratch_shapes=[pltpu.VMEM((rows, width), F32)],
        ),
        out_shape=jax.ShapeDtypeStruct((peers, sections, width), F32),
        compiler_params=pltpu.CompilerParams(vmem_limit_bytes=VMEM_LIMIT),
    )(hub_rows.reshape(-1), features)


def live_groups(list_ref, start, slots, group):
    count = jnp.int32(0)
    for first in range(0, slots, group):
        count = count + (list_ref[start + first] >= 0).astype(jnp.int32)
    return count


def gather_kernel(lists, list_ref, x_ref, out_ref, wide, buffer):
    step = pl.program_id(0)
    rows = x_ref.shape[0]
    slots = buffer.shape[0]

    @pl.when(step == 0)
    def _():
        wide[pl.ds(0, PAD), :] = jnp.zeros((PAD, wide.shape[1]), F32)
        wide[pl.ds(PAD, rows), :] = x_ref[...].astype(F32)

    for k in range(lists):
        start = (step * lists + k) * slots
        buffer[...] = jnp.zeros_like(buffer)

        def body(group, carry):
            base = pl.multiple_of(group * UNROLL, UNROLL)
            for slot in range(UNROLL):
                row = list_ref[start + base + slot]
                buffer[pl.ds(base + slot, 1), :] = wide[pl.ds(row + PAD, 1), :]
            return carry

        lax.fori_loop(0, live_groups(list_ref, start, slots, UNROLL), body, 0)
        out_ref[k] = buffer[...].astype(BF)


def gather_rows(features, send_lists):
    peers, slots = send_lists.shape
    rows, width = features.shape
    lists = 8
    return pl.pallas_call(
        functools.partial(gather_kernel, lists),
        grid_spec=pltpu.PrefetchScalarGridSpec(
            num_scalar_prefetch=1,
            grid=(peers // lists,),
            in_specs=[pl.BlockSpec((rows, width), lambda i, *_: (0, 0))],
            out_specs=pl.BlockSpec((lists, slots, width), lambda i, *_: (i, 0, 0)),
            scratch_shapes=[
                pltpu.VMEM((rows + PAD, width), F32),
                pltpu.VMEM((slots, width), F32),
            ],
        ),
        out_shape=jax.ShapeDtypeStruct((peers, slots, width), BF),
        compiler_params=pltpu.CompilerParams(vmem_limit_bytes=VMEM_LIMIT),
    )(send_lists.reshape(-1), features)


def layer_kernel(
    group,
    columns_ref,
    x_hbm,
    halo_hbm,
    hub_ref,
    w_ref,
    tiles_ref,
    hub_tiles_ref,
    cot_ref,
    out_ref,
    send_ref,
    own_ref,
    features,
    adjoint,
    hub_adjoint,
    grad_w,
    extra,
    sems,
):
    step = pl.program_id(0)
    steps = pl.num_programs(0)
    per_block = tiles_ref.shape[1]
    blk = tiles_ref.shape[2]
    own_blocks = x_hbm.shape[0]
    peers = halo_hbm.shape[0]
    sections = hub_tiles_ref.shape[0]
    width = hub_ref.shape[1]

    @pl.when(step == 0)
    def _():
        own = pltpu.make_async_copy(x_hbm, features.at[pl.ds(0, own_blocks)], sems.at[0])
        halo = pltpu.make_async_copy(halo_hbm, features.at[pl.ds(own_blocks, peers)], sems.at[1])
        own.start()
        halo.start()

        def clear(block, carry):
            adjoint[block] = jnp.zeros((width, blk), F32)
            return carry

        lax.fori_loop(0, own_blocks + peers, clear, 0, unroll=4)
        hub_adjoint[...] = jnp.zeros_like(hub_adjoint)
        grad_w[...] = jnp.zeros_like(grad_w)
        own.wait()
        halo.wait()

    weight = w_ref[...]
    weight_twice = jnp.concatenate([weight, weight], axis=0)
    hub_slab = jnp.concatenate([hub_tiles_ref[s] for s in range(sections)], axis=1)
    hub_part = jnp.dot(hub_slab, hub_ref[...], preferred_element_type=F32)
    projected_back = []
    for u in range(group):
        places = [columns_ref[(step * group + u) * per_block + t] for t in range(per_block)]
        slab = jnp.concatenate([tiles_ref[u, t] for t in range(per_block)], axis=1)
        blocks = jnp.concatenate([features[place] for place in places], axis=0)
        rows = pl.ds(u * blk, blk)
        z = jnp.dot(slab, blocks, preferred_element_type=F32) + hub_part[u * blk : (u + 1) * blk]
        z_high = z.astype(BF)
        z_low = (z - z_high.astype(F32)).astype(BF)
        preact = jnp.dot(
            jnp.concatenate([z_high, z_low], axis=1), weight_twice, preferred_element_type=F32
        )
        square = preact * preact
        t = jnp.tanh(preact * (GELU_A + (GELU_A * GELU_B) * square))
        half = 0.5 * (1.0 + t)
        out_ref[rows, :] = (preact * half).astype(BF)
        slope = half + (0.5 * preact) * (1.0 - t * t) * (GELU_A + (3.0 * GELU_A * GELU_B) * square)
        grad = (cot_ref[rows, :].astype(F32) * slope).astype(BF)
        grad_w[...] += lax.dot_general(
            z_high, grad, (((0,), (0,)), ((), ())), preferred_element_type=F32
        )
        back = lax.dot_general(
            weight, grad, (((1,), (1,)), ((), ())), preferred_element_type=F32
        ).astype(BF)
        projected_back.append(back)
        spread = jnp.dot(back, slab, preferred_element_type=F32)
        for t in range(per_block):
            adjoint[places[t]] += spread[:, t * blk : (t + 1) * blk]
    hub_adjoint[...] += jnp.dot(
        jnp.concatenate(projected_back, axis=1), hub_slab, preferred_element_type=F32
    )

    @pl.when(step == steps - 1)
    def _():
        for s in range(sections):
            extra[:, s, :] = hub_adjoint[:, s * blk : (s + 1) * blk].T
        total = grad_w[...]
        high = total.astype(BF).astype(F32)
        low = total - high
        pieces = total.shape[1] // width
        for piece in range(pieces):
            part = slice(piece * width, (piece + 1) * width)
            extra[:, sections + piece, :] = high[:, part]
            extra[:, sections + pieces + piece, :] = low[:, part]

        def finish_own(block, carry):
            own_ref[pl.ds(pl.multiple_of(block * blk, blk), blk), :] = adjoint[block].T
            return carry

        lax.fori_loop(0, own_blocks, finish_own, 0, unroll=4)

        def finish_halo(peer, carry):
            turned = adjoint[own_blocks + peer].T
            send_ref[peer] = jnp.concatenate([turned, extra[peer]], axis=0).astype(BF)
            return carry

        lax.fori_loop(0, peers, finish_halo, 0, unroll=4)


def layer(features, halo, hub, weight, tiles, tile_columns, hub_tiles, cotangent):
    blocks, per_block, blk, _ = tiles.shape
    peers = halo.shape[0]
    width, width_out = weight.shape
    sections = hub_tiles.shape[0]
    rows = blocks * blk
    group = 4
    extras = sections + 2 * (width_out // width)
    return pl.pallas_call(
        functools.partial(layer_kernel, group),
        grid_spec=pltpu.PrefetchScalarGridSpec(
            num_scalar_prefetch=1,
            grid=(blocks // group,),
            in_specs=[
                pl.BlockSpec(memory_space=pl.ANY),
                pl.BlockSpec(memory_space=pl.ANY),
                pl.BlockSpec((sections * blk, width), lambda i, *_: (0, 0)),
                pl.BlockSpec((width, width_out), lambda i, *_: (0, 0)),
                pl.BlockSpec((group, per_block, blk, blk), lambda i, *_: (i, 0, 0, 0)),
                pl.BlockSpec((sections, group * blk, blk), lambda i, *_: (0, i, 0)),
                pl.BlockSpec((group * blk, width_out), lambda i, *_: (i, 0)),
            ],
            out_specs=[
                pl.BlockSpec((group * blk, width_out), lambda i, *_: (i, 0)),
                pl.BlockSpec((peers, blk + extras, width), lambda i, *_: (0, 0, 0)),
                pl.BlockSpec((rows, width), lambda i, *_: (0, 0)),
            ],
            scratch_shapes=[
                pltpu.VMEM((blocks + peers, blk, width), BF),
                pltpu.VMEM((blocks + peers, width, blk), F32),
                pltpu.VMEM((width, sections * blk), F32),
                pltpu.VMEM((width, width_out), F32),
                pltpu.VMEM((peers, extras, width), F32),
                pltpu.SemaphoreType.DMA((2,)),
            ],
        ),
        out_shape=[
            jax.ShapeDtypeStruct((rows, width_out), BF),
            jax.ShapeDtypeStruct((peers, blk + extras, width), BF),
            jax.ShapeDtypeStruct((rows, width), F32),
        ],
        compiler_params=pltpu.CompilerParams(vmem_limit_bytes=VMEM_LIMIT),
    )(
        tile_columns.reshape(-1),
        features.reshape(blocks, blk, width),
        halo,
        hub,
        weight,
        tiles,
        hub_tiles,
        cotangent,
    )


def scatter_kernel(lists, list_ref, back_ref, own_ref, out_ref, t0, t1, t2, t3, buffer):
    step = pl.program_id(0)
    steps = pl.num_programs(0)
    totals = (t0, t1, t2, t3)
    slots = buffer.shape[0]
    rows = own_ref.shape[0]

    @pl.when(step == 0)
    def _():
        for total in totals:
            total[...] = jnp.zeros_like(total)

    for k in range(lists):
        start = (step * lists + k) * slots
        buffer[...] = back_ref[k, :slots, :].astype(F32)

        def body(group, carry):
            base = pl.multiple_of(group * UNROLL, UNROLL)
            for slot in range(0, UNROLL, 4):
                places = [list_ref[start + base + slot + v] + PAD for v in range(4)]
                sums = [
                    totals[v][pl.ds(places[v], 1), :] + buffer[pl.ds(base + slot + v, 1), :]
                    for v in range(4)
                ]
                for v in range(4):
                    totals[v][pl.ds(places[v], 1), :] = sums[v]
            return carry

        lax.fori_loop(0, live_groups(list_ref, start, slots, UNROLL), body, 0)

    @pl.when(step == steps - 1)
    def _():
        live = pl.ds(PAD, rows)
        out_ref[...] = ((t0[live, :] + t1[live, :]) + (t2[live, :] + t3[live, :])) + own_ref[...]


def scatter_rows(send_lists, returned, own):
    peers, slots = send_lists.shape
    rows, width = own.shape
    lists = 8
    return pl.pallas_call(
        functools.partial(scatter_kernel, lists),
        grid_spec=pltpu.PrefetchScalarGridSpec(
            num_scalar_prefetch=1,
            grid=(peers // lists,),
            in_specs=[
                pl.BlockSpec((lists, returned.shape[1], width), lambda i, *_: (i, 0, 0)),
                pl.BlockSpec((rows, width), lambda i, *_: (0, 0)),
            ],
            out_specs=pl.BlockSpec((rows, width), lambda i, *_: (0, 0)),
            scratch_shapes=[pltpu.VMEM((rows + PAD, width), F32)] * 4
            + [pltpu.VMEM((slots, width), F32)],
        ),
        out_shape=jax.ShapeDtypeStruct((rows, width), F32),
        compiler_params=pltpu.CompilerParams(vmem_limit_bytes=VMEM_LIMIT),
    )(send_lists.reshape(-1), returned, own)


def finish_kernel(owned_ref, rows_ref, hub_ref, total_ref, out_ref, total):
    sections, peers, _ = hub_ref.shape
    total[...] = total_ref[...]
    group = 16
    for section in range(sections):

        @pl.when(owned_ref[section] != 0)
        def _():
            def body(step, carry):
                first = pl.multiple_of(step * group, group)
                for slot in range(group):
                    row = rows_ref[section * peers + first + slot]
                    total[pl.ds(row, 1), :] += hub_ref[section, pl.ds(first + slot, 1), :]
                return carry

            lax.fori_loop(0, peers // group, body, 0)

    out_ref[...] = total[...].astype(BF)


def finish(total, hub_sums, hub_rows, owned):
    rows, width = total.shape
    sections, peers, _ = hub_sums.shape
    return pl.pallas_call(
        finish_kernel,
        grid_spec=pltpu.PrefetchScalarGridSpec(
            num_scalar_prefetch=2,
            grid=(1,),
            in_specs=[
                pl.BlockSpec((sections, peers, width), lambda i, *_: (0, 0, 0)),
                pl.BlockSpec((rows, width), lambda i, *_: (0, 0)),
            ],
            out_specs=pl.BlockSpec((rows, width), lambda i, *_: (0, 0)),
            scratch_shapes=[pltpu.VMEM((rows, width), F32)],
        ),
        out_shape=jax.ShapeDtypeStruct((rows, width), BF),
        compiler_params=pltpu.CompilerParams(vmem_limit_bytes=VMEM_LIMIT),
    )(owned.astype(jnp.int32), hub_rows.reshape(-1), hub_sums, total)


def exchange(array):
    return lax.all_to_all(array, "rows", split_axis=0, concat_axis=0, tiled=True)


def body(
    features,
    weight,
    adjacency_tiles,
    tile_columns,
    send_rows,
    hub_owner,
    hub_rows,
    hub_tiles,
    cotangent,
):
    device = lax.axis_index("rows")
    sections, peers = hub_rows.shape
    width, width_out = weight.shape
    pieces = width_out // width
    send_lists = send_rows[0]

    hub_out = hub_gather(features, hub_rows).astype(BF)
    hub_in = exchange(hub_out)
    hub_mine = hub_in[hub_owner, jnp.arange(sections)]
    hub_all = lax.all_gather(hub_mine, "rows")
    hub = hub_all.transpose(1, 0, 2).reshape(sections * peers, width)

    outgoing = gather_rows(features, send_lists)
    halo = exchange(outgoing)
    output, adjoint, own = layer(
        features, halo, hub, weight, adjacency_tiles, tile_columns, hub_tiles, cotangent
    )
    returned = exchange(adjoint)

    blk = send_lists.shape[1]
    sums = jnp.sum(returned[:, blk:, :].astype(F32), axis=0)
    weight_row = sums[sections : sections + pieces] + sums[sections + pieces :]
    high = weight_row.astype(BF)
    low = (weight_row - high.astype(F32)).astype(BF)
    mine = jnp.concatenate([sums[:sections].astype(BF), high, low], axis=0)
    everyone = exchange(jnp.broadcast_to(mine[None], (peers,) + mine.shape)).astype(F32)

    total = scatter_rows(send_lists, returned, own)
    hub_sums = everyone[:, :sections].transpose(1, 0, 2)
    grad_weight = everyone[:, sections : sections + pieces] + everyone[:, sections + pieces :]
    grad_features = finish(total, hub_sums, hub_rows, hub_owner == device)
    return (output, grad_features, grad_weight.reshape(width, width_out))


def solution(mesh):
    return jax.shard_map(
        body,
        mesh=mesh,
        in_specs=(
            P("rows", None),
            P(),
            P("rows", None, None, None),
            P("rows", None),
            P("rows", None, None),
            P(),
            P(),
            P(None, "rows", None),
            P("rows", None),
        ),
        out_specs=(P("rows", None), P("rows", None), P()),
        check_vma=False,
    )
```

time: 942 us -> 257 us (0.27)
  waiting for transfers between devices: 524 us -> 0.01 us
  other arithmetic: 200 us -> 2.4 us
  blocking collectives: 0 us -> 136 us
  local copies, waits for them, and re-layouts: 123 us -> 6.35 us
  Pallas kernels: 0 us -> 82.2 us
  matrix products: 57.2 us -> 0 us
  between operations: 16.6 us -> 0.72 us
    psum x3 -> x0, waiting for transfers between devices: 436 us -> none  [the longest x1 216 us: body(): hub_sums = lax.psum(hub_terms, 'rows')]
    scatter-add x8 -> x0, other arithmetic: 169 us -> none  [the longest x1 101 us: body(): grad_proj.at[safe_rows.reshape(-1)].add(returned.reshape(-1, width_out))]
    all_to_all x2 -> x3, waiting for transfers between devices: 87.7 us -> 0.01 us  [exchange(): lax.all_to_all(array, 'rows', split_axis=0, concat_axis=0, tiled=True)]
    pallas_call x0 -> x5, Pallas kernels: none -> 82.2 us  [the longest x1 33.5 us: layer(): pl.pallas_call(functools.partial(layer_kernel, group), grid_spec=pltpu.Pr...]
    gather x10 -> x1, local copies, waits for them, and re-layouts: 81.3 us -> 0.58 us  [body(): hub_mine = hub_in[hub_owner, jnp.arange(sections)]]
    all_gather x0 -> x1, blocking collectives: none -> 75.8 us  [body(): hub_all = lax.all_gather(hub_mine, 'rows')]
    all_to_all x0 -> x1, blocking collectives: none -> 60.6 us  [exchange(): lax.all_to_all(array, 'rows', split_axis=0, concat_axis=0, tiled=True)]
    dot_general x12 -> x0, matrix products: 57.2 us -> none  [the longest x6 23.7 us: add_tile(): jnp.einsum('bij,bih->bjh', tile_slab, grad_blocks, preferred_element_type...]
  transfers between devices with their start and end apart: 5 -> 3, of which waited for: 4 -> 0; matrix products, arithmetic and copies ran while one was open for 7% -> 1% of each run, Pallas kernels for 0% -> 16%
where the time goes in v1:
time: 257 us; the launch traced here: 256 us
  blocking collectives  136 us (53%)
  Pallas kernels  82.2 us (32%)
  starting transfers between devices  27.6 us (11%)
  local copies, waits for them, and re-layouts  6.35 us (2%)
    all_gather x1, blocking collectives, body(): hub_all = lax.all_gather(hub_mine, 'rows')  75.8 us
    all_to_all x1, blocking collectives, exchange(): lax.all_to_all(array, 'rows', split_axis=0, concat_axis=0, tiled=True)  60.6 us
    pallas_call x1, Pallas kernels, layer(): pl.pallas_call(functools.partial(layer_kernel, group), grid_spec=pltpu.Pr...  33.5 us
    all_to_all x3, starting transfers between devices, exchange(): lax.all_to_all(array, 'rows', split_axis=0, concat_axis=0, tiled=True)  27.6 us
    pallas_call x1, Pallas kernels, scatter_rows(): pl.pallas_call(functools.partial(scatter_kernel, lists), grid_spec=pltpu....  24.3 us
    pallas_call x1, Pallas kernels, gather_rows(): pl.pallas_call(functools.partial(gather_kernel, lists), grid_spec=pltpu.P...  17.6 us
  transfers between devices with their start and end apart: 3, of which 0 were waited for; matrix products, arithmetic and copies ran while one was open for 1% of the time, Pallas kernels for 16%

profile of v1, /device:TPU:1, one launch (start us, length us, event | category | flops | bytes accessed | tf_op | source)
XLA Modules:
  0.0 255.7 jit_solution(5500913846818171475)
XLA Ops:
  0.6 3.2 %shard_map.113 = f32[128,4,128]{2,1,0:T(4,128)} custom-call(s32[512]{0:T(512)} %bitcast.23, bf16[4096,128]{1,0:T(8,128)(2,1)} %x_ref.3), custom_call_target="tpu_custom_call" | custom-call | tf_op jit(solution)/shard_map/pallas_call | solution.py:38
  3.8 1.6 convert_element_type.22
  5.5 11.5 %all-to-all-start.1 = ((bf16[128,4,128]{2,1,0:T(4,128)(2,1)}), bf16[128,4,128]{2,1,0:T(4,128)(2,1)S(1)}, u32[]{:S(2)}, u32[]{:S(2)}) async-start(bf16[128,4,128]{2,1,0:T(4,128)(2,1)} %convert_element_type.22), calls=%async_computation.1 | async-start | bytes 262144 | tf_op jit(solution)/shard_map/all_to_all | solution.py:367
  17.0 17.6 %shard_map.112 = bf16[128,128,128]{2,1,0:T(8,128)(2,1)} custom-call(s32[16384]{0:T(1024)} %bitcast.21, bf16[4096,128]{1,0:T(8,128)(2,1)} %x_ref.3), custom_call_target="tpu_custom_call" | custom-call | tf_op jit(solution)/shard_map/pallas_call | solution.py:88
  34.6 0.0 copy-start.1
  34.6 0.0 copy-start.2
  34.6 0.0 all-to-all-done.1
  34.6 10.8 %all-to-all-start = ((bf16[128,128,128]{2,1,0:T(8,128)(2,1)}), bf16[128,128,128]{2,1,0:T(8,128)(2,1)}, u32[]{:S(2)}, u32[]{:S(2)}) async-start(bf16[128,128,128]{2,1,0:T(8,128)(2,1)} %shard_map.112), calls=%async_computation | async-start | bytes 8388608 | tf_op jit(solution)/shard_map/all_to_all | solution.py:367
  45.5 0.0 copy-done.1
  45.5 0.1 copy.17
  45.6 0.7 reshape.23.columns_ref
  46.2 0.0 copy-done.2
  46.2 0.6 gather_fusion
  46.8 75.8 %all-gather.1 = bf16[128,4,128]{2,1,0:T(4,128)(2,1)S(1)} all-gather(bf16[1,4,128]{2,1,0:T(4,128)(2,1)S(1)} %bitcast.25), channel_id=2, replica_groups=mesh['rows'=128] {'rows'}, dimensions={0}, use_global_device_ids=true | all-gather | bytes 132096 | tf_op jit(solution)/shard_map/all_gather | solution.py:390
  122.6 0.7 copy.18
  123.3 0.0 all-to-all-done.halo_hbm
  123.3 33.5 %shard_map.114 = (bf16[4096,256]{1,0:T(8,128)(2,1)}, bf16[128,136,128]{2,1,0:T(8,128)(2,1)}, f32[4096,128]{1,0:T(8,128)}) custom-call(s32[192]{0:T(256)} %reshape.23.columns_ref, bf16[32,128,128]{2,1,0:T(8,128)(2,1)} %bitcast.17, bf16[128,128,128]{2,1,0:T(8,128)(2,1)} %all-to-all-done.halo_hbm, bf16[512,128]{1,0:T(8,128)(2,1)} %bitcast.18, ...), custom_call_target="tpu_custom_call" | custom-call | tf_op jit(solution)/shard_map/pallas_call | solution.py:222
  156.8 60.6 %all_to_all.20.back_ref = bf16[128,136,128]{2,1,0:T(8,128)(2,1)S(1)} all-to-all(bf16[128,136,128]{2,1,0:T(8,128)(2,1)} %get-tuple-element.7), channel_id=1, replica_groups=mesh['rows'=128] {'rows'}, dimensions={0} | all-to-all | bytes 8912896 | tf_op jit(solution)/shard_map/all_to_all | solution.py:367
  217.4 0.0 copy-start
  217.4 2.0 copy-done
  219.4 0.1 convert_reduce_fusion
  219.6 0.7 broadcast_in_dim.5
  220.4 5.2 %all-to-all-start.3 = ((bf16[128,8,128]{2,1,0:T(8,128)(2,1)}), bf16[128,8,128]{2,1,0:T(8,128)(2,1)S(1)}, u32[]{:S(2)}, u32[]{:S(2)}) async-start(bf16[128,8,128]{2,1,0:T(8,128)(2,1)} %broadcast_in_dim.5), calls=%async_computation.3 | async-start | bytes 524288 | tf_op jit(solution)/shard_map/all_to_all | solution.py:367
  225.6 0.5 compare_convert_fusion.owned_ref
  226.1 24.3 %shard_map.115.total_ref = f32[4096,128]{1,0:T(8,128)} custom-call(s32[16384]{0:T(1024)} %bitcast.22, bf16[128,136,128]{2,1,0:T(8,128)(2,1)} %copy-done, f32[4096,128]{1,0:T(8,128)} %get-tuple-element.8.own_ref), custom_call_target="tpu_custom_call" | custom-call | tf_op jit(solution)/shard_map/pallas_call | solution.py:308
  250.5 0.0 all-to-all-done.3
  250.5 0.7 slice_bitcast_fusion.hub_ref
  251.2 0.1 copy.20
  251.3 0.8 copy.21
  252.1 3.6 %shard_map.116 = bf16[4096,128]{1,0:T(8,128)(2,1)} custom-call(s32[4]{0:T(128)} %compare_convert_fusion.owned_ref, s32[512]{0:T(512)} %bitcast.24, f32[4,128,128]{2,1,0:T(8,128)} %slice_bitcast_fusion.hub_ref, f32[4096,128]{1,0:T(8,128)} %shard_map.115.total_ref), custom_call_target="tpu_custom_call" | custom-call | tf_op jit(solution)/shard_map/pallas_call | solution.py:349
  (7 shorter events, 0.1 us)
Async XLA Ops:
  5.5 29.1 %all-to-all-start.1 = ((bf16[128,4,128]{2,1,0:T(4,128)(2,1)}), bf16[128,4,128]{2,1,0:T(4,128)(2,1)S(1)}, u32[]{:S(2)}, u32[]{:S(2)}) async-start(bf16[128,4,128]{2,1,0:T(4,128)(2,1)} %convert_element_type.22), calls=%async_computation.1 | async-start | bytes 262144 | tf_op jit(solution)/shard_map/all_to_all | solution.py:367
  34.6 10.9 %copy-start.1 = (s32[32,6]{0,1:T(8,128)S(1)}, s32[32,6]{0,1:T(8,128)}, u32[]{:S(2)}) copy-start(s32[32,6]{0,1:T(8,128)} %param.12) | copy-start | bytes 2308
  34.6 11.6 %copy-start.2 = (s32[4]{0:T(128)S(1)}, s32[4]{0:T(128)}, u32[]{:S(2)}) copy-start(s32[4]{0:T(128)} %param.14) | copy-start | bytes 52
  34.6 88.7 %all-to-all-start = ((bf16[128,128,128]{2,1,0:T(8,128)(2,1)}), bf16[128,128,128]{2,1,0:T(8,128)(2,1)}, u32[]{:S(2)}, u32[]{:S(2)}) async-start(bf16[128,128,128]{2,1,0:T(8,128)(2,1)} %shard_map.112), calls=%async_computation | async-start | bytes 8388608 | tf_op jit(solution)/shard_map/all_to_all | solution.py:367
  217.4 2.0 copy-start
  220.4 30.1 %all-to-all-start.3 = ((bf16[128,8,128]{2,1,0:T(8,128)(2,1)}), bf16[128,8,128]{2,1,0:T(8,128)(2,1)S(1)}, u32[]{:S(2)}, u32[]{:S(2)}) async-start(bf16[128,8,128]{2,1,0:T(8,128)(2,1)} %broadcast_in_dim.5), calls=%async_computation.3 | async-start | bytes 524288 | tf_op jit(solution)/shard_map/all_to_all | solution.py:367

commit v2 on v1

v2 whole, which is shorter than its diff:
```python
import functools

import jax
import jax.numpy as jnp
from jax import lax
from jax.experimental import pallas as pl
from jax.experimental.pallas import tpu as pltpu
from jax.sharding import PartitionSpec as P

BF = jnp.bfloat16
F32 = jnp.float32
MIB = 2**20
UNROLL = 32
PAD = 8
GELU_A = 0.7978845608028654
GELU_B = 0.044715


def live_groups(list_ref, start, slots, group):
    count = jnp.int32(0)
    for first in range(0, slots, group):
        count = count + (list_ref[start + first] >= 0).astype(jnp.int32)
    return count


def gather_kernel(lists, slots, list_ref, hub_ref, x_ref, out_ref, wide, buffer):
    step = pl.program_id(0)
    rows = x_ref.shape[0]
    peers = pl.num_programs(0) * lists
    sections = hub_ref.shape[0] // peers

    @pl.when(step == 0)
    def _():
        wide[pl.ds(0, PAD), :] = jnp.zeros((PAD, wide.shape[1]), F32)
        wide[pl.ds(PAD, rows), :] = x_ref[...].astype(F32)

    for k in range(lists):
        peer = step * lists + k
        start = peer * slots
        buffer[...] = jnp.zeros_like(buffer)
        for section in range(sections):
            row = hub_ref[section * peers + peer]
            buffer[slots + section : slots + section + 1, :] = wide[pl.ds(row + PAD, 1), :]

        def body(group, carry):
            base = pl.multiple_of(group * UNROLL, UNROLL)
            for slot in range(UNROLL):
                row = list_ref[start + base + slot]
                buffer[pl.ds(base + slot, 1), :] = wide[pl.ds(row + PAD, 1), :]
            return carry

        lax.fori_loop(0, live_groups(list_ref, start, slots, UNROLL), body, 0)
        out_ref[k] = buffer[...].astype(BF)


def gather_rows(features, send_lists, hub_rows):
    peers, slots = send_lists.shape
    rows, width = features.shape
    lists = 8
    height = slots + PAD
    return pl.pallas_call(
        functools.partial(gather_kernel, lists, slots),
        grid_spec=pltpu.PrefetchScalarGridSpec(
            num_scalar_prefetch=2,
            grid=(peers // lists,),
            in_specs=[pl.BlockSpec((rows, width), lambda i, *_: (0, 0))],
            out_specs=pl.BlockSpec((lists, height, width), lambda i, *_: (i, 0, 0)),
            scratch_shapes=[
                pltpu.VMEM((rows + PAD, width), F32),
                pltpu.VMEM((height, width), F32),
            ],
        ),
        out_shape=jax.ShapeDtypeStruct((peers, height, width), BF),
        compiler_params=pltpu.CompilerParams(vmem_limit_bytes=10 * MIB),
    )(send_lists.reshape(-1), hub_rows.reshape(-1), features)


def tiles_kernel(group, columns_ref, x_hbm, halo_hbm, tiles_ref, z_ref, features, sems):
    step = pl.program_id(0)
    per_block, blk = tiles_ref.shape[1:3]
    own_blocks = x_hbm.shape[0]
    peers = halo_hbm.shape[0]

    @pl.when(step == 0)
    def _():
        own = pltpu.make_async_copy(x_hbm, features.at[pl.ds(0, own_blocks)], sems.at[0])
        halo = pltpu.make_async_copy(
            halo_hbm.at[:, pl.ds(0, blk), :], features.at[pl.ds(own_blocks, peers)], sems.at[1]
        )
        own.start()
        halo.start()
        own.wait()
        halo.wait()

    for u in range(group):
        places = [columns_ref[(step * group + u) * per_block + t] for t in range(per_block)]
        slab = jnp.concatenate([tiles_ref[u, t] for t in range(per_block)], axis=1)
        blocks = jnp.concatenate([features[place] for place in places], axis=0)
        z_ref[pl.ds(u * blk, blk), :] = jnp.dot(slab, blocks, preferred_element_type=F32)


def tiles_part(features, halo, tiles, tile_columns):
    blocks, per_block, blk, _ = tiles.shape
    peers = halo.shape[0]
    width = features.shape[1]
    group = 8
    return pl.pallas_call(
        functools.partial(tiles_kernel, group),
        grid_spec=pltpu.PrefetchScalarGridSpec(
            num_scalar_prefetch=1,
            grid=(blocks // group,),
            in_specs=[
                pl.BlockSpec(memory_space=pl.ANY),
                pl.BlockSpec(memory_space=pl.ANY),
                pl.BlockSpec((group, per_block, blk, blk), lambda i, *_: (i, 0, 0, 0)),
            ],
            out_specs=pl.BlockSpec((group * blk, width), lambda i, *_: (i, 0)),
            scratch_shapes=[
                pltpu.VMEM((blocks + peers, blk, width), BF),
                pltpu.SemaphoreType.DMA((2,)),
            ],
        ),
        out_shape=jax.ShapeDtypeStruct((blocks * blk, width), F32),
        compiler_params=pltpu.CompilerParams(vmem_limit_bytes=14 * MIB),
    )(tile_columns.reshape(-1), features.reshape(blocks, blk, width), halo, tiles)


def layer_kernel(
    group,
    steps,
    columns_ref,
    z_ref,
    hub_ref,
    w_ref,
    tiles_ref,
    hub_tiles_ref,
    cot_ref,
    out_ref,
    send_ref,
    own_ref,
    adjoint,
    hub_adjoint,
    grad_w,
    extra,
):
    step = pl.program_id(0)
    per_block, blk = tiles_ref.shape[1:3]
    sections = hub_tiles_ref.shape[0]
    width = hub_ref.shape[1]
    own_part = own_ref.shape[0] // blk
    send_part = send_ref.shape[0]
    finals = pl.num_programs(0) - steps
    own_blocks = finals * own_part

    @pl.when(step == 0)
    def _():
        def clear(block, carry):
            adjoint[block] = jnp.zeros((blk, width), F32)
            return carry

        lax.fori_loop(0, adjoint.shape[0], clear, 0, unroll=4)
        hub_adjoint[...] = jnp.zeros_like(hub_adjoint)
        grad_w[...] = jnp.zeros_like(grad_w)

    @pl.when(step < steps)
    def _():
        weight = w_ref[...]
        weight_twice = jnp.concatenate([weight, weight], axis=0)
        hub_slab = jnp.concatenate([hub_tiles_ref[s] for s in range(sections)], axis=1)
        z = z_ref[...] + jnp.dot(hub_slab, hub_ref[...], preferred_element_type=F32)
        z_high = z.astype(BF)
        z_low = (z - z_high.astype(F32)).astype(BF)
        preact = jnp.dot(
            jnp.concatenate([z_high, z_low], axis=1), weight_twice, preferred_element_type=F32
        )
        square = preact * preact
        t = jnp.tanh(preact * (GELU_A + (GELU_A * GELU_B) * square))
        half = 0.5 + 0.5 * t
        out_ref[...] = (preact * half).astype(BF)
        slope = half + (0.5 * preact) * (1.0 - t * t) * (GELU_A + (3.0 * GELU_A * GELU_B) * square)
        grad = (cot_ref[...].astype(F32) * slope).astype(BF)
        grad_w[...] += lax.dot_general(
            z_high, grad, (((0,), (0,)), ((), ())), preferred_element_type=F32
        )
        back = lax.dot_general(
            grad, weight, (((1,), (1,)), ((), ())), preferred_element_type=F32
        ).astype(BF)
        hub_adjoint[...] += lax.dot_general(
            hub_slab, back, (((0,), (0,)), ((), ())), preferred_element_type=F32
        )
        for u in range(group):
            places = [columns_ref[(step * group + u) * per_block + t] for t in range(per_block)]
            slab = jnp.concatenate([tiles_ref[u, t] for t in range(per_block)], axis=1)
            spread = lax.dot_general(
                slab,
                back[u * blk : (u + 1) * blk],
                (((0,), (0,)), ((), ())),
                preferred_element_type=F32,
            )
            for t in range(per_block):
                adjoint[places[t]] += spread[t * blk : (t + 1) * blk]

    @pl.when(step == steps)
    def _():
        for s in range(sections):
            extra[:, s, :] = hub_adjoint[s * blk : (s + 1) * blk, :]
        total = grad_w[...]
        high = total.astype(BF).astype(F32)
        low = total - high
        pieces = total.shape[1] // width
        for piece in range(pieces):
            part = slice(piece * width, (piece + 1) * width)
            extra[:, sections + piece, :] = high[:, part]
            extra[:, sections + pieces + piece, :] = low[:, part]

    @pl.when(step >= steps)
    def _():
        final = step - steps
        for block in range(own_part):
            own_ref[pl.ds(block * blk, blk), :] = adjoint[final * own_part + block]

        def finish(k, carry):
            peer = final * send_part + k
            rows = jnp.concatenate([adjoint[own_blocks + peer], extra[peer]], axis=0)
            send_ref[k] = rows.astype(BF)
            return carry

        lax.fori_loop(0, send_part, finish, 0, unroll=4)


def layer(z, hub, weight, tiles, tile_columns, hub_tiles, cotangent, peers):
    blocks, per_block, blk, _ = tiles.shape
    width, width_out = weight.shape
    sections = hub_tiles.shape[0]
    rows = blocks * blk
    group = 8
    steps = blocks // group
    finals = 4
    extras = sections + 2 * (width_out // width)

    def work(i):
        return jnp.minimum(i, steps - 1)

    def final(i):
        return jnp.maximum(i - steps, 0)

    return pl.pallas_call(
        functools.partial(layer_kernel, group, steps),
        grid_spec=pltpu.PrefetchScalarGridSpec(
            num_scalar_prefetch=1,
            grid=(steps + finals,),
            in_specs=[
                pl.BlockSpec((group * blk, width), lambda i, *_: (work(i), 0)),
                pl.BlockSpec((sections * blk, width), lambda i, *_: (0, 0)),
                pl.BlockSpec((width, width_out), lambda i, *_: (0, 0)),
                pl.BlockSpec((group, per_block, blk, blk), lambda i, *_: (work(i), 0, 0, 0)),
                pl.BlockSpec((sections, group * blk, blk), lambda i, *_: (0, work(i), 0)),
                pl.BlockSpec((group * blk, width_out), lambda i, *_: (work(i), 0)),
            ],
            out_specs=[
                pl.BlockSpec((group * blk, width_out), lambda i, *_: (work(i), 0)),
                pl.BlockSpec((peers // finals, blk + extras, width), lambda i, *_: (final(i), 0, 0)),
                pl.BlockSpec((rows // finals, width), lambda i, *_: (final(i), 0)),
            ],
            scratch_shapes=[
                pltpu.VMEM((blocks + peers, blk, width), F32),
                pltpu.VMEM((sections * blk, width), F32),
                pltpu.VMEM((width, width_out), F32),
                pltpu.VMEM((peers, extras, width), F32),
            ],
        ),
        out_shape=[
            jax.ShapeDtypeStruct((rows, width_out), BF),
            jax.ShapeDtypeStruct((peers, blk + extras, width), BF),
            jax.ShapeDtypeStruct((rows, width), F32),
        ],
        compiler_params=pltpu.CompilerParams(vmem_limit_bytes=32 * MIB),
    )(tile_columns.reshape(-1), z, hub, weight, tiles, hub_tiles, cotangent)


def scatter_kernel(lists, list_ref, back_ref, own_ref, out_ref, t0, t1, t2, t3, buffer):
    step = pl.program_id(0)
    steps = pl.num_programs(0)
    totals = (t0, t1, t2, t3)
    slots = buffer.shape[0]
    rows = own_ref.shape[0]

    @pl.when(step == 0)
    def _():
        for total in totals:
            total[...] = jnp.zeros_like(total)

    for k in range(lists):
        start = (step * lists + k) * slots
        buffer[...] = back_ref[k, :slots, :].astype(F32)

        def body(group, carry):
            base = pl.multiple_of(group * UNROLL, UNROLL)
            for slot in range(0, UNROLL, 4):
                places = [list_ref[start + base + slot + v] + PAD for v in range(4)]
                sums = [
                    totals[v][pl.ds(places[v], 1), :] + buffer[pl.ds(base + slot + v, 1), :]
                    for v in range(4)
                ]
                for v in range(4):
                    totals[v][pl.ds(places[v], 1), :] = sums[v]
            return carry

        lax.fori_loop(0, live_groups(list_ref, start, slots, UNROLL), body, 0)

    @pl.when(step == steps - 1)
    def _():
        live = pl.ds(PAD, rows)
        out_ref[...] = ((t0[live, :] + t1[live, :]) + (t2[live, :] + t3[live, :])) + own_ref[...]


def scatter_rows(send_lists, returned, own):
    peers, slots = send_lists.shape
    rows, width = own.shape
    lists = 8
    return pl.pallas_call(
        functools.partial(scatter_kernel, lists),
        grid_spec=pltpu.PrefetchScalarGridSpec(
            num_scalar_prefetch=1,
            grid=(peers // lists,),
            in_specs=[
                pl.BlockSpec((lists, returned.shape[1], width), lambda i, *_: (i, 0, 0)),
                pl.BlockSpec((rows, width), lambda i, *_: (0, 0)),
            ],
            out_specs=pl.BlockSpec((rows, width), lambda i, *_: (0, 0)),
            scratch_shapes=[pltpu.VMEM((rows + PAD, width), F32)] * 4
            + [pltpu.VMEM((slots, width), F32)],
        ),
        out_shape=jax.ShapeDtypeStruct((rows, width), F32),
        compiler_params=pltpu.CompilerParams(vmem_limit_bytes=24 * MIB),
    )(send_lists.reshape(-1), returned, own)


def finish_kernel(owned_ref, rows_ref, hub_ref, total_ref, out_ref, total):
    sections, peers, _ = hub_ref.shape
    total[...] = total_ref[...]
    group = 16
    for section in range(sections):

        @pl.when(owned_ref[section] != 0)
        def _():
            def body(step, carry):
                first = pl.multiple_of(step * group, group)
                for slot in range(group):
                    row = rows_ref[section * peers + first + slot]
                    total[pl.ds(row, 1), :] += hub_ref[section, pl.ds(first + slot, 1), :]
                return carry

            lax.fori_loop(0, peers // group, body, 0)

    out_ref[...] = total[...].astype(BF)


def finish(total, hub_sums, hub_rows, owned):
    rows, width = total.shape
    sections, peers, _ = hub_sums.shape
    return pl.pallas_call(
        finish_kernel,
        grid_spec=pltpu.PrefetchScalarGridSpec(
            num_scalar_prefetch=2,
            grid=(1,),
            in_specs=[
                pl.BlockSpec((sections, peers, width), lambda i, *_: (0, 0, 0)),
                pl.BlockSpec((rows, width), lambda i, *_: (0, 0)),
            ],
            out_specs=pl.BlockSpec((rows, width), lambda i, *_: (0, 0)),
            scratch_shapes=[pltpu.VMEM((rows, width), F32)],
        ),
        out_shape=jax.ShapeDtypeStruct((rows, width), BF),
        compiler_params=pltpu.CompilerParams(vmem_limit_bytes=12 * MIB),
    )(owned.astype(jnp.int32), hub_rows.reshape(-1), hub_sums, total)


def exchange(array):
    return lax.all_to_all(array, "rows", split_axis=0, concat_axis=0, tiled=True)


def body(
    features,
    weight,
    adjacency_tiles,
    tile_columns,
    send_rows,
    hub_owner,
    hub_rows,
    hub_tiles,
    cotangent,
):
    device = lax.axis_index("rows")
    sections, peers = hub_rows.shape
    width, width_out = weight.shape
    pieces = width_out // width
    send_lists = send_rows[0]

    blk = send_lists.shape[1]
    halo = exchange(gather_rows(features, send_lists, hub_rows))
    hub_mine = halo[hub_owner, blk + jnp.arange(sections)]
    hub_all = exchange(jnp.broadcast_to(hub_mine[None], (peers, sections, width)))
    hub = hub_all.transpose(1, 0, 2).reshape(sections * peers, width)
    z = tiles_part(features, halo, adjacency_tiles, tile_columns)
    output, adjoint, own = layer(
        z, hub, weight, adjacency_tiles, tile_columns, hub_tiles, cotangent, peers
    )
    returned = exchange(adjoint)

    sums = jnp.sum(returned[:, blk:, :].astype(F32), axis=0)
    weight_row = sums[sections : sections + pieces] + sums[sections + pieces :]
    high = weight_row.astype(BF)
    low = (weight_row - high.astype(F32)).astype(BF)
    mine = jnp.concatenate([sums[:sections].astype(BF), high, low], axis=0)
    everyone = exchange(jnp.broadcast_to(mine[None], (peers,) + mine.shape)).astype(F32)

    total = scatter_rows(send_lists, returned, own)
    hub_sums = everyone[:, :sections].transpose(1, 0, 2)
    grad_weight = everyone[:, sections : sections + pieces] + everyone[:, sections + pieces :]
    grad_features = finish(total, hub_sums, hub_rows, hub_owner == device)
    return (output, grad_features, grad_weight.reshape(width, width_out))


def solution(mesh):
    return jax.shard_map(
        body,
        mesh=mesh,
        in_specs=(
            P("rows", None),
            P(),
            P("rows", None, None, None),
            P("rows", None),
            P("rows", None, None),
            P(),
            P(),
            P(None, "rows", None),
            P("rows", None),
        ),
        out_specs=(P("rows", None), P("rows", None), P()),
        check_vma=False,
    )
```

time: 257 us -> 226 us (0.88)
  blocking collectives: 136 us -> 63.8 us
  waiting for transfers between devices: 0.01 us -> 57.2 us
  Pallas kernels: 82.2 us -> 56.3 us
  local copies, waits for them, and re-layouts: 6.35 us -> 23.9 us
  starting transfers between devices: 27.6 us -> 22.8 us
    all_gather x1 -> x0, blocking collectives: 75.8 us -> none  [body(): hub_all = lax.all_gather(hub_mine, 'rows')]
    all_to_all x3, waiting for transfers between devices: 0.01 us -> 57.2 us  [exchange(): lax.all_to_all(array, 'rows', split_axis=0, concat_axis=0, tiled=True)]
    pallas_call x3, Pallas kernels: 54.3 us -> 33.5 us  [the longest x1 15.1 us: gather_rows(): pl.pallas_call(functools.partial(gather_kernel, lists, slots), grid_spec=...]
    unnamed x8 -> x38, local copies, waits for them, and re-layouts: 2.88 us -> 20.9 us
    all_to_all x3, starting transfers between devices: 27.6 us -> 22.8 us  [exchange(): lax.all_to_all(array, 'rows', split_axis=0, concat_axis=0, tiled=True)]
    pallas_call x1, Pallas kernels: 24.3 us -> 21.1 us  [scatter_rows(): pl.pallas_call(functools.partial(scatter_kernel, lists), grid_spec=pltpu....]
    all_to_all x1, blocking collectives: 60.6 us -> 63.8 us  [exchange(): lax.all_to_all(array, 'rows', split_axis=0, concat_axis=0, tiled=True)]
  transfers between devices with their start and end apart: 3 -> 3, of which waited for: 0 -> 2; matrix products, arithmetic and copies ran while one was open for 1% -> 0% of each run, Pallas kernels for 16% -> 12%
where the time goes in v2:
time: 226 us; the launch traced here: 225 us
  blocking collectives  63.8 us (28%)
  waiting for transfers between devices  57.2 us (25%)
  Pallas kernels  56.3 us (25%)
  local copies, waits for them, and re-layouts  23.9 us (11%)
  starting transfers between devices  22.8 us (10%)
    all_to_all x1, blocking collectives, exchange(): lax.all_to_all(array, 'rows', split_axis=0, concat_axis=0, tiled=True)  63.8 us
    all_to_all x3, waiting for transfers between devices, exchange(): lax.all_to_all(array, 'rows', split_axis=0, concat_axis=0, tiled=True)  57.2 us
    all_to_all x3, starting transfers between devices, exchange(): lax.all_to_all(array, 'rows', split_axis=0, concat_axis=0, tiled=True)  22.8 us
    pallas_call x1, Pallas kernels, scatter_rows(): pl.pallas_call(functools.partial(scatter_kernel, lists), grid_spec=pltpu....  21.1 us
    unnamed x38, local copies, waits for them, and re-layouts  20.9 us
    pallas_call x1, Pallas kernels, gather_rows(): pl.pallas_call(functools.partial(gather_kernel, lists, slots), grid_spec=...  15.1 us
    pallas_call x1, Pallas kernels, layer(): pl.pallas_call(functools.partial(layer_kernel, group, steps), grid_spec=p...  13.2 us
    pallas_call x1, Pallas kernels, tiles_part(): pl.pallas_call(functools.partial(tiles_kernel, group), grid_spec=pltpu.Pr...  5.13 us
  transfers between devices with their start and end apart: 3, of which 2 were waited for; matrix products, arithmetic and copies ran while one was open for 0% of the time, Pallas kernels for 12%

profile of v2, /device:TPU:1, one launch (start us, length us, event | category | flops | bytes accessed | tf_op | source)
XLA Modules:
  0.0 225.2 jit_solution(957402808159229470)
XLA Ops:
  0.6 0.0 copy-start.6
  0.6 1.2 copy-done.6
  1.9 0.0 copy-start.11
  1.9 0.8 copy-done.11
  2.7 0.0 copy-start.14
  2.7 0.7 copy-done.14
  3.4 15.1 %shard_map.112 = bf16[128,136,128]{2,1,0:T(8,128)(2,1)S(1)} custom-call(s32[16384]{0:T(1024)S(1)} %bitcast.16, s32[512]{0:T(512)S(1)} %bitcast.18, bf16[4096,128]{1,0:T(8,128)(2,1)S(1)} %copy-done.6), custom_call_target="tpu_custom_call" | custom-call | tf_op jit(solution)/shard_map/pallas_call | solution.py:61
  18.5 0.0 copy-start.4
  18.5 2.1 copy-done.4
  20.5 0.0 copy-start.17
  20.5 0.0 copy-start.16
  20.6 0.0 copy-start.7
  20.6 11.9 %all-to-all-start = ((bf16[128,136,128]{2,1,0:T(8,128)(2,1)}), bf16[128,136,128]{2,1,0:T(8,128)(2,1)}, u32[]{:S(2)}, u32[]{:S(2)}) async-start(bf16[128,136,128]{2,1,0:T(8,128)(2,1)} %copy-done.4), calls=%async_computation | async-start | bytes 8912896 | tf_op jit(solution)/shard_map/all_to_all | solution.py:380
  32.4 0.0 copy-done.17
  32.5 55.6 %all-to-all-done.halo_hbm = bf16[128,136,128]{2,1,0:T(8,128)(2,1)} async-done(((bf16[128,136,128]{2,1,0:T(8,128)(2,1)}), bf16[128,136,128]{2,1,0:T(8,128)(2,1)}, u32[]{:S(2)}, u32[]{:S(2)}) %all-to-all-start) | async-done | bytes 4456480 | tf_op jit(solution)/shard_map/all_to_all | solution.py:380
  88.1 1.3 gather_fusion
  89.4 0.7 broadcast_in_dim.7
  90.1 5.7 %all-to-all-start.1 = ((bf16[128,4,128]{2,1,0:T(4,128)(2,1)}), bf16[128,4,128]{2,1,0:T(4,128)(2,1)S(1)}, u32[]{:S(2)}, u32[]{:S(2)}) async-start(bf16[128,4,128]{2,1,0:T(4,128)(2,1)} %broadcast_in_dim.7), calls=%async_computation.1 | async-start | bytes 262144 | tf_op jit(solution)/shard_map/all_to_all | solution.py:380
  95.8 0.0 copy-done.16
  95.8 0.1 copy.15
  95.9 0.1 reshape.44.columns_ref
  96.0 0.0 copy-done.7
  96.0 0.0 copy-start
  96.0 2.8 %copy-done = bf16[32,6,128,128]{3,2,1,0:T(8,128)(2,1)S(1)} copy-done((bf16[32,6,128,128]{3,2,1,0:T(8,128)(2,1)S(1)}, bf16[32,6,128,128]{3,2,1,0:T(8,128)(2,1)}, u32[]{:S(2)}) %copy-start) | copy-done | bytes 6291480
  98.8 0.0 copy-start.13
  98.8 5.1 %shard_map.113.z_ref = f32[4096,128]{1,0:T(8,128)S(1)} custom-call(s32[192]{0:T(256)S(1)} %reshape.44.columns_ref, bf16[32,128,128]{2,1,0:T(8,128)(2,1)S(1)} %bitcast.14, bf16[128,136,128]{2,1,0:T(8,128)(2,1)} %all-to-all-done.halo_hbm, bf16[32,6,128,128]{3,2,1,0:T(8,128)(2,1)S(1)} %copy-done), custom_call_target="tpu_custom_call" | custom-call | tf_op jit(solution)/shard_map/pallas_call | solution.py:107
  103.9 1.6 all-to-all-done.1
  105.6 0.0 copy-done.13
  105.6 0.0 copy-start.1
  105.6 2.8 %copy-done.1 = bf16[32,6,128,128]{3,2,1,0:T(8,128)(2,1)S(1)} copy-done((bf16[32,6,128,128]{3,2,1,0:T(8,128)(2,1)S(1)}, bf16[32,6,128,128]{3,2,1,0:T(8,128)(2,1)}, u32[]{:S(2)}) %copy-start.1) | copy-done | bytes 6291480
  108.4 0.0 copy-start.5
  108.4 2.2 copy-done.5
  110.6 0.0 copy-start.10
  110.6 1.6 copy-done.10
  112.1 13.2 %shard_map.114 = (bf16[4096,256]{1,0:T(8,128)(2,1)}, bf16[128,136,128]{2,1,0:T(8,128)(2,1)S(1)}, f32[4096,128]{1,0:T(8,128)S(1)}) custom-call(s32[192]{0:T(256)S(1)} %reshape.44.columns_ref, f32[4096,128]{1,0:T(8,128)S(1)} %shard_map.113.z_ref, bf16[512,128]{1,0:T(8,128)(2,1)S(1)} %bitcast.15, bf16[128,256]{1,0:T(8,128)(2,1)S(1)} %copy-done.13, ...), custom_call_target="tpu_custom_call" | custom-call | tf_op jit(solution)/shard_map/pallas_call | solution.py:247
  125.4 0.0 copy-start.8
  125.4 0.0 copy-start.12
  125.4 63.8 %all_to_all.20.back_ref = bf16[128,136,128]{2,1,0:T(8,128)(2,1)S(1)} all-to-all(bf16[128,136,128]{2,1,0:T(8,128)(2,1)S(1)} %get-tuple-element.7), channel_id=1, replica_groups=mesh['rows'=128] {'rows'}, dimensions={0} | all-to-all | bytes 8912896 | tf_op jit(solution)/shard_map/all_to_all | solution.py:380
  189.2 0.0 copy-done.8
  189.2 0.1 convert_reduce_fusion
  189.4 0.0 copy-start.2
  189.4 2.1 copy-done.2
  191.5 0.7 broadcast_in_dim.8
  192.2 5.2 %all-to-all-start.3 = ((bf16[128,8,128]{2,1,0:T(8,128)(2,1)}), bf16[128,8,128]{2,1,0:T(8,128)(2,1)S(1)}, u32[]{:S(2)}, u32[]{:S(2)}) async-start(bf16[128,8,128]{2,1,0:T(8,128)(2,1)} %broadcast_in_dim.8), calls=%async_computation.3 | async-start | bytes 524288 | tf_op jit(solution)/shard_map/all_to_all | solution.py:380
  197.5 0.0 copy-done.12
  197.5 0.0 copy-start.3
  197.5 2.3 %copy-done.3 = bf16[128,136,128]{2,1,0:T(8,128)(2,1)S(1)} copy-done((bf16[128,136,128]{2,1,0:T(8,128)(2,1)S(1)}, bf16[128,136,128]{2,1,0:T(8,128)(2,1)}, u32[]{:S(2)}) %copy-start.3) | copy-done | bytes 4456472
  199.8 0.0 copy-start.9
  199.8 1.6 copy-done.9
  201.3 0.0 copy-start.15
  201.3 21.1 %shard_map.115.total_ref = f32[4096,128]{1,0:T(8,128)S(1)} custom-call(s32[16384]{0:T(1024)S(1)} %bitcast.17, bf16[128,136,128]{2,1,0:T(8,128)(2,1)S(1)} %copy-done.3, f32[4096,128]{1,0:T(8,128)S(1)} %copy-done.9), custom_call_target="tpu_custom_call" | custom-call | tf_op jit(solution)/shard_map/pallas_call | solution.py:321
  222.4 0.0 all-to-all-done.3
  222.5 0.1 copy.18
  222.6 0.8 copy.19
  223.4 0.0 copy-done.15
  223.4 1.8 shard_map.116
  (10 shorter events, 0.1 us)
Async XLA Ops:
  0.6 1.2 copy-start.6
  1.9 0.8 copy-start.11
  2.7 0.7 copy-start.14
  18.5 2.1 copy-start.4
  20.5 11.9 %copy-start.17 = (s32[4]{0:T(128)S(1)}, s32[4]{0:T(128)}, u32[]{:S(2)}) copy-start(s32[4]{0:T(128)} %param.14) | copy-start | bytes 52
  20.5 75.2 %copy-start.16 = (s32[32,6]{0,1:T(8,128)S(1)}, s32[32,6]{0,1:T(8,128)}, u32[]{:S(2)}) copy-start(s32[32,6]{0,1:T(8,128)} %param.12) | copy-start | bytes 2308
  20.6 75.5 %copy-start.7 = (bf16[4096,128]{1,0:T(8,128)(2,1)S(1)}, bf16[4096,128]{1,0:T(8,128)(2,1)}, u32[]{:S(2)}) copy-start(bf16[4096,128]{1,0:T(8,128)(2,1)} %x_ref.1) | copy-start | bytes 3145732
  20.6 67.5 %all-to-all-start = ((bf16[128,136,128]{2,1,0:T(8,128)(2,1)}), bf16[128,136,128]{2,1,0:T(8,128)(2,1)}, u32[]{:S(2)}, u32[]{:S(2)}) async-start(bf16[128,136,128]{2,1,0:T(8,128)(2,1)} %copy-done.4), calls=%async_computation | async-start | bytes 8912896 | tf_op jit(solution)/shard_map/all_to_all | solution.py:380
  90.1 15.5 %all-to-all-start.1 = ((bf16[128,4,128]{2,1,0:T(4,128)(2,1)}), bf16[128,4,128]{2,1,0:T(4,128)(2,1)S(1)}, u32[]{:S(2)}, u32[]{:S(2)}) async-start(bf16[128,4,128]{2,1,0:T(4,128)(2,1)} %broadcast_in_dim.7), calls=%async_computation.1 | async-start | bytes 262144 | tf_op jit(solution)/shard_map/all_to_all | solution.py:380
  96.0 2.8 %copy-start = (bf16[32,6,128,128]{3,2,1,0:T(8,128)(2,1)S(1)}, bf16[32,6,128,128]{3,2,1,0:T(8,128)(2,1)}, u32[]{:S(2)}) copy-start(bf16[32,6,128,128]{3,2,1,0:T(8,128)(2,1)} %tiles_ref.3) | copy-start | bytes 18874372
  98.8 6.8 %copy-start.13 = (bf16[128,256]{1,0:T(8,128)(2,1)S(1)}, bf16[128,256]{1,0:T(8,128)(2,1)}, u32[]{:S(2)}) copy-start(bf16[128,256]{1,0:T(8,128)(2,1)} %w_ref.1) | copy-start | bytes 196612
  105.6 2.8 %copy-start.1 = (bf16[32,6,128,128]{3,2,1,0:T(8,128)(2,1)S(1)}, bf16[32,6,128,128]{3,2,1,0:T(8,128)(2,1)}, u32[]{:S(2)}) copy-start(bf16[32,6,128,128]{3,2,1,0:T(8,128)(2,1)} %tiles_ref.3) | copy-start | bytes 18874372
  108.4 2.2 copy-start.5
  110.6 1.6 copy-start.10
  125.4 63.8 %copy-start.8 = (f32[4096,128]{1,0:T(8,128)}, f32[4096,128]{1,0:T(8,128)S(1)}, u32[]{:S(2)}) copy-start(f32[4096,128]{1,0:T(8,128)S(1)} %get-tuple-element.8.own_ref) | copy-start | bytes 6291460
  125.4 72.1 %copy-start.12 = (s32[1,128,128]{2,1,0:T(8,128)S(1)}, s32[1,128,128]{2,1,0:T(8,128)}, u32[]{:S(2)}) copy-start(s32[1,128,128]{2,1,0:T(8,128)} %param.13) | copy-start | bytes 196612
  189.4 2.1 copy-start.2
  192.2 30.2 %all-to-all-start.3 = ((bf16[128,8,128]{2,1,0:T(8,128)(2,1)}), bf16[128,8,128]{2,1,0:T(8,128)(2,1)S(1)}, u32[]{:S(2)}, u32[]{:S(2)}) async-start(bf16[128,8,128]{2,1,0:T(8,128)(2,1)} %broadcast_in_dim.8), calls=%async_computation.3 | async-start | bytes 524288 | tf_op jit(solution)/shard_map/all_to_all | solution.py:380
  197.5 2.3 %copy-start.3 = (bf16[128,136,128]{2,1,0:T(8,128)(2,1)S(1)}, bf16[128,136,128]{2,1,0:T(8,128)(2,1)}, u32[]{:S(2)}) copy-start(bf16[128,136,128]{2,1,0:T(8,128)(2,1)} %copy-done.2) | copy-start | bytes 13369348
  199.8 1.6 copy-start.9
  201.3 22.1 %copy-start.15 = (s32[4,128]{1,0:T(4,128)S(1)}, s32[4,128]{1,0:T(4,128)}, u32[]{:S(2)}) copy-start(s32[4,128]{1,0:T(4,128)} %param.15) | copy-start | bytes 6148

commit v3 on v2

v3 whole, which is shorter than its diff:
```python
import functools

import jax
import jax.numpy as jnp
from jax import lax
from jax.experimental import pallas as pl
from jax.experimental.pallas import tpu as pltpu
from jax.sharding import PartitionSpec as P

BF = jnp.bfloat16
F32 = jnp.float32
VMEM_LIMIT = 60 * 2**20
PAD = 8
EXTRA = 8
FIRST_OUT = 32
FIRST_BACK = 80
GELU_A = 0.7978845608028654
GELU_B = 0.044715


def live_groups(list_ref, start, first, stop, group):
    count = jnp.int32(0)
    for slot in range(first, stop, group):
        count = count + (list_ref[start + slot] >= 0).astype(jnp.int32)
    return count


def gather_kernel(lists, slots, first, stop, list_ref, hub_ref, x_ref, out_ref, wide, buffer):
    step = pl.program_id(0)
    rows = x_ref.shape[0]
    peers = pl.num_programs(0) * lists
    sections = hub_ref.shape[0] // peers
    count = stop - first
    group = 16

    @pl.when(step == 0)
    def _():
        wide[pl.ds(0, PAD), :] = jnp.zeros((PAD, wide.shape[1]), F32)
        wide[pl.ds(PAD, rows), :] = x_ref[...].astype(F32)
        buffer[pl.ds(count, EXTRA), :] = jnp.zeros((EXTRA, wide.shape[1]), F32)

    def one_list(k, carry):
        peer = step * lists + k
        start = peer * slots
        if first == 0:
            for slot in range(count):
                row = list_ref[start + slot]
                buffer[slot : slot + 1, :] = wide[pl.ds(row + PAD, 1), :]
            for section in range(sections):
                row = hub_ref[section * peers + peer]
                buffer[count + section : count + section + 1, :] = wide[pl.ds(row + PAD, 1), :]
        else:
            buffer[pl.ds(0, count), :] = jnp.zeros((count, wide.shape[1]), F32)

            def body(part, carry):
                base = pl.multiple_of(part * group, group)
                for slot in range(group):
                    row = list_ref[start + first + base + slot]
                    buffer[pl.ds(base + slot, 1), :] = wide[pl.ds(row + PAD, 1), :]
                return carry

            lax.fori_loop(0, live_groups(list_ref, start, first, stop, group), body, 0)
        out_ref[k] = buffer[...].astype(BF)
        return carry

    lax.fori_loop(0, lists, one_list, 0, unroll=2 if first == 0 else 1)


def gather_rows(features, send_lists, hub_rows, first, stop):
    peers, slots = send_lists.shape
    rows, width = features.shape
    lists = 32
    height = stop - first + EXTRA
    return pl.pallas_call(
        functools.partial(gather_kernel, lists, slots, first, stop),
        grid_spec=pltpu.PrefetchScalarGridSpec(
            num_scalar_prefetch=2,
            grid=(peers // lists,),
            in_specs=[pl.BlockSpec((rows, width), lambda i, *_: (0, 0))],
            out_specs=pl.BlockSpec((lists, height, width), lambda i, *_: (i, 0, 0)),
            scratch_shapes=[
                pltpu.VMEM((rows + PAD, width), F32),
                pltpu.VMEM((height, width), F32),
            ],
        ),
        out_shape=jax.ShapeDtypeStruct((peers, height, width), BF),
        compiler_params=pltpu.CompilerParams(vmem_limit_bytes=VMEM_LIMIT),
    )(send_lists.reshape(-1), hub_rows.reshape(-1), features)


def layer_kernel(
    group,
    steps,
    columns_ref,
    x_hbm,
    halo1_hbm,
    halo2_hbm,
    hub_ref,
    w_ref,
    tiles_ref,
    hub_tiles_ref,
    cot_ref,
    out_ref,
    send1_ref,
    send2_ref,
    own_ref,
    features,
    adjoint,
    hub_adjoint,
    grad_w,
    extra,
    sems,
):
    step = pl.program_id(0)
    per_block, blk = tiles_ref.shape[1:3]
    sections = hub_tiles_ref.shape[0]
    width = hub_ref.shape[1]
    own_part = own_ref.shape[0] // blk
    send_part = send1_ref.shape[0]
    own_blocks = x_hbm.shape[0]
    peers = halo1_hbm.shape[0]
    slots1 = halo1_hbm.shape[1] - EXTRA
    back1 = send1_ref.shape[1] - EXTRA

    @pl.when(step == 0)
    def _():
        halo = pl.ds(own_blocks, peers)
        copies = [
            pltpu.make_async_copy(x_hbm, features.at[pl.ds(0, own_blocks)], sems.at[0]),
            pltpu.make_async_copy(
                halo1_hbm.at[:, pl.ds(0, slots1), :],
                features.at[halo, pl.ds(0, slots1), :],
                sems.at[1],
            ),
            pltpu.make_async_copy(
                halo2_hbm.at[:, pl.ds(0, blk - slots1), :],
                features.at[halo, pl.ds(slots1, blk - slots1), :],
                sems.at[2],
            ),
        ]
        for copy in copies:
            copy.start()

        def clear(block, carry):
            adjoint[block] = jnp.zeros((blk, width), F32)
            return carry

        lax.fori_loop(0, adjoint.shape[0], clear, 0, unroll=4)
        hub_adjoint[...] = jnp.zeros_like(hub_adjoint)
        grad_w[...] = jnp.zeros_like(grad_w)
        for copy in copies:
            copy.wait()

    @pl.when(step < steps)
    def _():
        weight = w_ref[...]
        weight_twice = jnp.concatenate([weight, weight], axis=0)
        hub_slab = jnp.concatenate([hub_tiles_ref[s] for s in range(sections)], axis=1)
        places = []
        slabs = []
        tiled = []
        for u in range(group):
            first = (step * group + u) * per_block
            places.append([columns_ref[first + t] for t in range(per_block)])
            slabs.append(jnp.concatenate([tiles_ref[u, t] for t in range(per_block)], axis=1))
            blocks = jnp.concatenate([features[place] for place in places[u]], axis=0)
            tiled.append(jnp.dot(slabs[u], blocks, preferred_element_type=F32))
        z = jnp.concatenate(tiled, axis=0)
        z = z + jnp.dot(hub_slab, hub_ref[...], preferred_element_type=F32)
        z_high = z.astype(BF)
        z_low = (z - z_high.astype(F32)).astype(BF)
        preact = jnp.dot(
            jnp.concatenate([z_high, z_low], axis=1), weight_twice, preferred_element_type=F32
        )
        square = preact * preact
        t = jnp.tanh(preact * (GELU_A + (GELU_A * GELU_B) * square))
        half = 0.5 + 0.5 * t
        out_ref[...] = (preact * half).astype(BF)
        slope = half + (0.5 * preact) * (1.0 - t * t) * (GELU_A + (3.0 * GELU_A * GELU_B) * square)
        grad = (cot_ref[...].astype(F32) * slope).astype(BF)
        grad_w[...] += lax.dot_general(
            z_high, grad, (((0,), (0,)), ((), ())), preferred_element_type=F32
        )
        back = lax.dot_general(
            grad, weight, (((1,), (1,)), ((), ())), preferred_element_type=F32
        ).astype(BF)
        hub_adjoint[...] += lax.dot_general(
            hub_slab, back, (((0,), (0,)), ((), ())), preferred_element_type=F32
        )
        for u in range(group):
            spread = lax.dot_general(
                slabs[u],
                back[u * blk : (u + 1) * blk],
                (((0,), (0,)), ((), ())),
                preferred_element_type=F32,
            )
            for t in range(per_block):
                adjoint[places[u][t]] += spread[t * blk : (t + 1) * blk]

    @pl.when(step == steps)
    def _():
        for s in range(sections):
            extra[:, s, :] = hub_adjoint[s * blk : (s + 1) * blk, :]
        total = grad_w[...]
        high = total.astype(BF).astype(F32)
        low = total - high
        pieces = total.shape[1] // width
        for piece in range(pieces):
            part = slice(piece * width, (piece + 1) * width)
            extra[:, sections + piece, :] = high[:, part]
            extra[:, sections + pieces + piece, :] = low[:, part]

    @pl.when(step >= steps)
    def _():
        final = step - steps
        for block in range(own_part):
            own_ref[pl.ds(block * blk, blk), :] = adjoint[final * own_part + block]

        def finish(k, carry):
            peer = final * send_part + k
            rows = adjoint[own_blocks + peer]
            tail = extra[peer]
            send1_ref[k] = jnp.concatenate([rows[:back1], tail], axis=0).astype(BF)
            send2_ref[k] = jnp.concatenate([rows[back1:], tail], axis=0).astype(BF)
            return carry

        lax.fori_loop(0, send_part, finish, 0, unroll=4)


def layer(features, halo1, halo2, hub, weight, tiles, tile_columns, hub_tiles, cotangent):
    blocks, per_block, blk, _ = tiles.shape
    width, width_out = weight.shape
    sections = hub_tiles.shape[0]
    peers = halo1.shape[0]
    rows = blocks * blk
    group = 8
    steps = blocks // group
    finals = 4
    height1 = FIRST_BACK + EXTRA
    height2 = blk - FIRST_BACK + EXTRA

    def work(i):
        return jnp.minimum(i, steps - 1)

    def final(i):
        return jnp.maximum(i - steps, 0)

    return pl.pallas_call(
        functools.partial(layer_kernel, group, steps),
        grid_spec=pltpu.PrefetchScalarGridSpec(
            num_scalar_prefetch=1,
            grid=(steps + finals,),
            in_specs=[
                pl.BlockSpec(memory_space=pl.ANY),
                pl.BlockSpec(memory_space=pl.ANY),
                pl.BlockSpec(memory_space=pl.ANY),
                pl.BlockSpec((sections * blk, width), lambda i, *_: (0, 0)),
                pl.BlockSpec((width, width_out), lambda i, *_: (0, 0)),
                pl.BlockSpec((group, per_block, blk, blk), lambda i, *_: (work(i), 0, 0, 0)),
                pl.BlockSpec((sections, group * blk, blk), lambda i, *_: (0, work(i), 0)),
                pl.BlockSpec((group * blk, width_out), lambda i, *_: (work(i), 0)),
            ],
            out_specs=[
                pl.BlockSpec((group * blk, width_out), lambda i, *_: (work(i), 0)),
                pl.BlockSpec((peers // finals, height1, width), lambda i, *_: (final(i), 0, 0)),
                pl.BlockSpec((peers // finals, height2, width), lambda i, *_: (final(i), 0, 0)),
                pl.BlockSpec((rows // finals, width), lambda i, *_: (final(i), 0)),
            ],
            scratch_shapes=[
                pltpu.VMEM((blocks + peers, blk, width), BF),
                pltpu.VMEM((blocks + peers, blk, width), F32),
                pltpu.VMEM((sections * blk, width), F32),
                pltpu.VMEM((width, width_out), F32),
                pltpu.VMEM((peers, EXTRA, width), F32),
                pltpu.SemaphoreType.DMA((3,)),
            ],
        ),
        out_shape=[
            jax.ShapeDtypeStruct((rows, width_out), BF),
            jax.ShapeDtypeStruct((peers, height1, width), BF),
            jax.ShapeDtypeStruct((peers, height2, width), BF),
            jax.ShapeDtypeStruct((rows, width), F32),
        ],
        compiler_params=pltpu.CompilerParams(vmem_limit_bytes=VMEM_LIMIT),
    )(
        tile_columns.reshape(-1),
        features.reshape(blocks, blk, width),
        halo1,
        halo2,
        hub,
        weight,
        tiles,
        hub_tiles,
        cotangent,
    )


def scatter_kernel(
    lists, slots, first, stop, last, list_ref, hub_ref, back_ref, start_ref, out_ref, t0, t1, t2, t3, buffer
):
    step = pl.program_id(0)
    steps = pl.num_programs(0)
    totals = (t0, t1, t2, t3)
    rows, width = start_ref.shape
    peers = steps * lists
    sections = hub_ref.shape[0] // peers
    live = pl.ds(PAD, rows)
    group = 16

    @pl.when(step == 0)
    def _():
        t0[live, :] = start_ref[...]
        for total in totals[1:]:
            total[...] = jnp.zeros_like(total)

    def one_list(k, carry):
        peer = step * lists + k
        start = peer * slots
        buffer[...] = back_ref[k].astype(F32)

        def add(places, base):
            sums = [
                totals[v][pl.ds(place + PAD, 1), :] + buffer[pl.ds(base + v, 1), :]
                for v, place in enumerate(places)
            ]
            for v, place in enumerate(places):
                totals[v][pl.ds(place + PAD, 1), :] = sums[v]

        if last:
            for s in range(0, sections, 4):
                count = min(4, sections - s)
                add([hub_ref[(s + v) * peers + peer] for v in range(count)], stop - first + s)

        def body(part, carry):
            base = pl.multiple_of(part * group, group)
            for slot in range(0, group, 4):
                add([list_ref[start + first + base + slot + v] for v in range(4)], base + slot)
            return carry

        lax.fori_loop(0, live_groups(list_ref, start, first, stop, group), body, 0)
        return carry

    lax.fori_loop(0, lists, one_list, 0)

    @pl.when(step == steps - 1)
    def _():
        total = (t0[live, :] + t1[live, :]) + (t2[live, :] + t3[live, :])
        out_ref[...] = total.astype(out_ref.dtype)


def scatter_rows(send_lists, hub_places, returned, start, first, stop, last):
    peers, slots = send_lists.shape
    rows, width = start.shape
    lists = 32
    height = returned.shape[1]
    dtype = BF if last else F32
    return pl.pallas_call(
        functools.partial(scatter_kernel, lists, slots, first, stop, last),
        grid_spec=pltpu.PrefetchScalarGridSpec(
            num_scalar_prefetch=2,
            grid=(peers // lists,),
            in_specs=[
                pl.BlockSpec((lists, height, width), lambda i, *_: (i, 0, 0)),
                pl.BlockSpec((rows, width), lambda i, *_: (0, 0)),
            ],
            out_specs=pl.BlockSpec((rows, width), lambda i, *_: (0, 0)),
            scratch_shapes=[pltpu.VMEM((rows + PAD, width), F32)] * 4
            + [pltpu.VMEM((height, width), F32)],
        ),
        out_shape=jax.ShapeDtypeStruct((rows, width), dtype),
        compiler_params=pltpu.CompilerParams(vmem_limit_bytes=VMEM_LIMIT),
    )(send_lists.reshape(-1), hub_places.reshape(-1), returned, start)


def exchange(array):
    return lax.all_to_all(array, "rows", split_axis=0, concat_axis=0, tiled=True)


def body(
    features,
    weight,
    adjacency_tiles,
    tile_columns,
    send_rows,
    hub_owner,
    hub_rows,
    hub_tiles,
    cotangent,
):
    device = lax.axis_index("rows")
    sections, peers = hub_rows.shape
    width, width_out = weight.shape
    pieces = width_out // width
    send_lists = send_rows[0]
    slots = send_lists.shape[1]

    halo1 = exchange(gather_rows(features, send_lists, hub_rows, 0, FIRST_OUT))
    part = gather_rows(features, send_lists, hub_rows, FIRST_OUT, slots)
    hub_mine = halo1[hub_owner, FIRST_OUT + jnp.arange(sections)]
    end = slots - FIRST_OUT
    part = part.at[:, end : end + sections].set(
        jnp.broadcast_to(hub_mine[None], (peers, sections, width))
    )
    halo2 = exchange(part)
    hub = halo2[:, end : end + sections].transpose(1, 0, 2).reshape(sections * peers, width)

    output, send1, send2, own = layer(
        features, halo1, halo2, hub, weight, adjacency_tiles, tile_columns, hub_tiles, cotangent
    )

    back1 = exchange(send1)
    sums = jnp.sum(back1[:, FIRST_BACK:].astype(F32), axis=0)
    weight_row = sums[sections : sections + pieces] + sums[sections + pieces :]
    high = weight_row.astype(BF)
    low = (weight_row - high.astype(F32)).astype(BF)
    mine = jnp.concatenate([sums[:sections].astype(BF), high, low], axis=0)
    end = slots - FIRST_BACK
    send2 = send2.at[:, end:].set(jnp.broadcast_to(mine[None], (peers,) + mine.shape))
    back2 = exchange(send2)

    hub_places = jnp.where((hub_owner == device)[:, None], hub_rows, -1)
    total = scatter_rows(send_lists, hub_places, back1, own, 0, FIRST_BACK, False)
    grad_features = scatter_rows(send_lists, hub_places, back2, total, FIRST_BACK, slots, True)
    tail = back2[:, end + sections :].astype(F32)
    grad_weight = (tail[:, :pieces] + tail[:, pieces:]).reshape(width, width_out)
    return (output, grad_features, grad_weight)


def solution(mesh):
    return jax.shard_map(
        body,
        mesh=mesh,
        in_specs=(
            P("rows", None),
            P(),
            P("rows", None, None, None),
            P("rows", None),
            P("rows", None, None),
            P(),
            P(),
            P(None, "rows", None),
            P("rows", None),
        ),
        out_specs=(P("rows", None), P("rows", None), P()),
        check_vma=False,
    )
```

time: 226 us -> 209 us (0.925)
  Pallas kernels: 56.3 us -> 77.7 us
  blocking collectives: 63.8 us -> 43.8 us
  local copies, waits for them, and re-layouts: 23.9 us -> 6.06 us
    all_to_all x1, blocking collectives: 63.8 us -> 43.8 us  [exchange(): lax.all_to_all(array, 'rows', split_axis=0, concat_axis=0, tiled=True)]
    unnamed x38 -> x14, local copies, waits for them, and re-layouts: 20.9 us -> 2.3 us
    pallas_call x4, Pallas kernels: 43.1 us -> 57.4 us  [the longest x2 32.7 us: scatter_rows(): pl.pallas_call(functools.partial(scatter_kernel, lists, slots, first, sto...]
    pallas_call x1, Pallas kernels: 13.2 us -> 20.3 us  [layer(): pl.pallas_call(functools.partial(layer_kernel, group, steps), grid_spec=p...]
  transfers between devices with their start and end apart: 3 -> 3, of which waited for: 2 -> 3; matrix products, arithmetic and copies ran while one was open for 0% -> 1% of each run, Pallas kernels for 12% -> 18%
where the time goes in v3:
time: 209 us; the launch traced here: 208 us
  Pallas kernels  77.7 us (37%)
  waiting for transfers between devices  55.6 us (27%)
  blocking collectives  43.8 us (21%)
  starting transfers between devices  21.8 us (10%)
  local copies, waits for them, and re-layouts  6.06 us (3%)
    all_to_all x3, waiting for transfers between devices, exchange(): lax.all_to_all(array, 'rows', split_axis=0, concat_axis=0, tiled=True)  55.6 us
    all_to_all x1, blocking collectives, exchange(): lax.all_to_all(array, 'rows', split_axis=0, concat_axis=0, tiled=True)  43.8 us
    pallas_call x2, Pallas kernels, scatter_rows(): pl.pallas_call(functools.partial(scatter_kernel, lists, slots, first, sto...  32.7 us
    pallas_call x2, Pallas kernels, gather_rows(): pl.pallas_call(functools.partial(gather_kernel, lists, slots, first, stop...  24.6 us
    all_to_all x3, starting transfers between devices, exchange(): lax.all_to_all(array, 'rows', split_axis=0, concat_axis=0, tiled=True)  21.8 us
    pallas_call x1, Pallas kernels, layer(): pl.pallas_call(functools.partial(layer_kernel, group, steps), grid_spec=p...  20.3 us
  transfers between devices with their start and end apart: 3, of which 3 were waited for; matrix products, arithmetic and copies ran while one was open for 1% of the time, Pallas kernels for 18%

profile of v3, /device:TPU:1, one launch (start us, length us, event | category | flops | bytes accessed | tf_op | source)
XLA Modules:
  0.0 207.6 jit_solution(3910498823810830023)
XLA Ops:
  0.6 8.7 %shard_map.112 = bf16[128,40,128]{2,1,0:T(8,128)(2,1)} custom-call(s32[16384]{0:T(1024)} %bitcast.19, s32[512]{0:T(512)} %bitcast.26, bf16[4096,128]{1,0:T(8,128)(2,1)} %x_ref.3), custom_call_target="tpu_custom_call" | custom-call | tf_op jit(solution)/shard_map/pallas_call | solution.py:74
  9.3 11.5 %all-to-all-start = ((bf16[128,40,128]{2,1,0:T(8,128)(2,1)}), bf16[128,40,128]{2,1,0:T(8,128)(2,1)S(1)}, u32[]{:S(2)}, u32[]{:S(2)}) async-start(bf16[128,40,128]{2,1,0:T(8,128)(2,1)} %shard_map.112), calls=%async_computation | async-start | bytes 2621440 | tf_op jit(solution)/shard_map/all_to_all | solution.py:376
  20.8 0.0 copy-start.5
  20.9 15.9 %shard_map.113 = bf16[128,104,128]{2,1,0:T(8,128)(2,1)} custom-call(s32[16384]{0:T(1024)} %bitcast.20, s32[512]{0:T(512)} %bitcast.27, bf16[4096,128]{1,0:T(8,128)(2,1)} %x_ref.3), custom_call_target="tpu_custom_call" | custom-call | tf_op jit(solution)/shard_map/pallas_call | solution.py:74
  36.8 0.0 copy-done.5
  36.8 6.1 %all-to-all-done.halo1_hbm = bf16[128,40,128]{2,1,0:T(8,128)(2,1)S(1)} async-done(((bf16[128,40,128]{2,1,0:T(8,128)(2,1)}), bf16[128,40,128]{2,1,0:T(8,128)(2,1)S(1)}, u32[]{:S(2)}, u32[]{:S(2)}) %all-to-all-start) | async-done | bytes 1310752 | tf_op jit(solution)/shard_map/all_to_all | solution.py:376
  42.9 0.0 copy-start.2
  42.9 0.6 gather_fusion
  43.5 0.7 broadcast_dynamic-update-slice_fusion.1
  44.2 0.0 copy-start.4
  44.2 0.0 copy-done.2
  44.2 4.8 %all-to-all-start.1 = ((bf16[128,104,128]{2,1,0:T(8,128)(2,1)}), bf16[128,104,128]{2,1,0:T(8,128)(2,1)S(1)}, u32[]{:S(2)}, u32[]{:S(2)}) async-start(bf16[128,104,128]{2,1,0:T(8,128)(2,1)} %broadcast_dynamic-update-slice_fusion.1), calls=%async_computation.1 | async-start | bytes 6815744 | tf_op jit(solution)/shard_map/all_to_all | solution.py:376
  49.0 0.0 copy-done.4
  49.0 0.1 copy.13
  49.1 0.7 reshape.103.columns_ref
  49.8 44.1 %all-to-all-done.1.halo2_hbm = bf16[128,104,128]{2,1,0:T(8,128)(2,1)S(1)} async-done(((bf16[128,104,128]{2,1,0:T(8,128)(2,1)}), bf16[128,104,128]{2,1,0:T(8,128)(2,1)S(1)}, u32[]{:S(2)}, u32[]{:S(2)}) %all-to-all-start.1) | async-done | bytes 3407904 | tf_op jit(solution)/shard_map/all_to_all | solution.py:376
  93.8 0.0 copy-start
  93.9 0.8 copy.14
  94.7 1.0 copy-done
  95.6 20.3 %shard_map.114 = (bf16[4096,256]{1,0:T(8,128)(2,1)}, bf16[128,88,128]{2,1,0:T(8,128)(2,1)}, bf16[128,56,128]{2,1,0:T(8,128)(2,1)}, f32[4096,128]{1,0:T(8,128)}) custom-call(s32[192]{0:T(256)} %reshape.103.columns_ref, bf16[32,128,128]{2,1,0:T(8,128)(2,1)} %bitcast.18, bf16[128,40,128]{2,1,0:T(8,128)(2,1)} %copy-done.2, bf16[128,104,128]{2,1,0:T(8,128)(2,1)} %copy-done, ...), custom_call_target="tpu_custom_call" | custom-call | tf_op jit(solution)/shard_map/pallas_call | solution.py:248
  116.0 43.8 %all_to_all.20.back_ref = bf16[128,88,128]{2,1,0:T(8,128)(2,1)S(1)} all-to-all(bf16[128,88,128]{2,1,0:T(8,128)(2,1)} %get-tuple-element.33), channel_id=1, replica_groups=mesh['rows'=128] {'rows'}, dimensions={0} | all-to-all | bytes 5767168 | tf_op jit(solution)/shard_map/all_to_all | solution.py:376
  159.8 0.0 copy-start.1
  159.8 0.0 copy-start.3
  159.8 0.1 convert_reduce_fusion
  160.0 1.0 broadcast_dynamic-update-slice_fusion
  161.0 0.5 copy-done.1
  161.5 5.6 %all-to-all-start.3 = ((bf16[128,56,128]{2,1,0:T(8,128)(2,1)}), bf16[128,56,128]{2,1,0:T(8,128)(2,1)}, u32[]{:S(2)}, u32[]{:S(2)}) async-start(bf16[128,56,128]{2,1,0:T(8,128)(2,1)} %broadcast_dynamic-update-slice_fusion), calls=%async_computation.3 | async-start | bytes 3670016 | tf_op jit(solution)/shard_map/all_to_all | solution.py:376
  167.1 0.0 copy-done.3
  167.1 0.6 select_bitcast_fusion.hub_ref
  167.7 21.5 %shard_map.115.start_ref = f32[4096,128]{1,0:T(8,128)} custom-call(s32[16384]{0:T(1024)} %bitcast.21, s32[512]{0:T(512)} %select_bitcast_fusion.hub_ref, bf16[128,88,128]{2,1,0:T(8,128)(2,1)} %copy-done.1, f32[4096,128]{1,0:T(8,128)} %get-tuple-element.34.start_ref), custom_call_target="tpu_custom_call" | custom-call | tf_op jit(solution)/shard_map/pallas_call | solution.py:357
  189.2 5.4 %all-to-all-done.3.back_ref = bf16[128,56,128]{2,1,0:T(8,128)(2,1)} async-done(((bf16[128,56,128]{2,1,0:T(8,128)(2,1)}), bf16[128,56,128]{2,1,0:T(8,128)(2,1)}, u32[]{:S(2)}, u32[]{:S(2)}) %all-to-all-start.3) | async-done | bytes 1835040 | tf_op jit(solution)/shard_map/all_to_all | solution.py:376
  194.6 1.0 slice_convert_fusion
  195.6 0.1 slice_add_fusion
  195.7 0.7 copy.17
  196.4 11.2 %shard_map.116 = bf16[4096,128]{1,0:T(8,128)(2,1)} custom-call(s32[16384]{0:T(1024)} %bitcast.22, s32[512]{0:T(512)} %select_bitcast_fusion.hub_ref, bf16[128,56,128]{2,1,0:T(8,128)(2,1)} %all-to-all-done.3.back_ref, f32[4096,128]{1,0:T(8,128)} %shard_map.115.start_ref), custom_call_target="tpu_custom_call" | custom-call | tf_op jit(solution)/shard_map/pallas_call | solution.py:357
  (7 shorter events, 0.1 us)
Async XLA Ops:
  9.3 33.6 %all-to-all-start = ((bf16[128,40,128]{2,1,0:T(8,128)(2,1)}), bf16[128,40,128]{2,1,0:T(8,128)(2,1)S(1)}, u32[]{:S(2)}, u32[]{:S(2)}) async-start(bf16[128,40,128]{2,1,0:T(8,128)(2,1)} %shard_map.112), calls=%async_computation | async-start | bytes 2621440 | tf_op jit(solution)/shard_map/all_to_all | solution.py:376
  20.8 16.0 %copy-start.5 = (s32[4]{0:T(128)S(1)}, s32[4]{0:T(128)}, u32[]{:S(2)}) copy-start(s32[4]{0:T(128)} %param.18) | copy-start | bytes 52
  42.9 1.3 copy-start.2
  44.2 4.8 %copy-start.4 = (s32[32,6]{0,1:T(8,128)S(1)}, s32[32,6]{0,1:T(8,128)}, u32[]{:S(2)}) copy-start(s32[32,6]{0,1:T(8,128)} %param.16) | copy-start | bytes 2308
  44.2 49.6 %all-to-all-start.1 = ((bf16[128,104,128]{2,1,0:T(8,128)(2,1)}), bf16[128,104,128]{2,1,0:T(8,128)(2,1)S(1)}, u32[]{:S(2)}, u32[]{:S(2)}) async-start(bf16[128,104,128]{2,1,0:T(8,128)(2,1)} %broadcast_dynamic-update-slice_fusion.1), calls=%async_computation.1 | async-start | bytes 6815744 | tf_op jit(solution)/shard_map/all_to_all | solution.py:376
  93.8 1.8 copy-start
  159.8 1.7 copy-start.1
  159.8 7.3 %copy-start.3 = (s32[4,128]{1,0:T(4,128)S(1)}, s32[4,128]{1,0:T(4,128)}, u32[]{:S(2)}) copy-start(s32[4,128]{1,0:T(4,128)} %param.19) | copy-start | bytes 6148
  161.5 33.1 %all-to-all-start.3 = ((bf16[128,56,128]{2,1,0:T(8,128)(2,1)}), bf16[128,56,128]{2,1,0:T(8,128)(2,1)}, u32[]{:S(2)}, u32[]{:S(2)}) async-start(bf16[128,56,128]{2,1,0:T(8,128)(2,1)} %broadcast_dynamic-update-slice_fusion), calls=%async_computation.3 | async-start | bytes 3670016 | tf_op jit(solution)/shard_map/all_to_all | solution.py:376

commit v4 on v3

--- a/solution.py
+++ b/solution.py
@@ -18,11 +18,13 @@
 GELU_B = 0.044715
 
 
-def live_groups(list_ref, start, first, stop, group):
-    count = jnp.int32(0)
-    for slot in range(first, stop, group):
-        count = count + (list_ref[start + slot] >= 0).astype(jnp.int32)
-    return count
+def each_live_group(list_ref, start, base, stop, group, work):
+    if base < stop:
+
+        @pl.when(list_ref[start + base] >= 0)
+        def _():
+            work(base)
+            each_live_group(list_ref, start, base + group, stop, group, work)
 
 
 def gather_kernel(lists, slots, first, stop, list_ref, hub_ref, x_ref, out_ref, wide, buffer):
@@ -52,14 +54,12 @@
         else:
             buffer[pl.ds(0, count), :] = jnp.zeros((count, wide.shape[1]), F32)
 
-            def body(part, carry):
-                base = pl.multiple_of(part * group, group)
-                for slot in range(group):
-                    row = list_ref[start + first + base + slot]
-                    buffer[pl.ds(base + slot, 1), :] = wide[pl.ds(row + PAD, 1), :]
-                return carry
-
-            lax.fori_loop(0, live_groups(list_ref, start, first, stop, group), body, 0)
+            def work(base):
+                for slot in range(base, base + group):
+                    row = list_ref[start + slot]
+                    buffer[slot - first : slot - first + 1, :] = wide[pl.ds(row + PAD, 1), :]
+
+            each_live_group(list_ref, start, first, stop, group, work)
         out_ref[k] = buffer[...].astype(BF)
         return carry
 
@@ -184,9 +184,10 @@
         back = lax.dot_general(
             grad, weight, (((1,), (1,)), ((), ())), preferred_element_type=F32
         ).astype(BF)
-        hub_adjoint[...] += lax.dot_general(
-            hub_slab, back, (((0,), (0,)), ((), ())), preferred_element_type=F32
-        )
+        back_turned = lax.dot_general(
+            weight, grad, (((1,), (1,)), ((), ())), preferred_element_type=F32
+        ).astype(BF)
+        hub_adjoint[...] += jnp.dot(back_turned, hub_slab, preferred_element_type=F32)
         for u in range(group):
             spread = lax.dot_general(
                 slabs[u],
@@ -200,7 +201,7 @@
     @pl.when(step == steps)
     def _():
         for s in range(sections):
-            extra[:, s, :] = hub_adjoint[s * blk : (s + 1) * blk, :]
+            extra[:, s, :] = hub_adjoint[:, s * blk : (s + 1) * blk].T
         total = grad_w[...]
         high = total.astype(BF).astype(F32)
         low = total - high
@@ -269,7 +270,7 @@
             scratch_shapes=[
                 pltpu.VMEM((blocks + peers, blk, width), BF),
                 pltpu.VMEM((blocks + peers, blk, width), F32),
-                pltpu.VMEM((sections * blk, width), F32),
+                pltpu.VMEM((width, sections * blk), F32),
                 pltpu.VMEM((width, width_out), F32),
                 pltpu.VMEM((peers, EXTRA, width), F32),
                 pltpu.SemaphoreType.DMA((3,)),
@@ -295,69 +296,66 @@
     )
 
 
-def scatter_kernel(
-    lists, slots, first, stop, last, list_ref, hub_ref, back_ref, start_ref, out_ref, t0, t1, t2, t3, buffer
-):
+def add_rows(totals, places, buffer, base):
+    sums = [
+        totals[v][pl.ds(place + PAD, 1), :] + buffer[pl.ds(base + v, 1), :]
+        for v, place in enumerate(places)
+    ]
+    for v, place in enumerate(places):
+        totals[v][pl.ds(place + PAD, 1), :] = sums[v]
+
+
+def begin_totals(totals, start_ref):
+    totals[0][pl.ds(PAD, start_ref.shape[0]), :] = start_ref[...]
+    for total in totals[1:]:
+        total[...] = jnp.zeros_like(total)
+
+
+def sum_totals(totals, rows):
+    live = pl.ds(PAD, rows)
+    t0, t1, t2, t3 = totals
+    return (t0[live, :] + t1[live, :]) + (t2[live, :] + t3[live, :])
+
+
+def scatter_kernel(lists, slots, stop, list_ref, back_ref, start_ref, out_ref, t0, t1, t2, t3, buffer):
     step = pl.program_id(0)
-    steps = pl.num_programs(0)
     totals = (t0, t1, t2, t3)
-    rows, width = start_ref.shape
-    peers = steps * lists
-    sections = hub_ref.shape[0] // peers
-    live = pl.ds(PAD, rows)
     group = 16
 
     @pl.when(step == 0)
     def _():
-        t0[live, :] = start_ref[...]
-        for total in totals[1:]:
-            total[...] = jnp.zeros_like(total)
+        begin_totals(totals, start_ref)
 
     def one_list(k, carry):
-        peer = step * lists + k
-        start = peer * slots
+        start = (step * lists + k) * slots
         buffer[...] = back_ref[k].astype(F32)
 
-        def add(places, base):
-            sums = [
-                totals[v][pl.ds(place + PAD, 1), :] + buffer[pl.ds(base + v, 1), :]
-                for v, place in enumerate(places)
-            ]
-            for v, place in enumerate(places):
-                totals[v][pl.ds(place + PAD, 1), :] = sums[v]
-
-        if last:
-            for s in range(0, sections, 4):
-                count = min(4, sections - s)
-                add([hub_ref[(s + v) * peers + peer] for v in range(count)], stop - first + s)
-
-        def body(part, carry):
-            base = pl.multiple_of(part * group, group)
-            for slot in range(0, group, 4):
-                add([list_ref[start + first + base + slot + v] for v in range(4)], base + slot)
-            return carry
-
-        lax.fori_loop(0, live_groups(list_ref, start, first, stop, group), body, 0)
+        def work(base):
+            for slot in range(base, base + group, 4):
+                places = [list_ref[start + slot + v] for v in range(4)]
+                add_rows(totals, places, buffer, slot)
+
+        for base in range(0, 32, group):
+            work(base)
+        each_live_group(list_ref, start, 32, stop, group, work)
         return carry
 
     lax.fori_loop(0, lists, one_list, 0)
 
-    @pl.when(step == steps - 1)
-    def _():
-        total = (t0[live, :] + t1[live, :]) + (t2[live, :] + t3[live, :])
-        out_ref[...] = total.astype(out_ref.dtype)
-
-
-def scatter_rows(send_lists, hub_places, returned, start, first, stop, last):
+    @pl.when(step == pl.num_programs(0) - 1)
+    def _():
+        out_ref[...] = sum_totals(totals, start_ref.shape[0])
+
+
+def scatter_first(send_lists, returned, start):
     peers, slots = send_lists.shape
     rows, width = start.shape
     lists = 32
     height = returned.shape[1]
-    dtype = BF if last else F32
     return pl.pallas_call(
-        functools.partial(scatter_kernel, lists, slots, first, stop, last),
+        functools.partial(scatter_kernel, lists, slots, height - EXTRA),
         grid_spec=pltpu.PrefetchScalarGridSpec(
-            num_scalar_prefetch=2,
+            num_scalar_prefetch=1,
             grid=(peers // lists,),
             in_specs=[
                 pl.BlockSpec((lists, height, width), lambda i, *_: (i, 0, 0)),
@@ -367,9 +365,110 @@
             scratch_shapes=[pltpu.VMEM((rows + PAD, width), F32)] * 4
             + [pltpu.VMEM((height, width), F32)],
         ),
-        out_shape=jax.ShapeDtypeStruct((rows, width), dtype),
+        out_shape=jax.ShapeDtypeStruct((rows, width), F32),
         compiler_params=pltpu.CompilerParams(vmem_limit_bytes=VMEM_LIMIT),
-    )(send_lists.reshape(-1), hub_places.reshape(-1), returned, start)
+    )(send_lists.reshape(-1), returned, start)
+
+
+def last_kernel(
+    sections,
+    list_ref,
+    hub_ref,
+    owned_ref,
+    back_ref,
+    start_ref,
+    out_ref,
+    grad_w_ref,
+    t0,
+    t1,
+    t2,
+    t3,
+    buffer,
+    grad_w,
+):
+    totals = (t0, t1, t2, t3)
+    peers, height, width = back_ref.shape
+    count = height - EXTRA
+    group = 16
+    pieces = grad_w_ref.shape[1] // width
+    begin_totals(totals, start_ref)
+
+    def widen(part, carry):
+        for k in range(8):
+            peer = part * 8 + k
+            buffer[peer] = back_ref[peer].astype(F32)
+            for piece in range(pieces):
+                high = count + sections + piece
+                low = high + pieces
+                grad_w[piece, pl.ds(peer, 1), :] = (
+                    buffer[peer, high : high + 1, :] + buffer[peer, low : low + 1, :]
+                )
+        return carry
+
+    lax.fori_loop(0, peers // 8, widen, 0)
+
+    def one_list(peer, carry):
+        rows = buffer.at[peer]
+
+        def work(base):
+            for slot in range(base, base + group, 4):
+                places = [list_ref[peer * count + slot + v] for v in range(4)]
+                add_rows(totals, places, rows, slot)
+
+        each_live_group(list_ref, peer * count, 0, count, group, work)
+        return carry
+
+    lax.fori_loop(0, peers, one_list, 0, unroll=2)
+
+    for section in range(sections):
+
+        @pl.when(owned_ref[section] != 0)
+        def _():
+            def some_rows(part, carry):
+                for k in range(0, group, 4):
+                    for v in range(4):
+                        peer = part * group + k + v
+                        place = hub_ref[section * peers + peer] + PAD
+                        row = buffer[peer, count + section : count + section + 1, :]
+                        totals[v][pl.ds(place, 1), :] += row
+                return carry
+
+            lax.fori_loop(0, peers // group, some_rows, 0)
+
+    for piece in range(pieces):
+        grad_w_ref[:, piece * width : (piece + 1) * width] = grad_w[piece]
+    out_ref[...] = sum_totals(totals, start_ref.shape[0]).astype(BF)
+
+
+def scatter_last(send_lists, hub_rows, owned, returned, start, width_out):
+    peers = send_lists.shape[0]
+    rows, width = start.shape
+    height = returned.shape[1]
+    return pl.pallas_call(
+        functools.partial(last_kernel, hub_rows.shape[0]),
+        grid_spec=pltpu.PrefetchScalarGridSpec(
+            num_scalar_prefetch=3,
+            grid=(1,),
+            in_specs=[
+                pl.BlockSpec((peers, height, width), lambda i, *_: (0, 0, 0)),
+                pl.BlockSpec((rows, width), lambda i, *_: (0, 0)),
+            ],
+            out_specs=[
+                pl.BlockSpec((rows, width), lambda i, *_: (0, 0)),
+                pl.BlockSpec((width, width_out), lambda i, *_: (0, 0)),
+            ],
+            scratch_shapes=[pltpu.VMEM((rows + PAD, width), F32)] * 4
+            + [
+                pltpu.VMEM((peers, height, width), F32),
+                pltpu.VMEM((width_out // width, peers, width), F32),
+            ],
+        ),
+        out_shape=[
+            jax.ShapeDtypeStruct((rows, width), BF),
+            jax.ShapeDtypeStruct((width, width_out), F32),
+        ],
+        compiler_params=pltpu.CompilerParams(vmem_limit_bytes=VMEM_LIMIT),
+    )(send_lists.reshape(-1), hub_rows.reshape(-1), owned, returned, start)
 
 
 def exchange(array):
@@ -418,11 +517,11 @@
     send2 = send2.at[:, end:].set(jnp.broadcast_to(mine[None], (peers,) + mine.shape))
     back2 = exchange(send2)
 
-    hub_places = jnp.where((hub_owner == device)[:, None], hub_rows, -1)
-    total = scatter_rows(send_lists, hub_places, back1, own, 0, FIRST_BACK, False)
-    grad_features = scatter_rows(send_lists, hub_places, back2, total, FIRST_BACK, slots, True)
-    tail = back2[:, end + sections :].astype(F32)
-    grad_weight = (tail[:, :pieces] + tail[:, pieces:]).reshape(width, width_out)
+    owned = (hub_owner == device).astype(jnp.int32)
+    total = scatter_first(send_lists, back1, own)
+    grad_features, grad_weight = scatter_last(
+        send_lists[:, FIRST_BACK:], hub_rows, owned, back2, total, width_out
+    )
     return (output, grad_features, grad_weight)
 
 

time: 209 us -> 205 us (0.981)
  Pallas kernels: 77.7 us -> 71.5 us
  waiting for transfers between devices: 55.6 us -> 59.6 us
    all_to_all x3, waiting for transfers between devices: 55.6 us -> 59.6 us  [exchange(): lax.all_to_all(array, 'rows', split_axis=0, concat_axis=0, tiled=True)]
    pallas_call x2, Pallas kernels: 32.7 us -> 29 us  [the longest x1 19.2 us: scatter_first(): pl.pallas_call(functools.partial(scatter_kernel, lists, slots, height - E...]
    pallas_call x2, Pallas kernels: 24.6 us -> 22.2 us  [gather_rows(): pl.pallas_call(functools.partial(gather_kernel, lists, slots, first, stop...]
  transfers between devices with their start and end apart: 3 -> 3, of which waited for: 3 -> 3; matrix products, arithmetic and copies ran while one was open for 1% -> 1% of each run, Pallas kernels for 18% -> 16%
where the time goes in v4:
time: 205 us; the launch traced here: 204 us
  Pallas kernels  71.5 us (35%)
  waiting for transfers between devices  59.6 us (29%)
  blocking collectives  43.8 us (21%)
  starting transfers between devices  21.8 us (11%)
  local copies, waits for them, and re-layouts  6.21 us (3%)
    all_to_all x3, waiting for transfers between devices, exchange(): lax.all_to_all(array, 'rows', split_axis=0, concat_axis=0, tiled=True)  59.6 us
    all_to_all x1, blocking collectives, exchange(): lax.all_to_all(array, 'rows', split_axis=0, concat_axis=0, tiled=True)  43.8 us
    pallas_call x2, Pallas kernels, gather_rows(): pl.pallas_call(functools.partial(gather_kernel, lists, slots, first, stop...  22.2 us
    all_to_all x3, starting transfers between devices, exchange(): lax.all_to_all(array, 'rows', split_axis=0, concat_axis=0, tiled=True)  21.8 us
    pallas_call x1, Pallas kernels, layer(): pl.pallas_call(functools.partial(layer_kernel, group, steps), grid_spec=p...  20.2 us
    pallas_call x1, Pallas kernels, scatter_first(): pl.pallas_call(functools.partial(scatter_kernel, lists, slots, height - E...  19.2 us
    pallas_call x1, Pallas kernels, scatter_last(): pl.pallas_call(functools.partial(last_kernel, hub_rows.shape[0]), grid_sp...  9.78 us
  transfers between devices with their start and end apart: 3, of which 3 were waited for; matrix products, arithmetic and copies ran while one was open for 1% of the time, Pallas kernels for 16%

profile of v4, /device:TPU:1, one launch (start us, length us, event | category | flops | bytes accessed | tf_op | source)
XLA Modules:
  0.0 204.4 jit_solution(8685145368666898084)
XLA Ops:
  0.6 8.7 %shard_map.112 = bf16[128,40,128]{2,1,0:T(8,128)(2,1)} custom-call(s32[16384]{0:T(1024)} %bitcast.14, s32[512]{0:T(512)} %bitcast.19, bf16[4096,128]{1,0:T(8,128)(2,1)} %x_ref.3), custom_call_target="tpu_custom_call" | custom-call | tf_op jit(solution)/shard_map/pallas_call | solution.py:74
  9.3 11.5 %all-to-all-start = ((bf16[128,40,128]{2,1,0:T(8,128)(2,1)}), bf16[128,40,128]{2,1,0:T(8,128)(2,1)S(1)}, u32[]{:S(2)}, u32[]{:S(2)}) async-start(bf16[128,40,128]{2,1,0:T(8,128)(2,1)} %shard_map.112), calls=%async_computation | async-start | bytes 2621440 | tf_op jit(solution)/shard_map/all_to_all | solution.py:475
  20.8 0.0 copy-start.5
  20.9 13.5 %shard_map.113 = bf16[128,104,128]{2,1,0:T(8,128)(2,1)} custom-call(s32[16384]{0:T(1024)} %bitcast.15, s32[512]{0:T(512)} %bitcast.20, bf16[4096,128]{1,0:T(8,128)(2,1)} %x_ref.3), custom_call_target="tpu_custom_call" | custom-call | tf_op jit(solution)/shard_map/pallas_call | solution.py:74
  34.4 0.0 copy-done.5
  34.4 8.5 %all-to-all-done.halo1_hbm = bf16[128,40,128]{2,1,0:T(8,128)(2,1)S(1)} async-done(((bf16[128,40,128]{2,1,0:T(8,128)(2,1)}), bf16[128,40,128]{2,1,0:T(8,128)(2,1)S(1)}, u32[]{:S(2)}, u32[]{:S(2)}) %all-to-all-start) | async-done | bytes 1310752 | tf_op jit(solution)/shard_map/all_to_all | solution.py:475
  42.9 0.0 copy-start.2
  42.9 0.6 gather_fusion
  43.5 0.7 broadcast_dynamic-update-slice_fusion.1
  44.2 0.0 copy-start.4
  44.2 0.0 copy-done.2
  44.2 4.8 %all-to-all-start.1 = ((bf16[128,104,128]{2,1,0:T(8,128)(2,1)}), bf16[128,104,128]{2,1,0:T(8,128)(2,1)S(1)}, u32[]{:S(2)}, u32[]{:S(2)}) async-start(bf16[128,104,128]{2,1,0:T(8,128)(2,1)} %broadcast_dynamic-update-slice_fusion.1), calls=%async_computation.1 | async-start | bytes 6815744 | tf_op jit(solution)/shard_map/all_to_all | solution.py:475
  49.0 0.0 copy-done.4
  49.0 0.1 copy.13
  49.1 0.7 reshape.99.columns_ref
  49.8 44.1 %all-to-all-done.1.halo2_hbm = bf16[128,104,128]{2,1,0:T(8,128)(2,1)S(1)} async-done(((bf16[128,104,128]{2,1,0:T(8,128)(2,1)}), bf16[128,104,128]{2,1,0:T(8,128)(2,1)S(1)}, u32[]{:S(2)}, u32[]{:S(2)}) %all-to-all-start.1) | async-done | bytes 3407904 | tf_op jit(solution)/shard_map/all_to_all | solution.py:475
  93.8 0.0 copy-start
  93.9 0.8 copy.14
  94.6 1.0 copy-done
  95.7 20.2 %shard_map.114 = (bf16[4096,256]{1,0:T(8,128)(2,1)}, bf16[128,88,128]{2,1,0:T(8,128)(2,1)}, bf16[128,56,128]{2,1,0:T(8,128)(2,1)}, f32[4096,128]{1,0:T(8,128)}) custom-call(s32[192]{0:T(256)} %reshape.99.columns_ref, bf16[32,128,128]{2,1,0:T(8,128)(2,1)} %bitcast.13, bf16[128,40,128]{2,1,0:T(8,128)(2,1)} %copy-done.2, bf16[128,104,128]{2,1,0:T(8,128)(2,1)} %copy-done, ...), custom_call_target="tpu_custom_call" | custom-call | tf_op jit(solution)/shard_map/pallas_call | solution.py:249
  115.9 43.8 %all_to_all.20.back_ref = bf16[128,88,128]{2,1,0:T(8,128)(2,1)S(1)} all-to-all(bf16[128,88,128]{2,1,0:T(8,128)(2,1)} %get-tuple-element.35), channel_id=1, replica_groups=mesh['rows'=128] {'rows'}, dimensions={0} | all-to-all | bytes 5767168 | tf_op jit(solution)/shard_map/all_to_all | solution.py:475
  159.7 0.0 copy-start.1
  159.7 0.0 copy-start.3
  159.7 0.1 convert_reduce_fusion
  159.9 0.9 broadcast_dynamic-update-slice_fusion
  160.9 0.6 copy-done.1
  161.5 5.6 %all-to-all-start.3 = ((bf16[128,56,128]{2,1,0:T(8,128)(2,1)}), bf16[128,56,128]{2,1,0:T(8,128)(2,1)}, u32[]{:S(2)}, u32[]{:S(2)}) async-start(bf16[128,56,128]{2,1,0:T(8,128)(2,1)} %broadcast_dynamic-update-slice_fusion), calls=%async_computation.3 | async-start | bytes 3670016 | tf_op jit(solution)/shard_map/all_to_all | solution.py:475
  167.0 0.0 copy-done.3
  167.0 0.1 slice.72
  167.1 0.7 reshape.103.list_ref
  167.8 0.5 compare_convert_fusion.owned_ref
  168.3 19.2 %shard_map.115.start_ref = f32[4096,128]{1,0:T(8,128)} custom-call(s32[16384]{0:T(1024)} %bitcast.16, bf16[128,88,128]{2,1,0:T(8,128)(2,1)} %copy-done.1, f32[4096,128]{1,0:T(8,128)} %get-tuple-element.36.start_ref), custom_call_target="tpu_custom_call" | custom-call | tf_op jit(solution)/shard_map/pallas_call | solution.py:355
  187.6 7.0 %all-to-all-done.3.back_ref = bf16[128,56,128]{2,1,0:T(8,128)(2,1)} async-done(((bf16[128,56,128]{2,1,0:T(8,128)(2,1)}), bf16[128,56,128]{2,1,0:T(8,128)(2,1)}, u32[]{:S(2)}, u32[]{:S(2)}) %all-to-all-start.3) | async-done | bytes 1835040 | tf_op jit(solution)/shard_map/all_to_all | solution.py:475
  194.6 9.8 %shard_map.116 = (bf16[4096,128]{1,0:T(8,128)(2,1)}, f32[128,256]{1,0:T(8,128)}) custom-call(s32[6144]{0:T(1024)} %reshape.103.list_ref, s32[512]{0:T(512)} %bitcast.21, s32[4]{0:T(128)} %compare_convert_fusion.owned_ref, bf16[128,56,128]{2,1,0:T(8,128)(2,1)} %all-to-all-done.3.back_ref, f32[4096,128]{1,0:T(8,128)} %shard_map.115.start_ref), custom_call_target="tpu_custom_call" | custom-call | tf_op jit(solution)/shard_map/pallas_call | solution.py:447
  (6 shorter events, 0.1 us)
Async XLA Ops:
  9.3 33.6 %all-to-all-start = ((bf16[128,40,128]{2,1,0:T(8,128)(2,1)}), bf16[128,40,128]{2,1,0:T(8,128)(2,1)S(1)}, u32[]{:S(2)}, u32[]{:S(2)}) async-start(bf16[128,40,128]{2,1,0:T(8,128)(2,1)} %shard_map.112), calls=%async_computation | async-start | bytes 2621440 | tf_op jit(solution)/shard_map/all_to_all | solution.py:475
  20.8 13.5 %copy-start.5 = (s32[4]{0:T(128)S(1)}, s32[4]{0:T(128)}, u32[]{:S(2)}) copy-start(s32[4]{0:T(128)} %param.18) | copy-start | bytes 52
  42.9 1.3 copy-start.2
  44.2 4.8 %copy-start.4 = (s32[32,6]{0,1:T(8,128)S(1)}, s32[32,6]{0,1:T(8,128)}, u32[]{:S(2)}) copy-start(s32[32,6]{0,1:T(8,128)} %param.16) | copy-start | bytes 2308
  44.2 49.6 %all-to-all-start.1 = ((bf16[128,104,128]{2,1,0:T(8,128)(2,1)}), bf16[128,104,128]{2,1,0:T(8,128)(2,1)S(1)}, u32[]{:S(2)}, u32[]{:S(2)}) async-start(bf16[128,104,128]{2,1,0:T(8,128)(2,1)} %broadcast_dynamic-update-slice_fusion.1), calls=%async_computation.1 | async-start | bytes 6815744 | tf_op jit(solution)/shard_map/all_to_all | solution.py:475
  93.8 1.8 copy-start
  159.7 1.7 copy-start.1
  159.7 7.3 %copy-start.3 = (s32[1,128,128]{2,1,0:T(8,128)S(1)}, s32[1,128,128]{2,1,0:T(8,128)}, u32[]{:S(2)}) copy-start(s32[1,128,128]{2,1,0:T(8,128)} %param.17) | copy-start | bytes 196612
  161.5 33.1 %all-to-all-start.3 = ((bf16[128,56,128]{2,1,0:T(8,128)(2,1)}), bf16[128,56,128]{2,1,0:T(8,128)(2,1)}, u32[]{:S(2)}, u32[]{:S(2)}) async-start(bf16[128,56,128]{2,1,0:T(8,128)(2,1)} %broadcast_dynamic-update-slice_fusion), calls=%async_computation.3 | async-start | bytes 3670016 | tf_op jit(solution)/shard_map/all_to_all | solution.py:475

commit v5 on v4

--- a/solution.py
+++ b/solution.py
@@ -10,9 +10,12 @@
 BF = jnp.bfloat16
 F32 = jnp.float32
 VMEM_LIMIT = 60 * 2**20
+LAYER_LIMIT = 50 * 2**20
 PAD = 8
 EXTRA = 8
-FIRST_OUT = 32
+HUBS = 4
+FIRST_OUT = 36
+LIVE = 32
 FIRST_BACK = 80
 GELU_A = 0.7978845608028654
 GELU_B = 0.044715
@@ -20,11 +23,12 @@
 
 def each_live_group(list_ref, start, base, stop, group, work):
     if base < stop:
+        end = min(stop, (base // group + 1) * group)
 
         @pl.when(list_ref[start + base] >= 0)
         def _():
-            work(base)
-            each_live_group(list_ref, start, base + group, stop, group, work)
+            work(base, end)
+            each_live_group(list_ref, start, end, stop, group, work)
 
 
 def gather_kernel(lists, slots, first, stop, list_ref, hub_ref, x_ref, out_ref, wide, buffer):
@@ -33,13 +37,11 @@
     peers = pl.num_programs(0) * lists
     sections = hub_ref.shape[0] // peers
     count = stop - first
-    group = 16
 
     @pl.when(step == 0)
     def _():
         wide[pl.ds(0, PAD), :] = jnp.zeros((PAD, wide.shape[1]), F32)
         wide[pl.ds(PAD, rows), :] = x_ref[...].astype(F32)
-        buffer[pl.ds(count, EXTRA), :] = jnp.zeros((EXTRA, wide.shape[1]), F32)
 
     def one_list(k, carry):
         peer = step * lists + k
@@ -52,14 +54,15 @@
                 row = hub_ref[section * peers + peer]
                 buffer[count + section : count + section + 1, :] = wide[pl.ds(row + PAD, 1), :]
         else:
-            buffer[pl.ds(0, count), :] = jnp.zeros((count, wide.shape[1]), F32)
-
-            def work(base):
-                for slot in range(base, base + group):
+            buffer[...] = jnp.zeros_like(buffer)
+
+            def work(base, end):
+                for slot in range(base, end):
                     row = list_ref[start + slot]
-                    buffer[slot - first : slot - first + 1, :] = wide[pl.ds(row + PAD, 1), :]
-
-            each_live_group(list_ref, start, first, stop, group, work)
+                    place = HUBS + slot - first
+                    buffer[place : place + 1, :] = wide[pl.ds(row + PAD, 1), :]
+
+            each_live_group(list_ref, start, first, stop, 16, work)
         out_ref[k] = buffer[...].astype(BF)
         return carry
 
@@ -70,7 +73,7 @@
     peers, slots = send_lists.shape
     rows, width = features.shape
     lists = 32
-    height = stop - first + EXTRA
+    height = stop - first + HUBS
     return pl.pallas_call(
         functools.partial(gather_kernel, lists, slots, first, stop),
         grid_spec=pltpu.PrefetchScalarGridSpec(
@@ -93,7 +96,7 @@
     steps,
     columns_ref,
     x_hbm,
-    halo1_hbm,
+    halo1_ref,
     halo2_hbm,
     hub_ref,
     w_ref,
@@ -118,8 +121,10 @@
     own_part = own_ref.shape[0] // blk
     send_part = send1_ref.shape[0]
     own_blocks = x_hbm.shape[0]
-    peers = halo1_hbm.shape[0]
-    slots1 = halo1_hbm.shape[1] - EXTRA
+    peers = halo1_ref.shape[0]
+    height2 = halo2_hbm.shape[1]
+    ahead = blk - height2
+    odd = halo1_ref.shape[1] - HUBS - ahead
     back1 = send1_ref.shape[1] - EXTRA
 
     @pl.when(step == 0)
@@ -128,14 +133,7 @@
         copies = [
             pltpu.make_async_copy(x_hbm, features.at[pl.ds(0, own_blocks)], sems.at[0]),
             pltpu.make_async_copy(
-                halo1_hbm.at[:, pl.ds(0, slots1), :],
-                features.at[halo, pl.ds(0, slots1), :],
-                sems.at[1],
-            ),
-            pltpu.make_async_copy(
-                halo2_hbm.at[:, pl.ds(0, blk - slots1), :],
-                features.at[halo, pl.ds(slots1, blk - slots1), :],
-                sems.at[2],
+                halo2_hbm, features.at[halo, pl.ds(ahead, height2), :], sems.at[1]
             ),
         ]
         for copy in copies:
@@ -150,6 +148,18 @@
         grad_w[...] = jnp.zeros_like(grad_w)
         for copy in copies:
             copy.wait()
+
+        def join(peer, carry):
+            place = own_blocks + peer
+            features[place, pl.ds(0, ahead), :] = halo1_ref[peer, pl.ds(0, ahead), :]
+            late = halo1_ref[peer, pl.ds(ahead, 8), :].astype(F32)
+            seam = features[place, pl.ds(ahead, 16), :].astype(F32)
+            row = lax.broadcasted_iota(jnp.int32, (8, width), 0)
+            head = jnp.where(row < odd, late, seam[:8])
+            features[place, pl.ds(ahead, 16), :] = jnp.concatenate([head, seam[8:]]).astype(BF)
+            return carry
+
+        lax.fori_loop(0, peers, join, 0, unroll=4)
 
     @pl.when(step < steps)
     def _():
@@ -253,7 +263,7 @@
             grid=(steps + finals,),
             in_specs=[
                 pl.BlockSpec(memory_space=pl.ANY),
-                pl.BlockSpec(memory_space=pl.ANY),
+                pl.BlockSpec(halo1.shape, lambda i, *_: (0, 0, 0)),
                 pl.BlockSpec(memory_space=pl.ANY),
                 pl.BlockSpec((sections * blk, width), lambda i, *_: (0, 0)),
                 pl.BlockSpec((width, width_out), lambda i, *_: (0, 0)),
@@ -273,7 +283,7 @@
                 pltpu.VMEM((width, sections * blk), F32),
                 pltpu.VMEM((width, width_out), F32),
                 pltpu.VMEM((peers, EXTRA, width), F32),
-                pltpu.SemaphoreType.DMA((3,)),
+                pltpu.SemaphoreType.DMA((2,)),
             ],
         ),
         out_shape=[
@@ -282,7 +292,7 @@
             jax.ShapeDtypeStruct((peers, height2, width), BF),
             jax.ShapeDtypeStruct((rows, width), F32),
         ],
-        compiler_params=pltpu.CompilerParams(vmem_limit_bytes=VMEM_LIMIT),
+        compiler_params=pltpu.CompilerParams(vmem_limit_bytes=LAYER_LIMIT),
     )(
         tile_columns.reshape(-1),
         features.reshape(blocks, blk, width),
@@ -330,14 +340,13 @@
         start = (step * lists + k) * slots
         buffer[...] = back_ref[k].astype(F32)
 
-        def work(base):
-            for slot in range(base, base + group, 4):
+        def work(base, end):
+            for slot in range(base, end, 4):
                 places = [list_ref[start + slot + v] for v in range(4)]
                 add_rows(totals, places, buffer, slot)
 
-        for base in range(0, 32, group):
-            work(base)
-        each_live_group(list_ref, start, 32, stop, group, work)
+        work(0, LIVE)
+        each_live_group(list_ref, start, LIVE, stop, group, work)
         return carry
 
     lax.fori_loop(0, lists, one_list, 0)
@@ -410,8 +419,8 @@
     def one_list(peer, carry):
         rows = buffer.at[peer]
 
-        def work(base):
-            for slot in range(base, base + group, 4):
+        def work(base, end):
+            for slot in range(base, end, 4):
                 places = [list_ref[peer * count + slot + v] for v in range(4)]
                 add_rows(totals, places, rows, slot)
 
@@ -496,12 +505,11 @@
     halo1 = exchange(gather_rows(features, send_lists, hub_rows, 0, FIRST_OUT))
     part = gather_rows(features, send_lists, hub_rows, FIRST_OUT, slots)
     hub_mine = halo1[hub_owner, FIRST_OUT + jnp.arange(sections)]
-    end = slots - FIRST_OUT
-    part = part.at[:, end : end + sections].set(
+    part = part.at[:, :sections].set(
         jnp.broadcast_to(hub_mine[None], (peers, sections, width))
     )
     halo2 = exchange(part)
-    hub = halo2[:, end : end + sections].transpose(1, 0, 2).reshape(sections * peers, width)
+    hub = halo2[:, :sections].transpose(1, 0, 2).reshape(sections * peers, width)
 
     output, send1, send2, own = layer(
         features, halo1, halo2, hub, weight, adjacency_tiles, tile_columns, hub_tiles, cotangent

time: 205 us -> 203 us (level)
  waiting for transfers between devices: 59.6 us -> 57.5 us
    all_to_all x3, waiting for transfers between devices: 59.6 us -> 57.5 us  [exchange(): lax.all_to_all(array, 'rows', split_axis=0, concat_axis=0, tiled=True)]
where the time goes in v5:
time: 203 us; the launch traced here: 202 us
  Pallas kernels  71.2 us (35%)
  waiting for transfers between devices  57.5 us (28%)
  blocking collectives  43.9 us (22%)
  starting transfers between devices  22.8 us (11%)
  local copies, waits for them, and re-layouts  4.86 us (2%)
    all_to_all x3, waiting for transfers between devices, exchange(): lax.all_to_all(array, 'rows', split_axis=0, concat_axis=0, tiled=True)  57.5 us
    all_to_all x1, blocking collectives, exchange(): lax.all_to_all(array, 'rows', split_axis=0, concat_axis=0, tiled=True)  43.9 us
    all_to_all x3, starting transfers between devices, exchange(): lax.all_to_all(array, 'rows', split_axis=0, concat_axis=0, tiled=True)  22.8 us
    pallas_call x2, Pallas kernels, gather_rows(): pl.pallas_call(functools.partial(gather_kernel, lists, slots, first, stop...  22.4 us
    pallas_call x1, Pallas kernels, layer(): pl.pallas_call(functools.partial(layer_kernel, group, steps), grid_spec=p...  19.7 us
    pallas_call x1, Pallas kernels, scatter_first(): pl.pallas_call(functools.partial(scatter_kernel, lists, slots, height - E...  19.1 us
    pallas_call x1, Pallas kernels, scatter_last(): pl.pallas_call(functools.partial(last_kernel, hub_rows.shape[0]), grid_sp...  9.96 us
  transfers between devices with their start and end apart: 3, of which 3 were waited for; matrix products, arithmetic and copies ran while one was open for 1% of the time, Pallas kernels for 16%

profile of v5, /device:TPU:1, one launch (start us, length us, event | category | flops | bytes accessed | tf_op | source)
XLA Modules:
  0.0 201.7 jit_solution(5542435308385342602)
XLA Ops:
  0.6 9.3 %shard_map.112 = bf16[128,40,128]{2,1,0:T(8,128)(2,1)} custom-call(s32[16384]{0:T(1024)} %bitcast.15, s32[512]{0:T(512)} %bitcast.19, bf16[4096,128]{1,0:T(8,128)(2,1)} %x_ref.3), custom_call_target="tpu_custom_call" | custom-call | tf_op jit(solution)/shard_map/pallas_call | solution.py:77
  9.9 11.5 %all-to-all-start = ((bf16[128,40,128]{2,1,0:T(8,128)(2,1)}), bf16[128,40,128]{2,1,0:T(8,128)(2,1)S(1)}, u32[]{:S(2)}, u32[]{:S(2)}) async-start(bf16[128,40,128]{2,1,0:T(8,128)(2,1)} %shard_map.112), calls=%async_computation | async-start | bytes 2621440 | tf_op jit(solution)/shard_map/all_to_all | solution.py:484
  21.4 0.0 copy-start.5
  21.4 13.2 %shard_map.113 = bf16[128,96,128]{2,1,0:T(8,128)(2,1)} custom-call(s32[16384]{0:T(1024)} %bitcast.16, s32[512]{0:T(512)} %bitcast.20, bf16[4096,128]{1,0:T(8,128)(2,1)} %x_ref.3), custom_call_target="tpu_custom_call" | custom-call | tf_op jit(solution)/shard_map/pallas_call | solution.py:77
  34.6 0.0 copy-done.5
  34.6 8.9 %all-to-all-done.halo1_ref = bf16[128,40,128]{2,1,0:T(8,128)(2,1)S(1)} async-done(((bf16[128,40,128]{2,1,0:T(8,128)(2,1)}), bf16[128,40,128]{2,1,0:T(8,128)(2,1)S(1)}, u32[]{:S(2)}, u32[]{:S(2)}) %all-to-all-start) | async-done | bytes 1310752 | tf_op jit(solution)/shard_map/all_to_all | solution.py:484
  43.5 0.6 gather_fusion
  44.1 0.7 broadcast_dynamic-update-slice_fusion.1
  44.8 0.0 copy-start.4
  44.8 0.0 copy-start
  44.8 0.0 copy-start.1
  44.8 5.8 %all-to-all-start.1 = ((bf16[128,96,128]{2,1,0:T(8,128)(2,1)}), bf16[128,96,128]{2,1,0:T(8,128)(2,1)}, u32[]{:S(2)}, u32[]{:S(2)}) async-start(bf16[128,96,128]{2,1,0:T(8,128)(2,1)} %broadcast_dynamic-update-slice_fusion.1), calls=%async_computation.1 | async-start | bytes 6291456 | tf_op jit(solution)/shard_map/all_to_all | solution.py:484
  50.6 0.0 copy-done.4
  50.6 0.1 copy.13
  50.7 0.1 reshape.100.columns_ref
  50.8 41.5 %all-to-all-done.1.halo2_hbm = bf16[128,96,128]{2,1,0:T(8,128)(2,1)} async-done(((bf16[128,96,128]{2,1,0:T(8,128)(2,1)}), bf16[128,96,128]{2,1,0:T(8,128)(2,1)}, u32[]{:S(2)}, u32[]{:S(2)}) %all-to-all-start.1) | async-done | bytes 3145760 | tf_op jit(solution)/shard_map/all_to_all | solution.py:484
  92.3 1.0 slice_bitcast_fusion
  93.3 0.0 copy-done
  93.3 0.0 copy-done.1
  93.3 19.7 %shard_map.114 = (bf16[4096,256]{1,0:T(8,128)(2,1)}, bf16[128,88,128]{2,1,0:T(8,128)(2,1)}, bf16[128,56,128]{2,1,0:T(8,128)(2,1)}, f32[4096,128]{1,0:T(8,128)}) custom-call(s32[192]{0:T(256)S(1)} %reshape.100.columns_ref, bf16[32,128,128]{2,1,0:T(8,128)(2,1)S(1)} %bitcast.13, bf16[128,40,128]{2,1,0:T(8,128)(2,1)S(1)} %all-to-all-done.halo1_ref, ...), custom_call_target="tpu_custom_call" | custom-call | tf_op jit(solution)/shard_map/pallas_call | solution.py:259
  113.0 43.9 %all_to_all.20.back_ref = bf16[128,88,128]{2,1,0:T(8,128)(2,1)S(1)} all-to-all(bf16[128,88,128]{2,1,0:T(8,128)(2,1)} %get-tuple-element.35), channel_id=1, replica_groups=mesh['rows'=128] {'rows'}, dimensions={0} | all-to-all | bytes 5767168 | tf_op jit(solution)/shard_map/all_to_all | solution.py:484
  156.9 0.0 copy-start.2
  156.9 0.0 copy-start.3
  156.9 0.1 convert_reduce_fusion
  157.1 0.9 broadcast_dynamic-update-slice_fusion
  158.0 0.6 copy-done.2
  158.6 5.6 %all-to-all-start.3 = ((bf16[128,56,128]{2,1,0:T(8,128)(2,1)}), bf16[128,56,128]{2,1,0:T(8,128)(2,1)}, u32[]{:S(2)}, u32[]{:S(2)}) async-start(bf16[128,56,128]{2,1,0:T(8,128)(2,1)} %broadcast_dynamic-update-slice_fusion), calls=%async_computation.3 | async-start | bytes 3670016 | tf_op jit(solution)/shard_map/all_to_all | solution.py:484
  164.2 0.0 copy-done.3
  164.2 0.1 slice.72
  164.3 0.7 reshape.104.list_ref
  165.0 0.5 compare_convert_fusion.owned_ref
  165.5 19.1 %shard_map.115.start_ref = f32[4096,128]{1,0:T(8,128)} custom-call(s32[16384]{0:T(1024)} %bitcast.17, bf16[128,88,128]{2,1,0:T(8,128)(2,1)} %copy-done.2, f32[4096,128]{1,0:T(8,128)} %get-tuple-element.36.start_ref), custom_call_target="tpu_custom_call" | custom-call | tf_op jit(solution)/shard_map/pallas_call | solution.py:364
  184.6 7.1 %all-to-all-done.3.back_ref = bf16[128,56,128]{2,1,0:T(8,128)(2,1)} async-done(((bf16[128,56,128]{2,1,0:T(8,128)(2,1)}), bf16[128,56,128]{2,1,0:T(8,128)(2,1)}, u32[]{:S(2)}, u32[]{:S(2)}) %all-to-all-start.3) | async-done | bytes 1835040 | tf_op jit(solution)/shard_map/all_to_all | solution.py:484
  191.7 10.0 %shard_map.116 = (bf16[4096,128]{1,0:T(8,128)(2,1)}, f32[128,256]{1,0:T(8,128)}) custom-call(s32[6144]{0:T(1024)} %reshape.104.list_ref, s32[512]{0:T(512)} %bitcast.21, s32[4]{0:T(128)} %compare_convert_fusion.owned_ref, bf16[128,56,128]{2,1,0:T(8,128)(2,1)} %all-to-all-done.3.back_ref, f32[4096,128]{1,0:T(8,128)} %shard_map.115.start_ref), custom_call_target="tpu_custom_call" | custom-call | tf_op jit(solution)/shard_map/pallas_call | solution.py:456
  (6 shorter events, 0.1 us)
Async XLA Ops:
  9.9 33.6 %all-to-all-start = ((bf16[128,40,128]{2,1,0:T(8,128)(2,1)}), bf16[128,40,128]{2,1,0:T(8,128)(2,1)S(1)}, u32[]{:S(2)}, u32[]{:S(2)}) async-start(bf16[128,40,128]{2,1,0:T(8,128)(2,1)} %shard_map.112), calls=%async_computation | async-start | bytes 2621440 | tf_op jit(solution)/shard_map/all_to_all | solution.py:484
  21.4 13.2 %copy-start.5 = (s32[4]{0:T(128)S(1)}, s32[4]{0:T(128)}, u32[]{:S(2)}) copy-start(s32[4]{0:T(128)} %param.18) | copy-start | bytes 52
  44.8 5.8 %copy-start.4 = (s32[32,6]{0,1:T(8,128)S(1)}, s32[32,6]{0,1:T(8,128)}, u32[]{:S(2)}) copy-start(s32[32,6]{0,1:T(8,128)} %param.16) | copy-start | bytes 2308
  44.8 48.5 %copy-start = (bf16[4096,128]{1,0:T(8,128)(2,1)S(1)}, bf16[4096,128]{1,0:T(8,128)(2,1)}, u32[]{:S(2)}) copy-start(bf16[4096,128]{1,0:T(8,128)(2,1)} %x_ref.3) | copy-start | bytes 3145732
  44.8 48.5 %copy-start.1 = (bf16[128,256]{1,0:T(8,128)(2,1)S(1)}, bf16[128,256]{1,0:T(8,128)(2,1)}, u32[]{:S(2)}) copy-start(bf16[128,256]{1,0:T(8,128)(2,1)} %w_ref.1) | copy-start | bytes 196612
  44.8 47.5 %all-to-all-start.1 = ((bf16[128,96,128]{2,1,0:T(8,128)(2,1)}), bf16[128,96,128]{2,1,0:T(8,128)(2,1)}, u32[]{:S(2)}, u32[]{:S(2)}) async-start(bf16[128,96,128]{2,1,0:T(8,128)(2,1)} %broadcast_dynamic-update-slice_fusion.1), calls=%async_computation.1 | async-start | bytes 6291456 | tf_op jit(solution)/shard_map/all_to_all | solution.py:484
  156.9 1.7 copy-start.2
  156.9 7.3 %copy-start.3 = (s32[1,128,128]{2,1,0:T(8,128)S(1)}, s32[1,128,128]{2,1,0:T(8,128)}, u32[]{:S(2)}) copy-start(s32[1,128,128]{2,1,0:T(8,128)} %param.17) | copy-start | bytes 196612
  158.6 33.1 %all-to-all-start.3 = ((bf16[128,56,128]{2,1,0:T(8,128)(2,1)}), bf16[128,56,128]{2,1,0:T(8,128)(2,1)}, u32[]{:S(2)}, u32[]{:S(2)}) async-start(bf16[128,56,128]{2,1,0:T(8,128)(2,1)} %broadcast_dynamic-update-slice_fusion), calls=%async_computation.3 | async-start | bytes 3670016 | tf_op jit(solution)/shard_map/all_to_all | solution.py:484

commit v6 on v5

--- a/solution.py
+++ b/solution.py
@@ -98,16 +98,16 @@
     x_hbm,
     halo1_ref,
     halo2_hbm,
-    hub_ref,
     w_ref,
     tiles_ref,
     hub_tiles_ref,
     cot_ref,
     out_ref,
-    send1_ref,
-    send2_ref,
-    own_ref,
+    send_ref,
+    back_ref,
     features,
+    hub_rows,
+    hub,
     adjoint,
     hub_adjoint,
     grad_w,
@@ -117,15 +117,14 @@
     step = pl.program_id(0)
     per_block, blk = tiles_ref.shape[1:3]
     sections = hub_tiles_ref.shape[0]
-    width = hub_ref.shape[1]
-    own_part = own_ref.shape[0] // blk
-    send_part = send1_ref.shape[0]
+    width = w_ref.shape[0]
+    send_part = send_ref.shape[0]
     own_blocks = x_hbm.shape[0]
     peers = halo1_ref.shape[0]
     height2 = halo2_hbm.shape[1]
     ahead = blk - height2
     odd = halo1_ref.shape[1] - HUBS - ahead
-    back1 = send1_ref.shape[1] - EXTRA
+    kept = adjoint.shape[1]
 
     @pl.when(step == 0)
     def _():
@@ -140,7 +139,7 @@
             copy.start()
 
         def clear(block, carry):
-            adjoint[block] = jnp.zeros((blk, width), F32)
+            adjoint[block] = jnp.zeros((kept, width), F32)
             return carry
 
         lax.fori_loop(0, adjoint.shape[0], clear, 0, unroll=4)
@@ -154,12 +153,16 @@
             features[place, pl.ds(0, ahead), :] = halo1_ref[peer, pl.ds(0, ahead), :]
             late = halo1_ref[peer, pl.ds(ahead, 8), :].astype(F32)
             seam = features[place, pl.ds(ahead, 16), :].astype(F32)
+            for section in range(sections):
+                hub_rows[section, pl.ds(peer, 1), :] = seam[section : section + 1]
             row = lax.broadcasted_iota(jnp.int32, (8, width), 0)
             head = jnp.where(row < odd, late, seam[:8])
             features[place, pl.ds(ahead, 16), :] = jnp.concatenate([head, seam[8:]]).astype(BF)
             return carry
 
         lax.fori_loop(0, peers, join, 0, unroll=4)
+        for section in range(sections):
+            hub[pl.ds(section * blk, blk), :] = hub_rows[section].astype(BF)
 
     @pl.when(step < steps)
     def _():
@@ -176,7 +179,7 @@
             blocks = jnp.concatenate([features[place] for place in places[u]], axis=0)
             tiled.append(jnp.dot(slabs[u], blocks, preferred_element_type=F32))
         z = jnp.concatenate(tiled, axis=0)
-        z = z + jnp.dot(hub_slab, hub_ref[...], preferred_element_type=F32)
+        z = z + jnp.dot(hub_slab, hub[...], preferred_element_type=F32)
         z_high = z.astype(BF)
         z_low = (z - z_high.astype(F32)).astype(BF)
         preact = jnp.dot(
@@ -194,19 +197,19 @@
         back = lax.dot_general(
             grad, weight, (((1,), (1,)), ((), ())), preferred_element_type=F32
         ).astype(BF)
+        back_ref[...] = back
         back_turned = lax.dot_general(
             weight, grad, (((1,), (1,)), ((), ())), preferred_element_type=F32
         ).astype(BF)
         hub_adjoint[...] += jnp.dot(back_turned, hub_slab, preferred_element_type=F32)
         for u in range(group):
-            spread = lax.dot_general(
-                slabs[u],
-                back[u * blk : (u + 1) * blk],
-                (((0,), (0,)), ((), ())),
-                preferred_element_type=F32,
+            turned = slabs[u].T
+            turned = jnp.concatenate(
+                [turned[t * blk : t * blk + kept] for t in range(per_block)], axis=0
             )
+            spread = jnp.dot(turned, back[u * blk : (u + 1) * blk], preferred_element_type=F32)
             for t in range(per_block):
-                adjoint[places[u][t]] += spread[t * blk : (t + 1) * blk]
+                adjoint[places[u][t]] += spread[t * kept : (t + 1) * kept]
 
     @pl.when(step == steps)
     def _():
@@ -224,21 +227,17 @@
     @pl.when(step >= steps)
     def _():
         final = step - steps
-        for block in range(own_part):
-            own_ref[pl.ds(block * blk, blk), :] = adjoint[final * own_part + block]
 
         def finish(k, carry):
             peer = final * send_part + k
-            rows = adjoint[own_blocks + peer]
-            tail = extra[peer]
-            send1_ref[k] = jnp.concatenate([rows[:back1], tail], axis=0).astype(BF)
-            send2_ref[k] = jnp.concatenate([rows[back1:], tail], axis=0).astype(BF)
+            rows = jnp.concatenate([adjoint[own_blocks + peer], extra[peer]], axis=0)
+            send_ref[k] = rows.astype(BF)
             return carry
 
         lax.fori_loop(0, send_part, finish, 0, unroll=4)
 
 
-def layer(features, halo1, halo2, hub, weight, tiles, tile_columns, hub_tiles, cotangent):
+def layer(features, halo1, halo2, weight, tiles, tile_columns, hub_tiles, cotangent):
     blocks, per_block, blk, _ = tiles.shape
     width, width_out = weight.shape
     sections = hub_tiles.shape[0]
@@ -248,7 +247,6 @@
     steps = blocks // group
     finals = 4
     height1 = FIRST_BACK + EXTRA
-    height2 = blk - FIRST_BACK + EXTRA
 
     def work(i):
         return jnp.minimum(i, steps - 1)
@@ -265,7 +263,6 @@
                 pl.BlockSpec(memory_space=pl.ANY),
                 pl.BlockSpec(halo1.shape, lambda i, *_: (0, 0, 0)),
                 pl.BlockSpec(memory_space=pl.ANY),
-                pl.BlockSpec((sections * blk, width), lambda i, *_: (0, 0)),
                 pl.BlockSpec((width, width_out), lambda i, *_: (0, 0)),
                 pl.BlockSpec((group, per_block, blk, blk), lambda i, *_: (work(i), 0, 0, 0)),
                 pl.BlockSpec((sections, group * blk, blk), lambda i, *_: (0, work(i), 0)),
@@ -274,12 +271,13 @@
             out_specs=[
                 pl.BlockSpec((group * blk, width_out), lambda i, *_: (work(i), 0)),
                 pl.BlockSpec((peers // finals, height1, width), lambda i, *_: (final(i), 0, 0)),
-                pl.BlockSpec((peers // finals, height2, width), lambda i, *_: (final(i), 0, 0)),
-                pl.BlockSpec((rows // finals, width), lambda i, *_: (final(i), 0)),
+                pl.BlockSpec((group * blk, width), lambda i, *_: (work(i), 0)),
             ],
             scratch_shapes=[
                 pltpu.VMEM((blocks + peers, blk, width), BF),
-                pltpu.VMEM((blocks + peers, blk, width), F32),
+                pltpu.VMEM((sections, peers, width), F32),
+                pltpu.VMEM((sections * blk, width), BF),
+                pltpu.VMEM((blocks + peers, FIRST_BACK, width), F32),
                 pltpu.VMEM((width, sections * blk), F32),
                 pltpu.VMEM((width, width_out), F32),
                 pltpu.VMEM((peers, EXTRA, width), F32),
@@ -289,8 +287,7 @@
         out_shape=[
             jax.ShapeDtypeStruct((rows, width_out), BF),
             jax.ShapeDtypeStruct((peers, height1, width), BF),
-            jax.ShapeDtypeStruct((peers, height2, width), BF),
-            jax.ShapeDtypeStruct((rows, width), F32),
+            jax.ShapeDtypeStruct((rows, width), BF),
         ],
         compiler_params=pltpu.CompilerParams(vmem_limit_bytes=LAYER_LIMIT),
     )(
@@ -298,12 +295,93 @@
         features.reshape(blocks, blk, width),
         halo1,
         halo2,
-        hub,
         weight,
         tiles,
         hub_tiles,
         cotangent,
     )
+
+
+def rest_kernel(group, steps, columns_ref, back_ref, tiles_ref, send_ref, own_ref, adjoint):
+    step = pl.program_id(0)
+    per_block, blk = tiles_ref.shape[1:3]
+    width = back_ref.shape[1]
+    own_part = own_ref.shape[0] // blk
+    send_part, height, _ = send_ref.shape
+    own_blocks = own_part * (pl.num_programs(0) - steps)
+
+    @pl.when(step == 0)
+    def _():
+        def clear(block, carry):
+            adjoint[block] = jnp.zeros((blk, width), F32)
+            return carry
+
+        lax.fori_loop(0, adjoint.shape[0], clear, 0, unroll=4)
+
+    @pl.when(step < steps)
+    def _():
+        for u in range(group):
+            first = (step * group + u) * per_block
+            slab = jnp.concatenate([tiles_ref[u, t] for t in range(per_block)], axis=1)
+            spread = lax.dot_general(
+                slab,
+                back_ref[u * blk : (u + 1) * blk, :],
+                (((0,), (0,)), ((), ())),
+                preferred_element_type=F32,
+            )
+            for t in range(per_block):
+                adjoint[columns_ref[first + t]] += spread[t * blk : (t + 1) * blk]
+
+    @pl.when(step >= steps)
+    def _():
+        final = step - steps
+        for block in range(own_part):
+            own_ref[pl.ds(block * blk, blk), :] = adjoint[final * own_part + block]
+
+        def finish(k, carry):
+            rows = adjoint[own_blocks + final * send_part + k]
+            tail = jnp.zeros((EXTRA, width), F32)
+            send_ref[k] = jnp.concatenate([rows[blk + EXTRA - height :], tail], axis=0).astype(BF)
+            return carry
+
+        lax.fori_loop(0, send_part, finish, 0, unroll=4)
+
+
+def rest_of_adjoint(back, tiles, tile_columns, peers):
+    blocks, per_block, blk, _ = tiles.shape
+    rows, width = back.shape
+    group = 8
+    steps = blocks // group
+    finals = 4
+    height = blk - FIRST_BACK + EXTRA
+
+    def work(i):
+        return jnp.minimum(i, steps - 1)
+
+    def final(i):
+        return jnp.maximum(i - steps, 0)
+
+    return pl.pallas_call(
+        functools.partial(rest_kernel, group, steps),
+        grid_spec=pltpu.PrefetchScalarGridSpec(
+            num_scalar_prefetch=1,
+            grid=(steps + finals,),
+            in_specs=[
+                pl.BlockSpec((group * blk, width), lambda i, *_: (work(i), 0)),
+                pl.BlockSpec((group, per_block, blk, blk), lambda i, *_: (work(i), 0, 0, 0)),
+            ],
+            out_specs=[
+                pl.BlockSpec((peers // finals, height, width), lambda i, *_: (final(i), 0, 0)),
+                pl.BlockSpec((rows // finals, width), lambda i, *_: (final(i), 0)),
+            ],
+            scratch_shapes=[pltpu.VMEM((blocks + peers, blk, width), F32)],
+        ),
+        out_shape=[
+            jax.ShapeDtypeStruct((peers, height, width), BF),
+            jax.ShapeDtypeStruct((rows, width), F32),
+        ],
+        compiler_params=pltpu.CompilerParams(vmem_limit_bytes=VMEM_LIMIT),
+    )(tile_columns.reshape(-1), back, tiles)
 
 
 def add_rows(totals, places, buffer, base):
@@ -509,13 +587,13 @@
         jnp.broadcast_to(hub_mine[None], (peers, sections, width))
     )
     halo2 = exchange(part)
-    hub = halo2[:, :sections].transpose(1, 0, 2).reshape(sections * peers, width)
-
-    output, send1, send2, own = layer(
-        features, halo1, halo2, hub, weight, adjacency_tiles, tile_columns, hub_tiles, cotangent
+
+    output, send1, back = layer(
+        features, halo1, halo2, weight, adjacency_tiles, tile_columns, hub_tiles, cotangent
     )
 
     back1 = exchange(send1)
+    send2, own = rest_of_adjoint(back, adjacency_tiles, tile_columns, peers)
     sums = jnp.sum(back1[:, FIRST_BACK:].astype(F32), axis=0)
     weight_row = sums[sections : sections + pieces] + sums[sections + pieces :]
     high = weight_row.astype(BF)

time: 203 us -> 200 us (0.985)
  blocking collectives: 43.9 us -> 0 us
  waiting for transfers between devices: 57.5 us -> 86.9 us
  Pallas kernels: 71.2 us -> 79.1 us
  starting transfers between devices: 22.8 us -> 27.4 us
    all_to_all x1 -> x0, blocking collectives: 43.9 us -> none  [exchange(): lax.all_to_all(array, 'rows', split_axis=0, concat_axis=0, tiled=True)]
    all_to_all x3 -> x4, waiting for transfers between devices: 57.5 us -> 86.9 us  [exchange(): lax.all_to_all(array, 'rows', split_axis=0, concat_axis=0, tiled=True)]
    pallas_call x0 -> x1, Pallas kernels: none -> 9.18 us  [rest_of_adjoint(): pl.pallas_call(functools.partial(rest_kernel, group, steps), grid_spec=pl...]
    all_to_all x3 -> x4, starting transfers between devices: 22.8 us -> 27.4 us  [exchange(): lax.all_to_all(array, 'rows', split_axis=0, concat_axis=0, tiled=True)]
  transfers between devices with their start and end apart: 3 -> 4, of which waited for: 3 -> 4; matrix products, arithmetic and copies ran while one was open for 1% -> 1% of each run, Pallas kernels for 16% -> 21%
where the time goes in v6:
time: 200 us; the launch traced here: 199 us
  waiting for transfers between devices  86.9 us (43%)
  Pallas kernels  79.1 us (40%)
  starting transfers between devices  27.4 us (14%)
  local copies, waits for them, and re-layouts  4.75 us (2%)
    all_to_all x4, waiting for transfers between devices, exchange(): lax.all_to_all(array, 'rows', split_axis=0, concat_axis=0, tiled=True)  86.9 us
    all_to_all x4, starting transfers between devices, exchange(): lax.all_to_all(array, 'rows', split_axis=0, concat_axis=0, tiled=True)  27.4 us
    pallas_call x2, Pallas kernels, gather_rows(): pl.pallas_call(functools.partial(gather_kernel, lists, slots, first, stop...  22.6 us
    pallas_call x1, Pallas kernels, scatter_first(): pl.pallas_call(functools.partial(scatter_kernel, lists, slots, height - E...  19.5 us
    pallas_call x1, Pallas kernels, layer(): pl.pallas_call(functools.partial(layer_kernel, group, steps), grid_spec=p...  17.9 us
    pallas_call x1, Pallas kernels, scatter_last(): pl.pallas_call(functools.partial(last_kernel, hub_rows.shape[0]), grid_sp...  9.89 us
    pallas_call x1, Pallas kernels, rest_of_adjoint(): pl.pallas_call(functools.partial(rest_kernel, group, steps), grid_spec=pl...  9.18 us
  transfers between devices with their start and end apart: 4, of which 4 were waited for; matrix products, arithmetic and copies ran while one was open for 1% of the time, Pallas kernels for 21%

profile of v6, /device:TPU:1, one launch (start us, length us, event | category | flops | bytes accessed | tf_op | source)
XLA Modules:
  0.0 199.5 jit_solution(3152730107916001161)
XLA Ops:
  0.6 9.3 %shard_map.112 = bf16[128,40,128]{2,1,0:T(8,128)(2,1)} custom-call(s32[16384]{0:T(1024)} %bitcast.11, s32[512]{0:T(512)} %bitcast.15, bf16[4096,128]{1,0:T(8,128)(2,1)} %x_ref.3), custom_call_target="tpu_custom_call" | custom-call | tf_op jit(solution)/shard_map/pallas_call | solution.py:77
  9.9 11.5 %all-to-all-start = ((bf16[128,40,128]{2,1,0:T(8,128)(2,1)}), bf16[128,40,128]{2,1,0:T(8,128)(2,1)S(1)}, u32[]{:S(2)}, u32[]{:S(2)}) async-start(bf16[128,40,128]{2,1,0:T(8,128)(2,1)} %shard_map.112), calls=%async_computation | async-start | bytes 2621440 | tf_op jit(solution)/shard_map/all_to_all | solution.py:562
  21.4 0.0 copy-start.7
  21.4 13.3 %shard_map.113 = bf16[128,96,128]{2,1,0:T(8,128)(2,1)} custom-call(s32[16384]{0:T(1024)} %bitcast.12, s32[512]{0:T(512)} %bitcast.16, bf16[4096,128]{1,0:T(8,128)(2,1)} %x_ref.3), custom_call_target="tpu_custom_call" | custom-call | tf_op jit(solution)/shard_map/pallas_call | solution.py:77
  34.8 0.0 copy-done.7
  34.8 8.7 %all-to-all-done.halo1_ref = bf16[128,40,128]{2,1,0:T(8,128)(2,1)S(1)} async-done(((bf16[128,40,128]{2,1,0:T(8,128)(2,1)}), bf16[128,40,128]{2,1,0:T(8,128)(2,1)S(1)}, u32[]{:S(2)}, u32[]{:S(2)}) %all-to-all-start) | async-done | bytes 1310752 | tf_op jit(solution)/shard_map/all_to_all | solution.py:562
  43.5 0.6 gather_fusion
  44.1 0.7 broadcast_dynamic-update-slice_fusion.1
  44.8 0.0 copy-start.6
  44.8 0.0 copy-start
  44.8 0.0 copy-start.2
  44.8 5.8 %all-to-all-start.1 = ((bf16[128,96,128]{2,1,0:T(8,128)(2,1)}), bf16[128,96,128]{2,1,0:T(8,128)(2,1)}, u32[]{:S(2)}, u32[]{:S(2)}) async-start(bf16[128,96,128]{2,1,0:T(8,128)(2,1)} %broadcast_dynamic-update-slice_fusion.1), calls=%async_computation.1 | async-start | bytes 6291456 | tf_op jit(solution)/shard_map/all_to_all | solution.py:562
  50.6 0.0 copy-done.6
  50.6 0.1 copy.12
  50.7 0.1 reshape.98.columns_ref
  50.8 0.0 copy-start.3
  50.8 41.5 %all-to-all-done.1.halo2_hbm = bf16[128,96,128]{2,1,0:T(8,128)(2,1)} async-done(((bf16[128,96,128]{2,1,0:T(8,128)(2,1)}), bf16[128,96,128]{2,1,0:T(8,128)(2,1)}, u32[]{:S(2)}, u32[]{:S(2)}) %all-to-all-start.1) | async-done | bytes 3145760 | tf_op jit(solution)/shard_map/all_to_all | solution.py:562
  92.3 0.0 copy-done
  92.3 0.0 copy-done.2
  92.3 17.9 %shard_map.114 = (bf16[4096,256]{1,0:T(8,128)(2,1)}, bf16[128,88,128]{2,1,0:T(8,128)(2,1)}, bf16[4096,128]{1,0:T(8,128)(2,1)S(1)}) custom-call(s32[192]{0:T(256)S(1)} %reshape.98.columns_ref, bf16[32,128,128]{2,1,0:T(8,128)(2,1)S(1)} %bitcast.10, bf16[128,40,128]{2,1,0:T(8,128)(2,1)S(1)} %all-to-all-done.halo1_ref, ...), custom_call_target="tpu_custom_call" | custom-call | tf_op jit(solution)/shard_map/pallas_call | solution.py:257
  110.2 0.0 copy-done.3
  110.2 0.0 copy-start.1
  110.2 1.0 copy-done.1
  111.2 4.5 %all-to-all-start.2 = ((bf16[128,88,128]{2,1,0:T(8,128)(2,1)}), bf16[128,88,128]{2,1,0:T(8,128)(2,1)S(1)}, u32[]{:S(2)}, u32[]{:S(2)}) async-start(bf16[128,88,128]{2,1,0:T(8,128)(2,1)} %get-tuple-element.37), calls=%async_computation.2 | async-start | bytes 5767168 | tf_op jit(solution)/shard_map/all_to_all | solution.py:562
  115.7 9.2 %shard_map.115 = (bf16[128,56,128]{2,1,0:T(8,128)(2,1)}, f32[4096,128]{1,0:T(8,128)}) custom-call(s32[192]{0:T(256)} %copy-done.3, bf16[4096,128]{1,0:T(8,128)(2,1)} %copy-done.1, bf16[32,6,128,128]{3,2,1,0:T(8,128)(2,1)} %tiles_ref.3), custom_call_target="tpu_custom_call" | custom-call | tf_op jit(solution)/shard_map/pallas_call | solution.py:364
  124.9 0.0 copy-start.5
  124.9 29.9 %all-to-all-done.2.back_ref = bf16[128,88,128]{2,1,0:T(8,128)(2,1)S(1)} async-done(((bf16[128,88,128]{2,1,0:T(8,128)(2,1)}), bf16[128,88,128]{2,1,0:T(8,128)(2,1)S(1)}, u32[]{:S(2)}, u32[]{:S(2)}) %all-to-all-start.2) | async-done | bytes 2883616 | tf_op jit(solution)/shard_map/all_to_all | solution.py:562
  154.8 0.0 copy-start.4
  154.8 0.1 convert_reduce_fusion
  155.0 0.9 broadcast_dynamic-update-slice_fusion
  156.0 0.5 copy-done.4
  156.5 5.6 %all-to-all-start.3 = ((bf16[128,56,128]{2,1,0:T(8,128)(2,1)}), bf16[128,56,128]{2,1,0:T(8,128)(2,1)}, u32[]{:S(2)}, u32[]{:S(2)}) async-start(bf16[128,56,128]{2,1,0:T(8,128)(2,1)} %broadcast_dynamic-update-slice_fusion), calls=%async_computation.3 | async-start | bytes 3670016 | tf_op jit(solution)/shard_map/all_to_all | solution.py:562
  162.1 0.0 copy-done.5
  162.1 0.1 slice.67
  162.2 0.7 reshape.101.list_ref
  162.9 0.5 compare_convert_fusion.owned_ref
  163.4 19.5 %shard_map.116.start_ref = f32[4096,128]{1,0:T(8,128)} custom-call(s32[16384]{0:T(1024)} %bitcast.13, bf16[128,88,128]{2,1,0:T(8,128)(2,1)} %copy-done.4, f32[4096,128]{1,0:T(8,128)} %get-tuple-element.38.start_ref), custom_call_target="tpu_custom_call" | custom-call | tf_op jit(solution)/shard_map/pallas_call | solution.py:442
  182.9 6.7 %all-to-all-done.3.back_ref = bf16[128,56,128]{2,1,0:T(8,128)(2,1)} async-done(((bf16[128,56,128]{2,1,0:T(8,128)(2,1)}), bf16[128,56,128]{2,1,0:T(8,128)(2,1)}, u32[]{:S(2)}, u32[]{:S(2)}) %all-to-all-start.3) | async-done | bytes 1835040 | tf_op jit(solution)/shard_map/all_to_all | solution.py:562
  189.6 9.9 %shard_map.117 = (bf16[4096,128]{1,0:T(8,128)(2,1)}, f32[128,256]{1,0:T(8,128)}) custom-call(s32[6144]{0:T(1024)} %reshape.101.list_ref, s32[512]{0:T(512)} %bitcast.17, s32[4]{0:T(128)} %compare_convert_fusion.owned_ref, bf16[128,56,128]{2,1,0:T(8,128)(2,1)} %all-to-all-done.3.back_ref, f32[4096,128]{1,0:T(8,128)} %shard_map.116.start_ref), custom_call_target="tpu_custom_call" | custom-call | tf_op jit(solution)/shard_map/pallas_call | solution.py:534
  (5 shorter events, 0.0 us)
Async XLA Ops:
  9.9 33.6 %all-to-all-start = ((bf16[128,40,128]{2,1,0:T(8,128)(2,1)}), bf16[128,40,128]{2,1,0:T(8,128)(2,1)S(1)}, u32[]{:S(2)}, u32[]{:S(2)}) async-start(bf16[128,40,128]{2,1,0:T(8,128)(2,1)} %shard_map.112), calls=%async_computation | async-start | bytes 2621440 | tf_op jit(solution)/shard_map/all_to_all | solution.py:562
  21.4 13.4 %copy-start.7 = (s32[4]{0:T(128)S(1)}, s32[4]{0:T(128)}, u32[]{:S(2)}) copy-start(s32[4]{0:T(128)} %param.18) | copy-start | bytes 52
  44.8 5.8 %copy-start.6 = (s32[32,6]{0,1:T(8,128)S(1)}, s32[32,6]{0,1:T(8,128)}, u32[]{:S(2)}) copy-start(s32[32,6]{0,1:T(8,128)} %param.16) | copy-start | bytes 2308
  44.8 47.5 %copy-start = (bf16[4096,128]{1,0:T(8,128)(2,1)S(1)}, bf16[4096,128]{1,0:T(8,128)(2,1)}, u32[]{:S(2)}) copy-start(bf16[4096,128]{1,0:T(8,128)(2,1)} %x_ref.3) | copy-start | bytes 3145732
  44.8 47.5 %copy-start.2 = (bf16[128,256]{1,0:T(8,128)(2,1)S(1)}, bf16[128,256]{1,0:T(8,128)(2,1)}, u32[]{:S(2)}) copy-start(bf16[128,256]{1,0:T(8,128)(2,1)} %w_ref.1) | copy-start | bytes 196612
  44.8 47.5 %all-to-all-start.1 = ((bf16[128,96,128]{2,1,0:T(8,128)(2,1)}), bf16[128,96,128]{2,1,0:T(8,128)(2,1)}, u32[]{:S(2)}, u32[]{:S(2)}) async-start(bf16[128,96,128]{2,1,0:T(8,128)(2,1)} %broadcast_dynamic-update-slice_fusion.1), calls=%async_computation.1 | async-start | bytes 6291456 | tf_op jit(solution)/shard_map/all_to_all | solution.py:562
  50.8 59.4 %copy-start.3 = (s32[192]{0:T(256)}, s32[192]{0:T(256)S(1)}, u32[]{:S(2)}) copy-start(s32[192]{0:T(256)S(1)} %reshape.98.columns_ref) | copy-start | bytes 2308
  110.2 1.0 copy-start.1
  111.2 43.7 %all-to-all-start.2 = ((bf16[128,88,128]{2,1,0:T(8,128)(2,1)}), bf16[128,88,128]{2,1,0:T(8,128)(2,1)S(1)}, u32[]{:S(2)}, u32[]{:S(2)}) async-start(bf16[128,88,128]{2,1,0:T(8,128)(2,1)} %get-tuple-element.37), calls=%async_computation.2 | async-start | bytes 5767168 | tf_op jit(solution)/shard_map/all_to_all | solution.py:562
  124.9 37.2 %copy-start.5 = (s32[1,128,128]{2,1,0:T(8,128)S(1)}, s32[1,128,128]{2,1,0:T(8,128)}, u32[]{:S(2)}) copy-start(s32[1,128,128]{2,1,0:T(8,128)} %param.17) | copy-start | bytes 196612
  154.8 1.7 copy-start.4
  156.5 33.1 %all-to-all-start.3 = ((bf16[128,56,128]{2,1,0:T(8,128)(2,1)}), bf16[128,56,128]{2,1,0:T(8,128)(2,1)}, u32[]{:S(2)}, u32[]{:S(2)}) async-start(bf16[128,56,128]{2,1,0:T(8,128)(2,1)} %broadcast_dynamic-update-slice_fusion), calls=%async_computation.3 | async-start | bytes 3670016 | tf_op jit(solution)/shard_map/all_to_all | solution.py:562

commit v7 on v6

--- a/solution.py
+++ b/solution.py
@@ -16,7 +16,8 @@
 HUBS = 4
 FIRST_OUT = 36
 LIVE = 32
-FIRST_BACK = 80
+FIRST_BACK = 72
+KEPT = 80
 GELU_A = 0.7978845608028654
 GELU_B = 0.044715
 
@@ -43,30 +44,37 @@
         wide[pl.ds(0, PAD), :] = jnp.zeros((PAD, wide.shape[1]), F32)
         wide[pl.ds(PAD, rows), :] = x_ref[...].astype(F32)
 
-    def one_list(k, carry):
-        peer = step * lists + k
-        start = peer * slots
-        if first == 0:
-            for slot in range(count):
-                row = list_ref[start + slot]
-                buffer[slot : slot + 1, :] = wide[pl.ds(row + PAD, 1), :]
-            for section in range(sections):
-                row = hub_ref[section * peers + peer]
-                buffer[count + section : count + section + 1, :] = wide[pl.ds(row + PAD, 1), :]
-        else:
-            buffer[...] = jnp.zeros_like(buffer)
-
-            def work(base, end):
-                for slot in range(base, end):
+    height = count + HUBS
+    pair = 2
+
+    def one_pair(k, carry):
+        for half in range(pair):
+            peer = step * lists + k * pair + half
+            start = peer * slots
+            top = half * height
+            if first == 0:
+                for slot in range(count):
                     row = list_ref[start + slot]
-                    place = HUBS + slot - first
+                    buffer[top + slot : top + slot + 1, :] = wide[pl.ds(row + PAD, 1), :]
+                for section in range(sections):
+                    row = hub_ref[section * peers + peer]
+                    place = top + count + section
                     buffer[place : place + 1, :] = wide[pl.ds(row + PAD, 1), :]
-
-            each_live_group(list_ref, start, first, stop, 16, work)
-        out_ref[k] = buffer[...].astype(BF)
+            else:
+                buffer[top : top + height, :] = jnp.zeros((height, wide.shape[1]), F32)
+
+                def work(base, end):
+                    for slot in range(base, end):
+                        row = list_ref[start + slot]
+                        place = top + HUBS + slot - first
+                        buffer[place : place + 1, :] = wide[pl.ds(row + PAD, 1), :]
+
+                each_live_group(list_ref, start, first, stop, 16, work)
+        rows = pair * height
+        out_ref[pl.ds(pl.multiple_of(k * rows, rows), rows), :] = buffer[...].astype(BF)
         return carry
 
-    lax.fori_loop(0, lists, one_list, 0, unroll=2 if first == 0 else 1)
+    lax.fori_loop(0, lists // pair, one_pair, 0)
 
 
 def gather_rows(features, send_lists, hub_rows, first, stop):
@@ -80,15 +88,15 @@
             num_scalar_prefetch=2,
             grid=(peers // lists,),
             in_specs=[pl.BlockSpec((rows, width), lambda i, *_: (0, 0))],
-            out_specs=pl.BlockSpec((lists, height, width), lambda i, *_: (i, 0, 0)),
+            out_specs=pl.BlockSpec((lists * height, width), lambda i, *_: (i, 0)),
             scratch_shapes=[
                 pltpu.VMEM((rows + PAD, width), F32),
-                pltpu.VMEM((height, width), F32),
+                pltpu.VMEM((2 * height, width), F32),
             ],
         ),
-        out_shape=jax.ShapeDtypeStruct((peers, height, width), BF),
+        out_shape=jax.ShapeDtypeStruct((peers * height, width), BF),
         compiler_params=pltpu.CompilerParams(vmem_limit_bytes=VMEM_LIMIT),
-    )(send_lists.reshape(-1), hub_rows.reshape(-1), features)
+    )(send_lists.reshape(-1), hub_rows.reshape(-1), features).reshape(peers, height, width)
 
 
 def layer_kernel(
@@ -120,10 +128,10 @@
     width = w_ref.shape[0]
     send_part = send_ref.shape[0]
     own_blocks = x_hbm.shape[0]
-    peers = halo1_ref.shape[0]
-    height2 = halo2_hbm.shape[1]
+    peers, height2, _ = halo2_hbm.shape
+    height1 = halo1_ref.shape[0] // peers
     ahead = blk - height2
-    odd = halo1_ref.shape[1] - HUBS - ahead
+    odd = height1 - HUBS - ahead
     kept = adjoint.shape[1]
 
     @pl.when(step == 0)
@@ -148,19 +156,25 @@
         for copy in copies:
             copy.wait()
 
-        def join(peer, carry):
-            place = own_blocks + peer
-            features[place, pl.ds(0, ahead), :] = halo1_ref[peer, pl.ds(0, ahead), :]
-            late = halo1_ref[peer, pl.ds(ahead, 8), :].astype(F32)
-            seam = features[place, pl.ds(ahead, 16), :].astype(F32)
-            for section in range(sections):
-                hub_rows[section, pl.ds(peer, 1), :] = seam[section : section + 1]
-            row = lax.broadcasted_iota(jnp.int32, (8, width), 0)
-            head = jnp.where(row < odd, late, seam[:8])
-            features[place, pl.ds(ahead, 16), :] = jnp.concatenate([head, seam[8:]]).astype(BF)
+        def join(k, carry):
+            rows = 2 * height1
+            part1 = halo1_ref[pl.ds(pl.multiple_of(k * rows, rows), rows), :].astype(F32)
+            for half in range(2):
+                peer = 2 * k + half
+                place = own_blocks + peer
+                top = half * height1
+                features[place, pl.ds(0, ahead), :] = part1[top : top + ahead].astype(BF)
+                late = part1[top + ahead : top + ahead + 8]
+                seam = features[place, pl.ds(ahead, 16), :].astype(F32)
+                for section in range(sections):
+                    hub_rows[section, pl.ds(peer, 1), :] = seam[section : section + 1]
+                row = lax.broadcasted_iota(jnp.int32, (8, width), 0)
+                head = jnp.where(row < odd, late, seam[:8])
+                whole = jnp.concatenate([head, seam[8:]])
+                features[place, pl.ds(ahead, 16), :] = whole.astype(BF)
             return carry
 
-        lax.fori_loop(0, peers, join, 0, unroll=4)
+        lax.fori_loop(0, peers // 2, join, 0, unroll=2)
         for section in range(sections):
             hub[pl.ds(section * blk, blk), :] = hub_rows[section].astype(BF)
 
@@ -230,8 +244,8 @@
 
         def finish(k, carry):
             peer = final * send_part + k
-            rows = jnp.concatenate([adjoint[own_blocks + peer], extra[peer]], axis=0)
-            send_ref[k] = rows.astype(BF)
+            rows = adjoint[own_blocks + peer][: send_ref.shape[1] - EXTRA]
+            send_ref[k] = jnp.concatenate([rows, extra[peer]], axis=0).astype(BF)
             return carry
 
         lax.fori_loop(0, send_part, finish, 0, unroll=4)
@@ -261,7 +275,7 @@
             grid=(steps + finals,),
             in_specs=[
                 pl.BlockSpec(memory_space=pl.ANY),
-                pl.BlockSpec(halo1.shape, lambda i, *_: (0, 0, 0)),
+                pl.BlockSpec((peers * halo1.shape[1], width), lambda i, *_: (0, 0)),
                 pl.BlockSpec(memory_space=pl.ANY),
                 pl.BlockSpec((width, width_out), lambda i, *_: (0, 0)),
                 pl.BlockSpec((group, per_block, blk, blk), lambda i, *_: (work(i), 0, 0, 0)),
@@ -277,7 +291,7 @@
                 pltpu.VMEM((blocks + peers, blk, width), BF),
                 pltpu.VMEM((sections, peers, width), F32),
                 pltpu.VMEM((sections * blk, width), BF),
-                pltpu.VMEM((blocks + peers, FIRST_BACK, width), F32),
+                pltpu.VMEM((blocks + peers, KEPT, width), F32),
                 pltpu.VMEM((width, sections * blk), F32),
                 pltpu.VMEM((width, width_out), F32),
                 pltpu.VMEM((peers, EXTRA, width), F32),
@@ -293,7 +307,7 @@
     )(
         tile_columns.reshape(-1),
         features.reshape(blocks, blk, width),
-        halo1,
+        halo1.reshape(-1, width),
         halo2,
         weight,
         tiles,

time: 200 us -> 201 us (level)
  transfers between devices with their start and end apart: 4 -> 4, of which waited for: 4 -> 4; matrix products, arithmetic and copies ran while one was open for 1% -> 1% of each run, Pallas kernels for 21% -> 20%
where the time goes in v7:
time: 201 us; the launch traced here: 200 us
  waiting for transfers between devices  88.7 us (44%)
  Pallas kernels  77.9 us (39%)
  starting transfers between devices  27.4 us (14%)
  local copies, waits for them, and re-layouts  4.72 us (2%)
    all_to_all x4, waiting for transfers between devices, exchange(): lax.all_to_all(array, 'rows', split_axis=0, concat_axis=0, tiled=True)  88.7 us
    all_to_all x4, starting transfers between devices, exchange(): lax.all_to_all(array, 'rows', split_axis=0, concat_axis=0, tiled=True)  27.4 us
    pallas_call x2, Pallas kernels, gather_rows(): pl.pallas_call(functools.partial(gather_kernel, lists, slots, first, stop...  21.5 us
    pallas_call x1, Pallas kernels, scatter_first(): pl.pallas_call(functools.partial(scatter_kernel, lists, slots, height - E...  18.3 us
    pallas_call x1, Pallas kernels, layer(): pl.pallas_call(functools.partial(layer_kernel, group, steps), grid_spec=p...  18 us
    pallas_call x1, Pallas kernels, scatter_last(): pl.pallas_call(functools.partial(last_kernel, hub_rows.shape[0]), grid_sp...  10.8 us
    pallas_call x1, Pallas kernels, rest_of_adjoint(): pl.pallas_call(functools.partial(rest_kernel, group, steps), grid_spec=pl...  9.28 us
  transfers between devices with their start and end apart: 4, of which 4 were waited for; matrix products, arithmetic and copies ran while one was open for 1% of the time, Pallas kernels for 20%

profile of v7, /device:TPU:1, one launch (start us, length us, event | category | flops | bytes accessed | tf_op | source)
XLA Modules:
  0.0 200.2 jit_solution(10458274320899247473)
XLA Ops:
  0.6 9.1 %shard_map.112 = bf16[5120,128]{1,0:T(8,128)(2,1)} custom-call(s32[16384]{0:T(1024)} %bitcast.17, s32[512]{0:T(512)} %bitcast.21, bf16[4096,128]{1,0:T(8,128)(2,1)} %x_ref.3), custom_call_target="tpu_custom_call" | custom-call | tf_op jit(solution)/shard_map/pallas_call | solution.py:85
  9.7 11.5 %all-to-all-start = ((bf16[128,40,128]{2,1,0:T(8,128)(2,1)}), bf16[128,40,128]{2,1,0:T(8,128)(2,1)S(1)}, u32[]{:S(2)}, u32[]{:S(2)}) async-start(bf16[128,40,128]{2,1,0:T(8,128)(2,1)} %bitcast.16), calls=%async_computation | async-start | bytes 2621440 | tf_op jit(solution)/shard_map/all_to_all | solution.py:576
  21.2 0.0 copy-start.7
  21.2 12.4 %shard_map.113 = bf16[12288,128]{1,0:T(8,128)(2,1)} custom-call(s32[16384]{0:T(1024)} %bitcast.18, s32[512]{0:T(512)} %bitcast.22, bf16[4096,128]{1,0:T(8,128)(2,1)} %x_ref.3), custom_call_target="tpu_custom_call" | custom-call | tf_op jit(solution)/shard_map/pallas_call | solution.py:85
  33.6 0.0 copy-done.7
  33.6 9.7 %all-to-all-done = bf16[128,40,128]{2,1,0:T(8,128)(2,1)S(1)} async-done(((bf16[128,40,128]{2,1,0:T(8,128)(2,1)}), bf16[128,40,128]{2,1,0:T(8,128)(2,1)S(1)}, u32[]{:S(2)}, u32[]{:S(2)}) %all-to-all-start) | async-done | bytes 1310752 | tf_op jit(solution)/shard_map/all_to_all | solution.py:576
  43.3 0.6 gather_fusion
  43.9 0.7 broadcast_dynamic-update-slice_fusion.1
  44.6 0.0 copy-start.6
  44.6 0.0 copy-start
  44.6 0.0 copy-start.2
  44.6 5.8 %all-to-all-start.1 = ((bf16[128,96,128]{2,1,0:T(8,128)(2,1)}), bf16[128,96,128]{2,1,0:T(8,128)(2,1)}, u32[]{:S(2)}, u32[]{:S(2)}) async-start(bf16[128,96,128]{2,1,0:T(8,128)(2,1)} %broadcast_dynamic-update-slice_fusion.1), calls=%async_computation.1 | async-start | bytes 6291456 | tf_op jit(solution)/shard_map/all_to_all | solution.py:576
  50.4 0.0 copy-done.6
  50.4 0.1 copy.12
  50.5 0.1 reshape.107.columns_ref
  50.6 0.0 copy-start.3
  50.6 41.5 %all-to-all-done.1.halo2_hbm = bf16[128,96,128]{2,1,0:T(8,128)(2,1)} async-done(((bf16[128,96,128]{2,1,0:T(8,128)(2,1)}), bf16[128,96,128]{2,1,0:T(8,128)(2,1)}, u32[]{:S(2)}, u32[]{:S(2)}) %all-to-all-start.1) | async-done | bytes 3145760 | tf_op jit(solution)/shard_map/all_to_all | solution.py:576
  92.1 0.0 copy-done
  92.1 0.0 copy-done.2
  92.1 18.0 %shard_map.114 = (bf16[4096,256]{1,0:T(8,128)(2,1)}, bf16[128,80,128]{2,1,0:T(8,128)(2,1)}, bf16[4096,128]{1,0:T(8,128)(2,1)S(1)}) custom-call(s32[192]{0:T(256)S(1)} %reshape.107.columns_ref, bf16[32,128,128]{2,1,0:T(8,128)(2,1)S(1)} %bitcast.13, bf16[5120,128]{1,0:T(8,128)(2,1)S(1)} %bitcast.14, bf16[128,96,128]{2,1,0:T(8,128)(2,1)} %all-to-all-done.1.halo2_hbm, ...), custom_call_target="tpu_custom_call" | custom-call | tf_op jit(solution)/shard_map/pallas_call | solution.py:271
  110.1 0.0 copy-done.3
  110.1 0.0 copy-start.1
  110.1 1.0 copy-done.1
  111.1 4.5 %all-to-all-start.2 = ((bf16[128,80,128]{2,1,0:T(8,128)(2,1)}), bf16[128,80,128]{2,1,0:T(8,128)(2,1)S(1)}, u32[]{:S(2)}, u32[]{:S(2)}) async-start(bf16[128,80,128]{2,1,0:T(8,128)(2,1)} %get-tuple-element.37), calls=%async_computation.2 | async-start | bytes 5242880 | tf_op jit(solution)/shard_map/all_to_all | solution.py:576
  115.6 9.3 %shard_map.115 = (bf16[128,64,128]{2,1,0:T(8,128)(2,1)}, f32[4096,128]{1,0:T(8,128)}) custom-call(s32[192]{0:T(256)} %copy-done.3, bf16[4096,128]{1,0:T(8,128)(2,1)} %copy-done.1, bf16[32,6,128,128]{3,2,1,0:T(8,128)(2,1)} %tiles_ref.3), custom_call_target="tpu_custom_call" | custom-call | tf_op jit(solution)/shard_map/pallas_call | solution.py:378
  124.9 27.0 %all-to-all-done.2.back_ref = bf16[128,80,128]{2,1,0:T(8,128)(2,1)S(1)} async-done(((bf16[128,80,128]{2,1,0:T(8,128)(2,1)}), bf16[128,80,128]{2,1,0:T(8,128)(2,1)S(1)}, u32[]{:S(2)}, u32[]{:S(2)}) %all-to-all-start.2) | async-done | bytes 2621472 | tf_op jit(solution)/shard_map/all_to_all | solution.py:576
  151.9 0.0 copy-start.4
  151.9 0.1 convert_reduce_fusion
  152.1 0.9 broadcast_dynamic-update-slice_fusion
  153.0 0.0 copy-start.5
  153.0 0.5 copy-done.4
  153.5 5.7 %all-to-all-start.3 = ((bf16[128,64,128]{2,1,0:T(8,128)(2,1)}), bf16[128,64,128]{2,1,0:T(8,128)(2,1)}, u32[]{:S(2)}, u32[]{:S(2)}) async-start(bf16[128,64,128]{2,1,0:T(8,128)(2,1)} %broadcast_dynamic-update-slice_fusion), calls=%async_computation.3 | async-start | bytes 4194304 | tf_op jit(solution)/shard_map/all_to_all | solution.py:576
  159.2 0.0 copy-done.5
  159.2 0.1 slice.67
  159.3 0.7 reshape.113.list_ref
  160.0 0.6 compare_convert_fusion.owned_ref
  160.5 18.3 %shard_map.116.start_ref = f32[4096,128]{1,0:T(8,128)} custom-call(s32[16384]{0:T(1024)} %bitcast.19, bf16[128,80,128]{2,1,0:T(8,128)(2,1)} %copy-done.4, f32[4096,128]{1,0:T(8,128)} %get-tuple-element.38.start_ref), custom_call_target="tpu_custom_call" | custom-call | tf_op jit(solution)/shard_map/pallas_call | solution.py:456
  178.9 10.6 %all-to-all-done.3.back_ref = bf16[128,64,128]{2,1,0:T(8,128)(2,1)} async-done(((bf16[128,64,128]{2,1,0:T(8,128)(2,1)}), bf16[128,64,128]{2,1,0:T(8,128)(2,1)}, u32[]{:S(2)}, u32[]{:S(2)}) %all-to-all-start.3) | async-done | bytes 2097184 | tf_op jit(solution)/shard_map/all_to_all | solution.py:576
  189.5 10.8 %shard_map.117 = (bf16[4096,128]{1,0:T(8,128)(2,1)}, f32[128,256]{1,0:T(8,128)}) custom-call(s32[7168]{0:T(1024)} %reshape.113.list_ref, s32[512]{0:T(512)} %bitcast.23, s32[4]{0:T(128)} %compare_convert_fusion.owned_ref, bf16[128,64,128]{2,1,0:T(8,128)(2,1)} %all-to-all-done.3.back_ref, f32[4096,128]{1,0:T(8,128)} %shard_map.116.start_ref), custom_call_target="tpu_custom_call" | custom-call | tf_op jit(solution)/shard_map/pallas_call | solution.py:548
  (5 shorter events, 0.0 us)
Async XLA Ops:
  9.7 33.6 %all-to-all-start = ((bf16[128,40,128]{2,1,0:T(8,128)(2,1)}), bf16[128,40,128]{2,1,0:T(8,128)(2,1)S(1)}, u32[]{:S(2)}, u32[]{:S(2)}) async-start(bf16[128,40,128]{2,1,0:T(8,128)(2,1)} %bitcast.16), calls=%async_computation | async-start | bytes 2621440 | tf_op jit(solution)/shard_map/all_to_all | solution.py:576
  21.2 12.4 %copy-start.7 = (s32[4]{0:T(128)S(1)}, s32[4]{0:T(128)}, u32[]{:S(2)}) copy-start(s32[4]{0:T(128)} %param.18) | copy-start | bytes 52
  44.6 5.8 %copy-start.6 = (s32[32,6]{0,1:T(8,128)S(1)}, s32[32,6]{0,1:T(8,128)}, u32[]{:S(2)}) copy-start(s32[32,6]{0,1:T(8,128)} %param.16) | copy-start | bytes 2308
  44.6 47.5 %copy-start = (bf16[4096,128]{1,0:T(8,128)(2,1)S(1)}, bf16[4096,128]{1,0:T(8,128)(2,1)}, u32[]{:S(2)}) copy-start(bf16[4096,128]{1,0:T(8,128)(2,1)} %x_ref.3) | copy-start | bytes 3145732
  44.6 47.5 %copy-start.2 = (bf16[128,256]{1,0:T(8,128)(2,1)S(1)}, bf16[128,256]{1,0:T(8,128)(2,1)}, u32[]{:S(2)}) copy-start(bf16[128,256]{1,0:T(8,128)(2,1)} %w_ref.1) | copy-start | bytes 196612
  44.6 47.5 %all-to-all-start.1 = ((bf16[128,96,128]{2,1,0:T(8,128)(2,1)}), bf16[128,96,128]{2,1,0:T(8,128)(2,1)}, u32[]{:S(2)}, u32[]{:S(2)}) async-start(bf16[128,96,128]{2,1,0:T(8,128)(2,1)} %broadcast_dynamic-update-slice_fusion.1), calls=%async_computation.1 | async-start | bytes 6291456 | tf_op jit(solution)/shard_map/all_to_all | solution.py:576
  50.6 59.5 %copy-start.3 = (s32[192]{0:T(256)}, s32[192]{0:T(256)S(1)}, u32[]{:S(2)}) copy-start(s32[192]{0:T(256)S(1)} %reshape.107.columns_ref) | copy-start | bytes 2308
  110.1 1.0 copy-start.1
  111.1 40.8 %all-to-all-start.2 = ((bf16[128,80,128]{2,1,0:T(8,128)(2,1)}), bf16[128,80,128]{2,1,0:T(8,128)(2,1)S(1)}, u32[]{:S(2)}, u32[]{:S(2)}) async-start(bf16[128,80,128]{2,1,0:T(8,128)(2,1)} %get-tuple-element.37), calls=%async_computation.2 | async-start | bytes 5242880 | tf_op jit(solution)/shard_map/all_to_all | solution.py:576
  151.9 1.6 copy-start.4
  153.0 6.2 %copy-start.5 = (s32[1,128,128]{2,1,0:T(8,128)S(1)}, s32[1,128,128]{2,1,0:T(8,128)}, u32[]{:S(2)}) copy-start(s32[1,128,128]{2,1,0:T(8,128)} %param.17) | copy-start | bytes 196612
  153.5 36.0 %all-to-all-start.3 = ((bf16[128,64,128]{2,1,0:T(8,128)(2,1)}), bf16[128,64,128]{2,1,0:T(8,128)(2,1)}, u32[]{:S(2)}, u32[]{:S(2)}) async-start(bf16[128,64,128]{2,1,0:T(8,128)(2,1)} %broadcast_dynamic-update-slice_fusion), calls=%async_computation.3 | async-start | bytes 4194304 | tf_op jit(solution)/shard_map/all_to_all | solution.py:576

commit v8 on v7

--- a/solution.py
+++ b/solution.py
@@ -16,8 +16,8 @@
 HUBS = 4
 FIRST_OUT = 36
 LIVE = 32
-FIRST_BACK = 72
-KEPT = 80
+FIRST_BACK = 88
+KEPT = 96
 GELU_A = 0.7978845608028654
 GELU_B = 0.044715
 

time: 201 us -> 199 us (0.990)
    pallas_call x1, Pallas kernels: 10.8 us -> 8.6 us  [scatter_last(): pl.pallas_call(functools.partial(last_kernel, hub_rows.shape[0]), grid_sp...]
  transfers between devices with their start and end apart: 4 -> 4, of which waited for: 4 -> 4; matrix products, arithmetic and copies ran while one was open for 1% -> 1% of each run, Pallas kernels for 20% -> 21%
where the time goes in v8:
time: 199 us; the launch traced here: 198 us
  waiting for transfers between devices  87.7 us (44%)
  Pallas kernels  77.2 us (39%)
  starting transfers between devices  27.3 us (14%)
  local copies, waits for them, and re-layouts  4.24 us (2%)
    all_to_all x4, waiting for transfers between devices, exchange(): lax.all_to_all(array, 'rows', split_axis=0, concat_axis=0, tiled=True)  87.7 us
    all_to_all x4, starting transfers between devices, exchange(): lax.all_to_all(array, 'rows', split_axis=0, concat_axis=0, tiled=True)  27.3 us
    pallas_call x2, Pallas kernels, gather_rows(): pl.pallas_call(functools.partial(gather_kernel, lists, slots, first, stop...  21.2 us
    pallas_call x1, Pallas kernels, scatter_first(): pl.pallas_call(functools.partial(scatter_kernel, lists, slots, height - E...  19.9 us
    pallas_call x1, Pallas kernels, layer(): pl.pallas_call(functools.partial(layer_kernel, group, steps), grid_spec=p...  18.3 us
    pallas_call x1, Pallas kernels, rest_of_adjoint(): pl.pallas_call(functools.partial(rest_kernel, group, steps), grid_spec=pl...  9.18 us
    pallas_call x1, Pallas kernels, scatter_last(): pl.pallas_call(functools.partial(last_kernel, hub_rows.shape[0]), grid_sp...  8.6 us
  transfers between devices with their start and end apart: 4, of which 4 were waited for; matrix products, arithmetic and copies ran while one was open for 1% of the time, Pallas kernels for 21%

profile of v8, /device:TPU:1, one launch (start us, length us, event | category | flops | bytes accessed | tf_op | source)
XLA Modules:
  0.0 197.9 jit_solution(10069664951860612117)
XLA Ops:
  0.6 9.1 %shard_map.112 = bf16[5120,128]{1,0:T(8,128)(2,1)} custom-call(s32[16384]{0:T(1024)} %bitcast.17, s32[512]{0:T(512)} %bitcast.21, bf16[4096,128]{1,0:T(8,128)(2,1)} %x_ref.3), custom_call_target="tpu_custom_call" | custom-call | tf_op jit(solution)/shard_map/pallas_call | solution.py:85
  9.7 11.5 %all-to-all-start = ((bf16[128,40,128]{2,1,0:T(8,128)(2,1)}), bf16[128,40,128]{2,1,0:T(8,128)(2,1)S(1)}, u32[]{:S(2)}, u32[]{:S(2)}) async-start(bf16[128,40,128]{2,1,0:T(8,128)(2,1)} %bitcast.16), calls=%async_computation | async-start | bytes 2621440 | tf_op jit(solution)/shard_map/all_to_all | solution.py:576
  21.2 0.0 copy-start.7
  21.2 12.1 %shard_map.113 = bf16[12288,128]{1,0:T(8,128)(2,1)} custom-call(s32[16384]{0:T(1024)} %bitcast.18, s32[512]{0:T(512)} %bitcast.22, bf16[4096,128]{1,0:T(8,128)(2,1)} %x_ref.3), custom_call_target="tpu_custom_call" | custom-call | tf_op jit(solution)/shard_map/pallas_call | solution.py:85
  33.4 0.0 copy-done.7
  33.4 9.9 %all-to-all-done = bf16[128,40,128]{2,1,0:T(8,128)(2,1)S(1)} async-done(((bf16[128,40,128]{2,1,0:T(8,128)(2,1)}), bf16[128,40,128]{2,1,0:T(8,128)(2,1)S(1)}, u32[]{:S(2)}, u32[]{:S(2)}) %all-to-all-start) | async-done | bytes 1310752 | tf_op jit(solution)/shard_map/all_to_all | solution.py:576
  43.3 0.6 gather_fusion
  43.9 0.7 broadcast_dynamic-update-slice_fusion.1
  44.6 0.0 copy-start.6
  44.6 0.0 copy-start
  44.6 0.0 copy-start.2
  44.6 5.8 %all-to-all-start.1 = ((bf16[128,96,128]{2,1,0:T(8,128)(2,1)}), bf16[128,96,128]{2,1,0:T(8,128)(2,1)}, u32[]{:S(2)}, u32[]{:S(2)}) async-start(bf16[128,96,128]{2,1,0:T(8,128)(2,1)} %broadcast_dynamic-update-slice_fusion.1), calls=%async_computation.1 | async-start | bytes 6291456 | tf_op jit(solution)/shard_map/all_to_all | solution.py:576
  50.4 0.0 copy-done.6
  50.4 0.1 copy.12
  50.5 0.1 reshape.107.columns_ref
  50.6 0.0 copy-start.3
  50.6 41.5 %all-to-all-done.1.halo2_hbm = bf16[128,96,128]{2,1,0:T(8,128)(2,1)} async-done(((bf16[128,96,128]{2,1,0:T(8,128)(2,1)}), bf16[128,96,128]{2,1,0:T(8,128)(2,1)}, u32[]{:S(2)}, u32[]{:S(2)}) %all-to-all-start.1) | async-done | bytes 3145760 | tf_op jit(solution)/shard_map/all_to_all | solution.py:576
  92.1 0.0 copy-done
  92.1 0.0 copy-done.2
  92.1 18.3 %shard_map.114 = (bf16[4096,256]{1,0:T(8,128)(2,1)}, bf16[128,96,128]{2,1,0:T(8,128)(2,1)}, bf16[4096,128]{1,0:T(8,128)(2,1)S(1)}) custom-call(s32[192]{0:T(256)S(1)} %reshape.107.columns_ref, bf16[32,128,128]{2,1,0:T(8,128)(2,1)S(1)} %bitcast.13, bf16[5120,128]{1,0:T(8,128)(2,1)S(1)} %bitcast.14, bf16[128,96,128]{2,1,0:T(8,128)(2,1)} %all-to-all-done.1.halo2_hbm, ...), custom_call_target="tpu_custom_call" | custom-call | tf_op jit(solution)/shard_map/pallas_call | solution.py:271
  110.4 0.0 copy-done.3
  110.4 0.0 copy-start.1
  110.4 1.0 copy-done.1
  111.4 4.5 %all-to-all-start.2 = ((bf16[128,96,128]{2,1,0:T(8,128)(2,1)}), bf16[128,96,128]{2,1,0:T(8,128)(2,1)S(1)}, u32[]{:S(2)}, u32[]{:S(2)}) async-start(bf16[128,96,128]{2,1,0:T(8,128)(2,1)} %get-tuple-element.37), calls=%async_computation.2 | async-start | bytes 6291456 | tf_op jit(solution)/shard_map/all_to_all | solution.py:576
  115.9 9.2 %shard_map.115 = (bf16[128,48,128]{2,1,0:T(8,128)(2,1)}, f32[4096,128]{1,0:T(8,128)}) custom-call(s32[192]{0:T(256)} %copy-done.3, bf16[4096,128]{1,0:T(8,128)(2,1)} %copy-done.1, bf16[32,6,128,128]{3,2,1,0:T(8,128)(2,1)} %tiles_ref.3), custom_call_target="tpu_custom_call" | custom-call | tf_op jit(solution)/shard_map/pallas_call | solution.py:378
  125.1 0.0 copy-start.5
  125.1 32.8 %all-to-all-done.2.back_ref = bf16[128,96,128]{2,1,0:T(8,128)(2,1)S(1)} async-done(((bf16[128,96,128]{2,1,0:T(8,128)(2,1)}), bf16[128,96,128]{2,1,0:T(8,128)(2,1)S(1)}, u32[]{:S(2)}, u32[]{:S(2)}) %all-to-all-start.2) | async-done | bytes 3145760 | tf_op jit(solution)/shard_map/all_to_all | solution.py:576
  157.9 0.0 copy-start.4
  157.9 0.1 convert_reduce_fusion
  158.1 1.0 broadcast_dynamic-update-slice_fusion
  159.1 5.5 %all-to-all-start.3 = ((bf16[128,48,128]{2,1,0:T(8,128)(2,1)}), bf16[128,48,128]{2,1,0:T(8,128)(2,1)}, u32[]{:S(2)}, u32[]{:S(2)}) async-start(bf16[128,48,128]{2,1,0:T(8,128)(2,1)} %broadcast_dynamic-update-slice_fusion), calls=%async_computation.3 | async-start | bytes 3145728 | tf_op jit(solution)/shard_map/all_to_all | solution.py:576
  164.6 0.0 copy-done.5
  164.6 0.1 slice.67
  164.7 0.7 reshape.113.list_ref
  165.4 0.5 compare_convert_fusion.owned_ref
  165.9 0.0 copy-done.4
  165.9 19.9 %shard_map.116.start_ref = f32[4096,128]{1,0:T(8,128)} custom-call(s32[16384]{0:T(1024)} %bitcast.19, bf16[128,96,128]{2,1,0:T(8,128)(2,1)} %copy-done.4, f32[4096,128]{1,0:T(8,128)} %get-tuple-element.38.start_ref), custom_call_target="tpu_custom_call" | custom-call | tf_op jit(solution)/shard_map/pallas_call | solution.py:456
  185.8 3.5 %all-to-all-done.3.back_ref = bf16[128,48,128]{2,1,0:T(8,128)(2,1)} async-done(((bf16[128,48,128]{2,1,0:T(8,128)(2,1)}), bf16[128,48,128]{2,1,0:T(8,128)(2,1)}, u32[]{:S(2)}, u32[]{:S(2)}) %all-to-all-start.3) | async-done | bytes 1572896 | tf_op jit(solution)/shard_map/all_to_all | solution.py:576
  189.3 8.6 %shard_map.117 = (bf16[4096,128]{1,0:T(8,128)(2,1)}, f32[128,256]{1,0:T(8,128)}) custom-call(s32[5120]{0:T(1024)} %reshape.113.list_ref, s32[512]{0:T(512)} %bitcast.23, s32[4]{0:T(128)} %compare_convert_fusion.owned_ref, bf16[128,48,128]{2,1,0:T(8,128)(2,1)} %all-to-all-done.3.back_ref, f32[4096,128]{1,0:T(8,128)} %shard_map.116.start_ref), custom_call_target="tpu_custom_call" | custom-call | tf_op jit(solution)/shard_map/pallas_call | solution.py:548
  (5 shorter events, 0.0 us)
Async XLA Ops:
  9.7 33.6 %all-to-all-start = ((bf16[128,40,128]{2,1,0:T(8,128)(2,1)}), bf16[128,40,128]{2,1,0:T(8,128)(2,1)S(1)}, u32[]{:S(2)}, u32[]{:S(2)}) async-start(bf16[128,40,128]{2,1,0:T(8,128)(2,1)} %bitcast.16), calls=%async_computation | async-start | bytes 2621440 | tf_op jit(solution)/shard_map/all_to_all | solution.py:576
  21.2 12.2 %copy-start.7 = (s32[4]{0:T(128)S(1)}, s32[4]{0:T(128)}, u32[]{:S(2)}) copy-start(s32[4]{0:T(128)} %param.18) | copy-start | bytes 52
  44.6 5.8 %copy-start.6 = (s32[32,6]{0,1:T(8,128)S(1)}, s32[32,6]{0,1:T(8,128)}, u32[]{:S(2)}) copy-start(s32[32,6]{0,1:T(8,128)} %param.16) | copy-start | bytes 2308
  44.6 47.5 %copy-start = (bf16[4096,128]{1,0:T(8,128)(2,1)S(1)}, bf16[4096,128]{1,0:T(8,128)(2,1)}, u32[]{:S(2)}) copy-start(bf16[4096,128]{1,0:T(8,128)(2,1)} %x_ref.3) | copy-start | bytes 3145732
  44.6 47.5 %copy-start.2 = (bf16[128,256]{1,0:T(8,128)(2,1)S(1)}, bf16[128,256]{1,0:T(8,128)(2,1)}, u32[]{:S(2)}) copy-start(bf16[128,256]{1,0:T(8,128)(2,1)} %w_ref.1) | copy-start | bytes 196612
  44.6 47.5 %all-to-all-start.1 = ((bf16[128,96,128]{2,1,0:T(8,128)(2,1)}), bf16[128,96,128]{2,1,0:T(8,128)(2,1)}, u32[]{:S(2)}, u32[]{:S(2)}) async-start(bf16[128,96,128]{2,1,0:T(8,128)(2,1)} %broadcast_dynamic-update-slice_fusion.1), calls=%async_computation.1 | async-start | bytes 6291456 | tf_op jit(solution)/shard_map/all_to_all | solution.py:576
  50.6 59.8 %copy-start.3 = (s32[192]{0:T(256)}, s32[192]{0:T(256)S(1)}, u32[]{:S(2)}) copy-start(s32[192]{0:T(256)S(1)} %reshape.107.columns_ref) | copy-start | bytes 2308
  110.4 1.0 copy-start.1
  111.4 46.5 %all-to-all-start.2 = ((bf16[128,96,128]{2,1,0:T(8,128)(2,1)}), bf16[128,96,128]{2,1,0:T(8,128)(2,1)S(1)}, u32[]{:S(2)}, u32[]{:S(2)}) async-start(bf16[128,96,128]{2,1,0:T(8,128)(2,1)} %get-tuple-element.37), calls=%async_computation.2 | async-start | bytes 6291456 | tf_op jit(solution)/shard_map/all_to_all | solution.py:576
  125.1 39.5 %copy-start.5 = (s32[1,128,128]{2,1,0:T(8,128)S(1)}, s32[1,128,128]{2,1,0:T(8,128)}, u32[]{:S(2)}) copy-start(s32[1,128,128]{2,1,0:T(8,128)} %param.17) | copy-start | bytes 196612
  157.9 8.0 %copy-start.4 = (bf16[128,96,128]{2,1,0:T(8,128)(2,1)}, bf16[128,96,128]{2,1,0:T(8,128)(2,1)S(1)}, u32[]{:S(2)}) copy-start(bf16[128,96,128]{2,1,0:T(8,128)(2,1)S(1)} %all-to-all-done.2.back_ref) | copy-start | bytes 9437188
  159.1 30.2 %all-to-all-start.3 = ((bf16[128,48,128]{2,1,0:T(8,128)(2,1)}), bf16[128,48,128]{2,1,0:T(8,128)(2,1)}, u32[]{:S(2)}, u32[]{:S(2)}) async-start(bf16[128,48,128]{2,1,0:T(8,128)(2,1)} %broadcast_dynamic-update-slice_fusion), calls=%async_computation.3 | async-start | bytes 3145728 | tf_op jit(solution)/shard_map/all_to_all | solution.py:576
